TPU v7x, 32 devices: a whole 2x2x4 slice. The times are simulated.
32 devices in a mesh: ctx: 16 (over z, y, x), pipe: 2 (over core).
Axes of the slice: x: 2, y: 2, z: 4, core: 2. Of those that a mesh axis runs over, the one named last changes fastest.
Arguments:
- loaded: bfloat16 [2, 32, 128, 4096], P('pipe', 'ctx'), may hold values from -6 to 6
- counts: int32 [16], P('ctx'), may hold values from 0 to 2, as said below
- destinations: int32 [32], P('ctx'), may hold values from -1 to 15, as said below
- bounds: int32 [16], replicated, may hold values from 0 to 128, as said below
- se_gate: bfloat16 [2, 2048, 4096], P('pipe', 'ctx'), may hold values from -6 to 6
- mr_gate: bfloat16 [2, 2048, 4096], P('pipe', 'ctx'), may hold values from -6 to 6
- phase_grads: bfloat16 [2, 2048, 4096], P('pipe', 'ctx'), may hold values from -6 to 6
- se_taps: float32 [2, 256, 7], P('pipe'), may hold values from -2.5 to 2.5
- mr_taps: float32 [2, 256, 128], P('pipe'), may hold values from -0.5 to 0.5
Outputs:
- grad_input: bfloat16 [2, 2048, 4096], P('pipe', 'ctx')
- grad_se_gate: bfloat16 [2, 2048, 4096], P('pipe', 'ctx')
- grad_mr_gate: bfloat16 [2, 2048, 4096], P('pipe', 'ctx')
- grad_se_taps: float32 [2, 256, 7], P('pipe')
- grad_mr_taps: float32 [2, 256, 128], P('pipe')
Inputs may be any that keep to these rules, and one draw needn't show every extreme that they name: `counts`: loaders hold 0 to 2 tiles, 16 in all; taken loader by loader and slot by slot they are the sequence's tiles in order, and loader i's first tile is tile i or i + 1. The first loader holds 2 and the last holds none. `destinations`: entry 2 i + j is the sequence tile held in slot j of loader i, and -1 where j is not below that loader's count. `bounds`: entry t is the offset within tile t at which a new segment starts, at most one a tile, or 128 where none starts; tile 0's is 0 and the last tile's is 128.
All inputs are finite; a program needn't handle non-finite values.
Results may differ from a plain program's by a relative error of at most 0.0085.
Values may be sent and summed in bfloat16 or wider, within the bound.
No kernel may reach another device: no remote copies, remote signals or barrier semaphores. Data moves between devices by JAX's collectives and lax.ppermute only.
A program may use at most 192 MiB of HBM per device.

v0:
```python
import math

import jax
import jax.numpy as jnp
from jax import lax
from jax.sharding import PartitionSpec as P

GROUP = 16


far_before = -1000000


def from_behind(block, axis, distance):
    devices = range(lax.axis_size(axis))
    route = [(i - distance, i) for i in devices if i - distance in devices]
    return lax.ppermute(block, axis, route)


def partner(value, axis, apart):
    mask = 2**apart
    pairs = [(source, source ^ mask) for source in range(lax.axis_size(axis))]
    return lax.ppermute(value, axis, pairs)


def toeplitz_rows(tap_table, starts):
    group_count = tap_table.shape[0]
    tap_count = tap_table.shape[1]
    row_count = starts.shape[0]
    col_count = 2 * tap_count
    tap_line = jnp.concatenate(
        [
            jnp.zeros((group_count, 1), tap_table.dtype),
            tap_table[:, ::-1],
            jnp.zeros((group_count, col_count - tap_count), tap_table.dtype),
        ],
        axis=1,
    )
    spread_rows = jnp.broadcast_to(
        tap_line[:, None, :], (group_count, row_count, col_count + 1)
    ).reshape(group_count, row_count * (col_count + 1))
    toeplitz = spread_rows[:, : row_count * col_count].reshape(group_count, row_count, col_count)
    columns = jnp.arange(col_count, dtype=jnp.int32)
    keep_mask = columns[None, :] - tap_count >= starts[:, None]
    return (jnp.where(keep_mask[None], toeplitz, jnp.zeros((), tap_table.dtype)), keep_mask)


def tap_sums(products):
    group_count = products.shape[0]
    row_count = products.shape[1]
    col_count = products.shape[2]
    flat = products.reshape(group_count, row_count * col_count)
    flat = jnp.pad(flat, ((0, 0), (0, row_count)))
    lagged = flat.reshape(group_count, row_count, col_count + 1)
    return jnp.sum(lagged[:, :, 1 : row_count + 1], axis=1)[:, ::-1]


def channel_major(values, group_count):
    return values.T.reshape(group_count, GROUP, values.shape[0])


def token_major(values):
    return values.reshape(-1, values.shape[2]).T


def lag_grads_major(weighted_major, mid_major, keep_mask):
    pieces = 4
    group_count = weighted_major.shape[0]
    row_count = weighted_major.shape[2]
    front_all = weighted_major.reshape(pieces, group_count // pieces, GROUP, row_count)
    back_all = mid_major.reshape(pieces, group_count // pieces, GROUP, mid_major.shape[2])

    def block_taps(operand_pair):
        front_part, back_part = operand_pair
        products = jnp.einsum(
            "gcr,gcs->grs", front_part, back_part, preferred_element_type=jnp.float32
        )
        products = jnp.where(keep_mask[None], products, 0.0)
        return tap_sums(products)

    return lax.map(block_taps, (front_all, back_all)).reshape(group_count, row_count)


def short_forward(extended, tap_table, starts):
    row_count = starts.shape[0]
    lead_rows = extended.shape[0] - row_count
    channel_taps = jnp.repeat(tap_table, GROUP, axis=0)
    positions = jnp.arange(row_count, dtype=jnp.int32)
    running = jnp.zeros((row_count, extended.shape[1]), jnp.float32)
    for offset in range(tap_table.shape[1]):
        shifted = extended[lead_rows - offset : lead_rows - offset + row_count].astype(jnp.float32)
        allowed = (positions - offset >= starts)[:, None]
        running = running + jnp.where(allowed, channel_taps[:, offset][None, :] * shifted, 0.0)
    return running


def short_back(extended, tap_table, starts_ext):
    row_count = extended.shape[0] - 8
    channel_taps = jnp.repeat(tap_table, GROUP, axis=0)
    positions = jnp.arange(row_count, dtype=jnp.int32)
    running = jnp.zeros((row_count, extended.shape[1]), jnp.float32)
    for offset in range(tap_table.shape[1]):
        shifted = extended[offset : offset + row_count].astype(jnp.float32)
        allowed = (positions >= starts_ext[offset : offset + row_count])[:, None]
        running = running + jnp.where(allowed, channel_taps[:, offset][None, :] * shifted, 0.0)
    return running


def short_taps_grad(weighted, extended, tap_table, starts):
    row_count = starts.shape[0]
    lead_rows = extended.shape[0] - row_count
    positions = jnp.arange(row_count, dtype=jnp.int32)
    weighted_f = weighted.astype(jnp.float32)
    columns = []
    for offset in range(tap_table.shape[1]):
        shifted = extended[lead_rows - offset : lead_rows - offset + row_count].astype(jnp.float32)
        allowed = (positions - offset >= starts)[:, None]
        summed = jnp.sum(jnp.where(allowed, weighted_f * shifted, 0.0), axis=0)
        columns.append(jnp.sum(summed.reshape(-1, GROUP), axis=1))
    return jnp.stack(columns, axis=1)


def body(loaded, counts, destinations, bounds, se_gate, mr_gate, phase_grads, se_taps, mr_taps):
    ctx_count = lax.axis_size("ctx")
    shard_index = lax.axis_index("ctx")
    slot_tiles = loaded[0]
    row_count = slot_tiles.shape[1]
    channel_count = slot_tiles.shape[2]
    group_count = channel_count // GROUP
    rim_rows = 8
    held_count = counts[0]
    first_dest = destinations[0]
    second_dest = destinations[1]
    own_tile = (held_count >= 1) & (first_dest == shard_index)
    send_first = (held_count >= 1) & (first_dest == shard_index + 1)
    send_second = (held_count >= 2) & (second_dest == shard_index + 1)
    outgoing = jnp.where(
        send_first,
        slot_tiles[0],
        jnp.where(send_second, slot_tiles[1], jnp.zeros_like(slot_tiles[0])),
    )
    arrived = from_behind(outgoing, "ctx", 1)
    layer_input = jnp.where(own_tile, slot_tiles[0], arrived)
    incoming = partner(phase_grads, "pipe", 0)[0]
    gate_se = se_gate[0]
    gate_mr = mr_gate[0]
    taps_se = se_taps[0]
    taps_low = mr_taps[0].astype(jnp.bfloat16)
    tile_total = bounds.shape[0]
    positions = jnp.arange(row_count, dtype=jnp.int32)

    def bound_at(tile_num):
        inside = (tile_num >= 0) & (tile_num < tile_total)
        return jnp.where(inside, bounds[jnp.clip(tile_num, 0, tile_total - 1)], row_count)

    def starts_of(tile_num):
        current = bound_at(tile_num)
        earlier = bound_at(tile_num - 1)
        return jnp.where(
            positions >= current,
            current,
            jnp.where(earlier < row_count, earlier - row_count, far_before),
        )

    start_here = starts_of(shard_index)
    start_next = starts_of(shard_index + 1)
    before_rows = from_behind(layer_input[row_count - rim_rows :], "ctx", 1)
    input_ext = jnp.concatenate([before_rows, layer_input], axis=0)
    se_mix = short_forward(input_ext, taps_se, start_here)
    mid_acts = (layer_input.astype(jnp.float32) + gate_se.astype(jnp.float32) * se_mix).astype(
        jnp.bfloat16
    )
    mid_prior = from_behind(mid_acts, "ctx", 1)
    mid_major = channel_major(jnp.concatenate([mid_prior, mid_acts], axis=0), group_count)
    matrix_here, keep_here = toeplitz_rows(taps_low, start_here)
    mr_mix_major = jnp.einsum(
        "gcs,grs->gcr", mid_major, matrix_here, preferred_element_type=jnp.float32
    )
    mr_mix = token_major(mr_mix_major)
    grad_gate_mr = (incoming.astype(jnp.float32) * mr_mix).astype(jnp.bfloat16)
    weighted = (gate_mr.astype(jnp.float32) * incoming.astype(jnp.float32)).astype(jnp.bfloat16)
    weighted_next = from_behind(weighted, "ctx", -1)
    weighted_major = channel_major(weighted, group_count)
    next_major = channel_major(weighted_next, group_count)
    matrix_next, keep_next = toeplitz_rows(taps_low, start_next)
    back_here = jnp.einsum(
        "gcr,grs->gcs",
        weighted_major,
        matrix_here[:, :, row_count:],
        preferred_element_type=jnp.float32,
    )
    back_next = jnp.einsum(
        "gcr,grs->gcs",
        next_major,
        matrix_next[:, :, :row_count],
        preferred_element_type=jnp.float32,
    )
    grad_mid = (incoming.astype(jnp.float32) + token_major(back_here + back_next)).astype(
        jnp.bfloat16
    )
    mr_grad = lag_grads_major(weighted_major, mid_major, keep_here)
    grad_gate_se = (grad_mid.astype(jnp.float32) * se_mix).astype(jnp.bfloat16)
    weighted_se = (gate_se.astype(jnp.float32) * grad_mid.astype(jnp.float32)).astype(jnp.bfloat16)
    after_rows = from_behind(weighted_se[:rim_rows], "ctx", -1)
    after_ext = jnp.concatenate([weighted_se, after_rows], axis=0)
    starts_ext = jnp.concatenate([start_here, start_next[:rim_rows] + row_count])
    grad_x = (grad_mid.astype(jnp.float32) + short_back(after_ext, taps_se, starts_ext)).astype(
        jnp.bfloat16
    )
    se_grad = short_taps_grad(weighted_se, input_ext, taps_se, start_here)
    scale = 1.0 / math.sqrt(ctx_count * row_count * GROUP)
    se_total, mr_total = lax.psum((se_grad, mr_grad), "ctx")
    return (
        grad_x[None],
        grad_gate_se[None],
        grad_gate_mr[None],
        (se_total * scale)[None],
        (mr_total * scale)[None],
    )


def solution(mesh):
    return jax.shard_map(
        body,
        mesh=mesh,
        in_specs=(
            P("pipe", "ctx", None, None),
            P("ctx"),
            P("ctx"),
            P(),
            P("pipe", "ctx", None),
            P("pipe", "ctx", None),
            P("pipe", "ctx", None),
            P("pipe", None, None),
            P("pipe", None, None),
        ),
        out_specs=(
            P("pipe", "ctx", None),
            P("pipe", "ctx", None),
            P("pipe", "ctx", None),
            P("pipe", None, None),
            P("pipe", None, None),
        ),
        check_vma=False,
    )
```

profile of v0, /device:TPU:0, one launch (start us, length us, event | category | flops | bytes accessed | tf_op | source)
XLA Modules:
  0.0 471.6 jit_solution(7010963330927730759)
XLA Ops:
  7.2 1.7 fusion.69
  14.0 5.9 %collective-permute-start.3 = (bf16[128,4096]{0,1:T(8,128)(2,1)}, bf16[128,4096]{0,1:T(8,128)(2,1)}, u32[]{:S(2)}, u32[]{:S(2)}) collective-permute-start(bf16[128,4096]{0,1:T(8,128)(2,1)} %bitcast_select_fusion), channel_id=1, source_target_pairs={{0,2},{2,4},{4,6},{6,8},{8,10},{10,12},{12,14},{14,16},{16,18},{18... | collective-permute-start | bytes 3145736 | tf_op jit(solution)/shard_map/ppermute | solution.py:17
  26.0 6.3 %broadcast_in_dim.234 = bf16[256,128,257]{0,2,1:T(8,128)(2,1)} broadcast(bf16[256,257]{0,1:T(8,128)(2,1)S(1)} %copy.44), dimensions={0,2} | broadcast | bytes 16974336 | tf_op jit(solution)/shard_map/broadcast_in_dim | solution.py:39
  32.3 19.2 %reshape.224 = bf16[256,32896]{0,1:T(8,128)(2,1)} reshape(bf16[256,128,257]{0,2,1:T(8,128)(2,1)} %broadcast_in_dim.234) | data formatting | bytes 33685504 | tf_op jit(solution)/shard_map/reshape | solution.py:41
  51.5 13.8 %slice.165 = bf16[256,32768]{0,1:T(8,128)(2,1)} slice(bf16[256,32896]{0,1:T(8,128)(2,1)} %reshape.224), slice={[0:256], [0:32768]} | slice | bytes 33554432 | tf_op jit(solution)/shard_map/slice | solution.py:42
  65.3 23.0 %copy.56 = bf16[256,128,256]{2,1,0:T(8,128)(2,1)} copy(bf16[256,128,256]{0,2,1:T(8,128)(2,1)} %bitcast.110) | data formatting | bytes 33554432 | tf_op jit(solution)/shard_map/reshape | solution.py:42
  88.3 1.3 copy.43
  91.3 3.7 collective-permute-start.4
  95.0 2.0 collective-permute-done.4
  97.5 8.6 %fusion.28 = (bf16[128,4096]{0,1:T(8,128)(2,1)S(1)}, f32[128,4096]{0,1:T(8,128)}) fusion(bf16[128,4096]{0,1:T(8,128)(2,1)S(1)} %bitcast_select_fusion.1, bf16[1,128,4096]{1,2,0:T(8,128)(2,1)S(1)} %copy.46, bf16[8,4096]{0,1:T(8,128)(2,1)S(1)} %copy.52, f32[4096]{0:T(1024)S(1)} %bitcast.117, pred[128]{0:T(512)(128)(4,1)S(1)} %get-tuple-element.152, ...), kind=kLoop, calls=%fused_computation.76 | loop fusion | flops 25690112 | bytes 5424000 | tf_op jit(solution)/shard_map/convert_element_type | solution.py:170
  106.0 4.4 collective-permute-start.5
  110.5 14.0 %broadcast_select_fusion.1 = bf16[256,128,256]{2,1,0:T(8,128)(2,1)} fusion(bf16[256,128,256]{2,1,0:T(8,128)(2,1)} %copy.56, pred[128,256]{1,0:T(8,128)(4,1)S(1)} %get-tuple-element.150), kind=kLoop, calls=%fused_computation.10 | loop fusion | flops 8388608 | bytes 33587200 | tf_op jit(solution)/shard_map/jit(_where)/select_n | solution.py:45
  124.5 8.2 %collective-permute-done.5 = bf16[128,4096]{0,1:T(8,128)(2,1)S(1)} collective-permute-done((bf16[128,4096]{0,1:T(8,128)(2,1)S(1)}, bf16[128,4096]{0,1:T(8,128)(2,1)S(1)}, u32[]{:S(2)}, u32[]{:S(2)}) %collective-permute-start.5) | collective-permute-done | bytes 1048608 | tf_op jit(solution)/shard_map/ppermute | solution.py:17
  132.9 11.6 %fusion.74 = f32[256,16,128]{2,1,0:T(8,128)} fusion(bf16[256,16,256]{2,1,0:T(8,128)(2,1)S(1)} %bitcast.111, bf16[256,128,256]{2,1,0:T(8,128)(2,1)} %broadcast_select_fusion.1), kind=kOutput, calls=%fused_computation.149 | convolution fusion | flops 268435456 | bytes 20971520 | tf_op jit(solution)/shard_map/gcs,grs->gcr/dot_general | solution.py:176
  144.5 3.9 fusion.31
  148.4 1.5 collective-permute-start.1
  149.8 121.6 %while.13 = (s32[]{:T(128)}, f32[4,64,128]{2,1,0:T(8,128)}, bf16[4,64,16,128]{3,2,1,0:T(8,128)(2,1)}, bf16[4,64,16,256]{3,2,1,0:T(8,128)(2,1)S(1)}, s32[128]{0:T...) while((s32[]{:T(128)}, f32[4,64,128]{2,1,0:T(8,128)}, ...), condition=%wide.region_17.18_spmd.clone, body=%wide.region_15.17_spmd.clone.sunk | while | flops 70279168 | bytes 64031332 | solution.py:81
  150.0 2.3 broadcast_select_fusion.3
  152.2 4.7 %copy.64 = f32[8,8,128,256]{3,1,2,0:T(8,128)S(1)} copy(f32[8,8,128,256]{3,2,1,0:T(8,128)S(1)} %bitcast.109) | data formatting | bytes 16777216 | tf_op jit(solution)/shard_map/while
  157.0 3.8 pad.181
  160.8 14.1 %reshape.246 = f32[64,128,257]{2,1,0:T(8,128)} reshape(f32[64,32896]{1,0:T(8,128)} %pad.181) | data formatting | bytes 16842752 | tf_op jit(solution)/shard_map/while/body/eval_jaxpr/reshape | solution.py:54
  174.9 4.6 slice_reduce_fusion.2
  180.3 2.3 broadcast_select_fusion.3
  182.6 4.7 %copy.64 = f32[8,8,128,256]{3,1,2,0:T(8,128)S(1)} copy(f32[8,8,128,256]{3,2,1,0:T(8,128)S(1)} %bitcast.109) | data formatting | bytes 16777216 | tf_op jit(solution)/shard_map/while
  187.3 3.8 pad.181
  191.2 14.1 %reshape.246 = f32[64,128,257]{2,1,0:T(8,128)} reshape(f32[64,32896]{1,0:T(8,128)} %pad.181) | data formatting | bytes 16842752 | tf_op jit(solution)/shard_map/while/body/eval_jaxpr/reshape | solution.py:54
  205.3 4.6 slice_reduce_fusion.2
  210.7 2.3 broadcast_select_fusion.3
  213.0 4.7 %copy.64 = f32[8,8,128,256]{3,1,2,0:T(8,128)S(1)} copy(f32[8,8,128,256]{3,2,1,0:T(8,128)S(1)} %bitcast.109) | data formatting | bytes 16777216 | tf_op jit(solution)/shard_map/while
  217.7 3.8 pad.181
  221.6 14.1 %reshape.246 = f32[64,128,257]{2,1,0:T(8,128)} reshape(f32[64,32896]{1,0:T(8,128)} %pad.181) | data formatting | bytes 16842752 | tf_op jit(solution)/shard_map/while/body/eval_jaxpr/reshape | solution.py:54
  235.7 4.6 slice_reduce_fusion.2
  241.1 2.3 broadcast_select_fusion.3
  243.4 4.7 %copy.64 = f32[8,8,128,256]{3,1,2,0:T(8,128)S(1)} copy(f32[8,8,128,256]{3,2,1,0:T(8,128)S(1)} %bitcast.109) | data formatting | bytes 16777216 | tf_op jit(solution)/shard_map/while
  248.1 3.8 pad.181
  252.0 14.1 %reshape.246 = f32[64,128,257]{2,1,0:T(8,128)} reshape(f32[64,32896]{1,0:T(8,128)} %pad.181) | data formatting | bytes 16842752 | tf_op jit(solution)/shard_map/while/body/eval_jaxpr/reshape | solution.py:54
  266.1 4.6 slice_reduce_fusion.2
  271.5 2.3 copy.55
  273.8 107.9 %all-reduce.3.cloned.1.call-done = f32[256,128]{1,0:T(8,128)} async-done(((f32[256,128]{1,0:T(8,128)}), f32[256,128]{1,0:T(8,128)}) %all-reduce.3.cloned.1.call-update) | async-done | bytes 131088 | tf_op jit(solution)/shard_map/psum | solution.py:212
  381.7 1.6 multiply_bitcast_fusion
  383.3 6.0 %fusion.7 = f32[256,16,128]{2,1,0:T(8,128)S(1)} fusion(bf16[256,16,128]{2,1,0:T(8,128)(2,1)} %bitcast.10, bf16[256,128,256]{2,1,0:T(8,128)(2,1)} %copy.56, pred[128,128]{1,0:T(8,128)(4,1)S(1)} %slice.167), kind=kOutput, calls=%fused_computation.12 | convolution fusion | flops 138412032 | bytes 11550720 | tf_op jit(solution)/shard_map/gcr,grs->gcs/dot_general | solution.py:192
  389.3 6.2 %fusion.73 = f32[256,16,128]{2,1,0:T(8,128)S(1)} fusion(f32[256,16,128]{2,1,0:T(8,128)S(1)} %fusion.7, bf16[256,16,128]{2,1,0:T(8,128)(2,1)} %bitcast.4, bf16[256,128,256]{2,1,0:T(8,128)(2,1)} %broadcast_select_fusion.1), kind=kOutput, calls=%fused_computation.148 | convolution fusion | flops 134742016 | bytes 13631488 | tf_op jit(solution)/shard_map/gcr,grs->gcs/dot_general | solution.py:186
  395.5 8.2 %fusion.52 = (f32[4096]{0:T(1024)S(1)}, f32[4096]{0:T(1024)S(1)}, f32[4096]{0:T(1024)S(1)}, f32[4096]{0:T(1024)S(1)}, f32[4096]{0:T(1024)S(1)}, /*index=5*/f32[4...) fusion(pred[128]{0:T(512)(128)(4,1)S(1)} %get-tuple-element.152, ...), kind=kLoop, calls=%fused_computation.100 | loop fusion | flops 26189824 | bytes 7504640 | tf_op jit(solution)/shard_map/reduce_sum | solution.py:118
  407.5 42.4 %psum.14 = f32[256,7]{0,1:T(8,128)S(1)} all-reduce(f32[256,7]{0,1:T(8,128)S(1)} %stack.31), channel_id=1, replica_groups=mesh['ctx'=16,'pipe'=2] {'ctx'}, use_global_device_ids=true, to_apply=%region_14.15 | all-reduce | flops 1792 | bytes 14336 | tf_op jit(solution)/shard_map/psum | solution.py:212
  449.9 1.8 fusion.53
  451.7 1.3 copy.54
  454.1 8.4 %fusion.64 = bf16[1,128,4096]{1,2,0:T(8,128)(2,1)} fusion(bf16[8,4096]{0,1:T(8,128)(2,1)S(1)} %copy.48, bf16[128,4096]{0,1:T(8,128)(2,1)S(1)} %get-tuple-element.126, f32[4096]{0:T(1024)S(1)} %bitcast.118, pred[128]{0:T(512)(128)(4,1)S(1)} %get-tuple-element.144, f32[4096]{0:T(1024)S(1)} %bitcast.120, pred[128]{0:T(512)(128)(4,1)S(1)} %get-tuple-element.145, ...), kind=kLoop, calls=%fused_computation.117 | loop fusion | flops 25165824 | bytes 3326848 | tf_op jit(solution)/shard_map/broadcast_in_dim | solution.py:214
  462.5 2.3 copy.53
  (95 shorter events, 16.7 us)
Async XLA Ops:
  7.2 374.6 %all-reduce.3.cloned.1.call-start = ((), (), s32[]{:S(2)}) async-start(), calls=%async_computation | async-start | bytes 262144 | tf_op jit(solution)/shard_map/psum | solution.py:212
  8.9 2.1 copy-start.10
  10.2 9.7 %copy-start.4 = (bf16[1,128,4096]{2,1,0:T(8,128)(2,1)S(1)}, bf16[1,128,4096]{2,1,0:T(8,128)(2,1)}, u32[]{:S(2)}) copy-start(bf16[1,128,4096]{2,1,0:T(8,128)(2,1)} %param.17) | copy-start | bytes 3145732
  12.9 9.1 %copy-start.9 = (s32[16]{0:T(128)S(1)}, s32[16]{0:T(128)}, u32[]{:S(2)}) copy-start(s32[16]{0:T(128)} %param.14) | copy-start | bytes 196
  14.0 9.9 %copy-start.5 = (bf16[1,128,4096]{2,1,0:T(8,128)(2,1)S(1)}, bf16[1,128,4096]{2,1,0:T(8,128)(2,1)}, u32[]{:S(2)}) copy-start(bf16[1,128,4096]{2,1,0:T(8,128)(2,1)} %param.15) | copy-start | bytes 3145732
  14.0 10.6 %copy-start.8 = (f32[1,256,7]{1,0,2:T(1,128)S(1)}, f32[1,256,7]{1,0,2:T(1,128)}, u32[]{:S(2)}) copy-start(f32[1,256,7]{1,0,2:T(1,128)} %param.18) | copy-start | bytes 21508
  14.0 76.5 %collective-permute-start.3 = (bf16[128,4096]{0,1:T(8,128)(2,1)}, bf16[128,4096]{0,1:T(8,128)(2,1)}, u32[]{:S(2)}, u32[]{:S(2)}) collective-permute-start(bf16[128,4096]{0,1:T(8,128)(2,1)} %bitcast_select_fusion), channel_id=1, source_target_pairs={{0,2},{2,4},{4,6},{6,8},{8,10},{10,12},{12,14},{14,16},{16,18},{18... | collective-permute-start | bytes 3145736 | tf_op jit(solution)/shard_map/ppermute | solution.py:17
  21.2 4.2 copy-start.7
  21.2 123.2 %collective-permute-start = (bf16[1,128,4096]{1,2,0:T(8,128)(2,1)}, bf16[1,128,4096]{1,2,0:T(8,128)(2,1)}, u32[]{:S(2)}, u32[]{:S(2)}) collective-permute-start(bf16[1,128,4096]{1,2,0:T(8,128)(2,1)} %copy.42), channel_id=1, source_target_pairs={{0,1},{1,0},{2,3},{3,2},{4,5},{5,4},{6,7},{7,6},{8,9},{9,8},{10,11... | collective-permute-start | bytes 3145736 | tf_op jit(solution)/shard_map/ppermute | solution.py:23
  24.6 72.8 %copy-start = (bf16[1,128,4096]{1,2,0:T(8,128)(2,1)}, bf16[1,128,4096]{1,2,0:T(8,128)(2,1)S(1)}, u32[]{:S(2)}) copy-start(bf16[1,128,4096]{1,2,0:T(8,128)(2,1)S(1)} %copy.46) | copy-start | bytes 3145732
  65.3 23.0 %copy-start.6 = (bf16[1,128,4096]{2,1,0:T(8,128)(2,1)S(1)}, bf16[1,128,4096]{2,1,0:T(8,128)(2,1)}, u32[]{:S(2)}) copy-start(bf16[1,128,4096]{2,1,0:T(8,128)(2,1)} %param.16) | copy-start | bytes 3145732
  91.3 5.6 %collective-permute-start.4 = (bf16[8,4096]{1,0:T(8,128)(2,1)S(1)}, bf16[8,4096]{1,0:T(8,128)(2,1)S(1)}, u32[]{:S(2)}, u32[]{:S(2)}) collective-permute-start(bf16[8,4096]{1,0:T(8,128)(2,1)S(1)} %copy.51), channel_id=1, source_target_pairs={{0,2},{2,4},{4,6},{6,8},{8,10},{10,12},{12,14},{14,16},{16,18},{18... | collective-permute-start | bytes 196616 | tf_op jit(solution)/shard_map/ppermute | solution.py:17
  97.4 8.6 %copy-start.2 = (bf16[8,4096]{0,1:T(8,128)(2,1)}, bf16[8,4096]{0,1:T(8,128)(2,1)S(1)}, u32[]{:S(2)}) copy-start(bf16[8,4096]{0,1:T(8,128)(2,1)S(1)} %copy.52) | copy-start | bytes 196612
  106.0 26.6 %collective-permute-start.5 = (bf16[128,4096]{0,1:T(8,128)(2,1)S(1)}, bf16[128,4096]{0,1:T(8,128)(2,1)S(1)}, u32[]{:S(2)}, u32[]{:S(2)}) collective-permute-start(bf16[128,4096]{0,1:T(8,128)(2,1)S(1)} %get-tuple-element.128), channel_id=1, source_target_pairs={{0,2},{2,4},{4,6},{6,8},{8,10},{10,12},{12,14},{14,16},{16,18},{18... | collective-permute-start | bytes 3145736 | tf_op jit(solution)/shard_map/ppermute | solution.py:17
  148.4 234.9 %collective-permute-start.1 = (bf16[128,4096]{0,1:T(8,128)(2,1)}, bf16[128,4096]{0,1:T(8,128)(2,1)}, u32[]{:S(2)}, u32[]{:S(2)}) collective-permute-start(bf16[128,4096]{0,1:T(8,128)(2,1)} %get-tuple-element.135), channel_id=1, source_target_pairs={{2,0},{4,2},{6,4},{8,6},{10,8},{12,10},{14,12},{16,14},{18,16},{20... | collective-permute-start | bytes 3145736 | tf_op jit(solution)/shard_map/ppermute | solution.py:17
  389.3 6.2 %copy-start.1 = (bf16[1,128,4096]{1,2,0:T(8,128)(2,1)S(1)}, bf16[1,128,4096]{1,2,0:T(8,128)(2,1)}, u32[]{:S(2)}) copy-start(bf16[1,128,4096]{1,2,0:T(8,128)(2,1)} %copy-done) | copy-start | bytes 3145732
  389.3 6.2 %copy-start.3 = (bf16[8,4096]{0,1:T(8,128)(2,1)S(1)}, bf16[8,4096]{0,1:T(8,128)(2,1)}, u32[]{:S(2)}) copy-start(bf16[8,4096]{0,1:T(8,128)(2,1)} %copy-done.2) | copy-start | bytes 196612
  404.7 49.0 %collective-permute-start.2 = (bf16[8,4096]{1,0:T(8,128)(2,1)S(1)}, bf16[8,4096]{1,0:T(8,128)(2,1)S(1)}, u32[]{:S(2)}, u32[]{:S(2)}) collective-permute-start(bf16[8,4096]{1,0:T(8,128)(2,1)S(1)} %copy.47), channel_id=1, source_target_pairs={{2,0},{4,2},{6,4},{8,6},{10,8},{12,10},{14,12},{16,14},{18,16},{20... | collective-permute-start | bytes 196616 | tf_op jit(solution)/shard_map/ppermute | solution.py:17
Sparse Core Ops, SparseCore 0:
  271.6 110.1 all-reduce.2
where the time goes:
time: 475 us; the launch traced here: 472 us
  local copies, waits for them, and re-layouts  174 us (37%)
  waiting for transfers between devices  118 us (25%)
  other arithmetic  68.4 us (14%)
  blocking collectives  42.4 us (9%)
  matrix products  32.8 us (7%)
  between operations  19.2 us (4%)
  starting transfers between devices  16.8 us (4%)
    psum x1, waiting for transfers between devices, body(): se_total, mr_total = lax.psum((se_grad, mr_grad), 'ctx')  108 us
    reshape x4, local copies, waits for them, and re-layouts, tap_sums(): lagged = flat.reshape(group_count, row_count, col_count + 1)  56.6 us
    psum x1, blocking collectives, body(): se_total, mr_total = lax.psum((se_grad, mr_grad), 'ctx')  42.4 us
    reshape x1, local copies, waits for them, and re-layouts, toeplitz_rows(): spread_rows[:, :row_count * col_count]  23 us
    reshape x1, local copies, waits for them, and re-layouts, toeplitz_rows(): spread_rows = jnp.broadcast_to(tap_line[:, None, :], (group_count, row_co...  19.2 us
    while x4, local copies, waits for them, and re-layouts  18.9 us
    reduce_sum x4, other arithmetic, tap_sums(): return jnp.sum(lagged[:, :, 1:row_count + 1], axis=1)[:, ::-1]  18.5 us
    ppermute x5, starting transfers between devices, from_behind(): return lax.ppermute(block, axis, route)  16.8 us
  transfers between devices with their start and end apart: 7, of which 3 were waited for; matrix products, arithmetic and copies ran while one was open for 50% of the time, Pallas kernels for 0%

commit v1 on v0

v1 whole, which is shorter than its diff:
```python
import functools
import math

import jax
import jax.numpy as jnp
from jax import lax
from jax.experimental import pallas as pl
from jax.experimental.pallas import tpu as pltpu
from jax.sharding import PartitionSpec as P

GROUP = 16
LANES = 128
PER_BLOCK = LANES // GROUP
RIM = 8
FAR = 1 << 20
PIECES = 2
BLOCK = 512

F32 = jnp.float32
BF16 = jnp.bfloat16


def from_behind(block, axis, distance):
    devices = range(lax.axis_size(axis))
    route = [(i - distance, i) for i in devices if i - distance in devices]
    return lax.ppermute(block, axis, route)


def partner(value, axis, mask):
    pairs = [(source, source ^ mask) for source in range(lax.axis_size(axis))]
    return lax.ppermute(value, axis, pairs)


def grid_of(rows, which):
    return lax.broadcasted_iota(jnp.int32, (rows, rows), which)


def same_tile(out_row, in_row, bound):
    return (out_row >= in_row) & ((out_row < bound) | (in_row >= bound))


def tile_before(out_row, in_row, bound, earlier, rows):
    return (out_row < in_row) & (out_row < bound) & ((earlier >= rows) | (in_row >= earlier))


def as_mask(flags, dtype):
    return jnp.where(flags, 1.0, 0.0).astype(F32).astype(dtype)


def room_of(row, bound, earlier, rows):
    before = jnp.where(earlier < rows, row + (rows - earlier), FAR)
    return jnp.where(row >= bound, row - bound, before)


def rolled(line, rows):
    return pltpu.roll(jnp.broadcast_to(line, (rows, rows)), 0, 1, stride=1, stride_axis=0)


def lanes(start):
    return pl.ds(start, LANES)


def middle_kernel(sc, slot, arrived, rim_a, rim_b, gate, taps, hr, x_out, mid_out, mix_out, own_out, ext, room, mask):
    rows = slot.shape[0]
    earlier, bound, has_own = sc[0], sc[1], sc[3]

    @pl.when(pl.program_id(0) == 0)
    def _():
        row = lax.broadcasted_iota(jnp.int32, (rows, LANES), 0)
        room[...] = room_of(row, bound, earlier, rows)
        mask[...] = as_mask(same_tile(grid_of(rows, 0), grid_of(rows, 1), bound), BF16)

    lane_group = lax.broadcasted_iota(jnp.int32, (rows, LANES), 1) // GROUP
    for block in range(slot.shape[1] // LANES):
        at = lanes(block * LANES)
        x = jnp.where(has_own > 0, slot[:, at].astype(F32), arrived[:, at].astype(F32))
        rim = rim_a[:, at].astype(F32) + rim_b[:, at].astype(F32)
        x_out[:, at] = x.astype(BF16)
        ext[block, :RIM] = rim
        ext[block, RIM:] = x
        mix = jnp.zeros((rows, LANES), F32)
        for lag in range(taps.shape[0] - 1):
            shifted = ext[block, RIM - lag : RIM - lag + rows]
            mix = mix + jnp.where(room[...] >= lag, taps[lag : lag + 1, at] * shifted, 0.0)
        mix_out[:, at] = mix
        mid = (x + gate[:, at].astype(F32) * mix).astype(BF16)
        mid_out[:, at] = mid
        own = jnp.zeros((rows, LANES), F32)
        for group in range(PER_BLOCK):
            at_group = block * PER_BLOCK + group
            matrix = rolled(hr[at_group : at_group + 1], rows).astype(BF16) * mask[...]
            product = jnp.dot(matrix, mid, preferred_element_type=F32)
            own = jnp.where(lane_group == group, product, own)
        own_out[:, at] = own


def middle(sc, slot, arrived, rim_a, rim_b, gate, taps, hr):
    rows, channels = gate.shape
    wide = lambda height: pl.BlockSpec((height, BLOCK), lambda i: (0, i))
    shape = lambda dtype: jax.ShapeDtypeStruct((rows, channels), dtype)
    return pl.pallas_call(
        middle_kernel,
        grid=(channels // BLOCK,),
        in_specs=[
            pl.BlockSpec(memory_space=pltpu.SMEM),
            wide(rows),
            wide(rows),
            wide(RIM),
            wide(RIM),
            wide(rows),
            wide(taps.shape[0]),
            pl.BlockSpec((BLOCK // GROUP, rows), lambda i: (i, 0)),
        ],
        out_specs=[wide(rows)] * 4,
        out_shape=[shape(BF16), shape(BF16), shape(F32), shape(F32)],
        scratch_shapes=[
            pltpu.VMEM((BLOCK // LANES, rows + RIM, LANES), F32),
            pltpu.VMEM((rows, LANES), jnp.int32),
            pltpu.VMEM((rows, rows), BF16),
        ],
        compiler_params=pltpu.CompilerParams(vmem_limit_bytes=40 << 20),
        cost_estimate=pl.CostEstimate(flops=2 * rows * rows * channels, bytes_accessed=18 * rows * channels, transcendentals=0),
    )(sc, slot, arrived, rim_a, rim_b, gate, taps, hr)


def back_kernel(
    shift, sc, weighted, after, incoming, mid, x, rim_a, rim_b, mix, gate, h,
    mid_grad, gate_grad, wse_out, lag_out, se_out,
    ext, room, mask_own, mask_next, lag_own, lag_next, flip,
):
    rows = weighted.shape[0]
    step = pl.program_id(0)
    earlier, bound, later = sc[0], sc[1], sc[2]

    @pl.when(step == 0)
    def _():
        row = lax.broadcasted_iota(jnp.int32, (rows, LANES), 0)
        room[...] = room_of(row, bound, earlier, rows)
        source, target = grid_of(rows, 0), grid_of(rows, 1)
        mask_own[...] = as_mask(same_tile(target, source, bound), BF16)
        mask_next[...] = as_mask(tile_before(target, source, later, bound, rows), BF16)
        mirrored = rows - 1 - source
        lag_own[...] = as_mask(same_tile(target, mirrored, bound), F32)
        lag_next[...] = as_mask(tile_before(target, mirrored, later, bound, rows), F32)
        flip[...] = as_mask(mirrored == target, BF16)
        se_out[...] = jnp.zeros_like(se_out)

    lane_group = lax.broadcasted_iota(jnp.int32, (rows, LANES), 1) // GROUP
    one_row = lax.broadcasted_iota(jnp.int32, (1, LANES), 1) // GROUP
    channel = grid_of(LANES, 0) // GROUP
    column = grid_of(LANES, 1)
    for block in range(weighted.shape[1] // LANES):
        at = lanes(block * LANES)
        pair = jnp.concatenate([weighted[:, at], after[:, at]], axis=0)
        total = jnp.zeros((rows, LANES), F32)
        for group in range(PER_BLOCK):
            at_group = block * PER_BLOCK + group
            circle = rolled(h[at_group : at_group + 1], rows).astype(BF16)
            matrix = jnp.concatenate([circle * mask_own[...], circle * mask_next[...]], axis=1)
            product = jnp.dot(matrix, pair, preferred_element_type=F32)
            total = jnp.where(lane_group == group, product, total)
        grad = (incoming[:, at].astype(F32) + total).astype(BF16)
        mid_grad[:, at] = grad
        grad_wide = grad.astype(F32)
        gate_grad[:, at] = (grad_wide * mix[:, at]).astype(BF16)
        wse = (gate[:, at].astype(F32) * grad_wide).astype(BF16)
        wse_out[:, at] = wse
        wse_wide = wse.astype(F32)
        ext[block, :RIM] = rim_a[:, at].astype(F32) + rim_b[:, at].astype(F32)
        ext[block, RIM:] = x[:, at].astype(F32)
        sums = []
        for lag in range(se_out.shape[0] - 1):
            shifted = ext[block, RIM - lag : RIM - lag + rows]
            sums.append(jnp.sum(jnp.where(room[...] >= lag, wse_wide * shifted, 0.0), axis=0, keepdims=True))
        sums.append(jnp.zeros((1, LANES), F32))
        place = shift + (step * (weighted.shape[1] // LANES) + block) * PER_BLOCK
        spread = as_mask(column == channel + place, F32)
        se_out[...] += jnp.dot(
            jnp.concatenate(sums, axis=0), spread, preferred_element_type=F32, precision=lax.Precision.HIGHEST
        )
        mirrored_mid = jnp.dot(flip[...], mid[:, at], preferred_element_type=F32).astype(BF16)
        lags = []
        for group in range(PER_BLOCK):
            chosen = mirrored_mid * as_mask(one_row == group, BF16)
            products = lax.dot_general(chosen, pair, (((1,), (1,)), ((), ())), preferred_element_type=F32)
            kept = products[:, :rows] * lag_own[...] + products[:, rows:] * lag_next[...]
            kept = pltpu.roll(kept, 1, 1, stride=1, stride_axis=0)
            lags.append(jnp.sum(kept, axis=0, keepdims=True))
        lag_out[block * PER_BLOCK : (block + 1) * PER_BLOCK] = jnp.concatenate(lags, axis=0)


def back(piece, pieces, sc, weighted, after, incoming, mid, x, rim_a, rim_b, mix, gate, h):
    rows, channels = weighted.shape
    part = channels // pieces
    groups = part // GROUP
    first = piece * part // BLOCK
    full = lambda height: pl.BlockSpec((height, BLOCK), lambda i: (0, first + i))
    own = lambda height: pl.BlockSpec((height, BLOCK), lambda i: (0, i))
    shape = lambda dtype: jax.ShapeDtypeStruct((rows, part), dtype)
    square = lambda dtype: pltpu.VMEM((rows, rows), dtype)
    return pl.pallas_call(
        functools.partial(back_kernel, (piece * groups) % LANES),
        grid=(part // BLOCK,),
        in_specs=[
            pl.BlockSpec(memory_space=pltpu.SMEM),
            full(rows),
            own(rows),
            full(rows),
            full(rows),
            full(rows),
            full(RIM),
            full(RIM),
            full(rows),
            full(rows),
            pl.BlockSpec((BLOCK // GROUP, rows), lambda i: (first + i, 0)),
        ],
        out_specs=[
            own(rows),
            own(rows),
            own(rows),
            pl.BlockSpec((BLOCK // GROUP, rows), lambda i: (i, 0)),
            pl.BlockSpec((RIM, LANES), lambda i: (0, 0)),
        ],
        out_shape=[
            shape(BF16),
            shape(BF16),
            shape(BF16),
            jax.ShapeDtypeStruct((groups, rows), F32),
            jax.ShapeDtypeStruct((RIM, LANES), F32),
        ],
        scratch_shapes=[
            pltpu.VMEM((BLOCK // LANES, rows + RIM, LANES), F32),
            pltpu.VMEM((rows, LANES), jnp.int32),
            square(BF16),
            square(BF16),
            square(F32),
            square(F32),
            square(BF16),
        ],
        compiler_params=pltpu.CompilerParams(vmem_limit_bytes=40 << 20),
        cost_estimate=pl.CostEstimate(flops=8 * rows * rows * part, bytes_accessed=22 * rows * part, transcendentals=0),
    )(sc, weighted, after, incoming, mid, x, rim_a, rim_b, mix, gate, h)


def input_kernel(sc, *refs):
    pieces = (len(refs) - 5) // 2
    grads, wses = refs[:pieces], refs[pieces : 2 * pieces]
    rim, taps, out, ext, room = refs[2 * pieces :]
    rows = out.shape[0]
    bound, later = sc[1], sc[2]
    step = pl.program_id(0)

    @pl.when(step == 0)
    def _():
        row = lax.broadcasted_iota(jnp.int32, (rows, LANES), 0)
        room[:rows] = room_of(row, bound, sc[0], rows)
        rim_row = lax.broadcasted_iota(jnp.int32, (RIM, LANES), 0)
        room[rows:] = room_of(rim_row, later, bound, rows)

    per = pl.num_programs(0) // pieces
    for piece in range(pieces):

        @pl.when((step >= piece * per) & (step < (piece + 1) * per))
        def _(piece=piece):
            for block in range(out.shape[1] // LANES):
                at = lanes(block * LANES)
                ext[block, :rows] = wses[piece][:, at].astype(F32)
                ext[block, rows:] = rim[:, at].astype(F32)
                total = grads[piece][:, at].astype(F32)
                for lag in range(taps.shape[0] - 1):
                    shifted = ext[block, lag : lag + rows]
                    total = total + jnp.where(room[lag : lag + rows] >= lag, taps[lag : lag + 1, at] * shifted, 0.0)
                out[:, at] = total.astype(BF16)


def input_grad(sc, grads, wses, rim, taps):
    pieces = len(grads)
    rows = grads[0].shape[0]
    channels = rim.shape[1]
    per = channels // BLOCK // pieces
    wide = lambda height: pl.BlockSpec((height, BLOCK), lambda i: (0, i))
    held = [
        pl.BlockSpec((rows, BLOCK), lambda i, piece=piece: (0, jnp.clip(i - piece * per, 0, per - 1)))
        for piece in range(pieces)
    ]
    return pl.pallas_call(
        input_kernel,
        grid=(channels // BLOCK,),
        in_specs=[pl.BlockSpec(memory_space=pltpu.SMEM), *held, *held, wide(RIM), wide(taps.shape[0])],
        out_specs=wide(rows),
        out_shape=jax.ShapeDtypeStruct((rows, channels), BF16),
        scratch_shapes=[
            pltpu.VMEM((BLOCK // LANES, rows + RIM, LANES), F32),
            pltpu.VMEM((rows + RIM, LANES), jnp.int32),
        ],
        compiler_params=pltpu.CompilerParams(vmem_limit_bytes=40 << 20),
        cost_estimate=pl.CostEstimate(flops=14 * rows * channels, bytes_accessed=6 * rows * channels, transcendentals=0),
    )(sc, *grads, *wses, rim, taps)


def gate_kernel(sc, prior, own, incoming, hr, *rest):
    out, mask = rest[-2:]
    rows = prior.shape[0]

    @pl.when(pl.program_id(0) == 0)
    def _():
        mask[...] = as_mask(tile_before(grid_of(rows, 0), grid_of(rows, 1), sc[1], sc[0], rows), BF16)

    lane_group = lax.broadcasted_iota(jnp.int32, (rows, LANES), 1) // GROUP
    for block in range(prior.shape[1] // LANES):
        at = lanes(block * LANES)
        total = jnp.zeros((rows, LANES), F32)
        for group in range(PER_BLOCK):
            at_group = block * PER_BLOCK + group
            matrix = rolled(hr[at_group : at_group + 1], rows).astype(BF16) * mask[...]
            product = jnp.dot(matrix, prior[:, at], preferred_element_type=F32)
            total = jnp.where(lane_group == group, product, total)
        out[:, at] = (incoming[:, at].astype(F32) * (own[:, at] + total)).astype(BF16)


def gate_grad(piece, pieces, sc, prior, own, incoming, hr, held):
    rows, channels = own.shape
    part = channels // pieces
    first = piece * part // BLOCK
    full = lambda: pl.BlockSpec((rows, BLOCK), lambda i: (0, first + i))
    return pl.pallas_call(
        gate_kernel,
        grid=(part // BLOCK,),
        in_specs=[
            pl.BlockSpec(memory_space=pltpu.SMEM),
            pl.BlockSpec((rows, BLOCK), lambda i: (0, i)),
            full(),
            full(),
            pl.BlockSpec((BLOCK // GROUP, rows), lambda i: (first + i, 0)),
        ]
        + [pl.BlockSpec(memory_space=pl.ANY)] * len(held),
        out_specs=full(),
        out_shape=jax.ShapeDtypeStruct((rows, channels), BF16),
        scratch_shapes=[pltpu.VMEM((rows, rows), BF16)],
        input_output_aliases={5: 0} if held else {},
        compiler_params=pltpu.CompilerParams(vmem_limit_bytes=40 << 20),
        cost_estimate=pl.CostEstimate(flops=2 * rows * rows * part, bytes_accessed=10 * rows * part, transcendentals=0),
    )(sc, prior, own, incoming, hr, *held)


def body(loaded, counts, destinations, bounds, se_gate, mr_gate, phase_grads, se_taps, mr_taps):
    ctx_count = lax.axis_size("ctx")
    shard_index = lax.axis_index("ctx")
    slots = loaded[0]
    rows, channels = slots.shape[1], slots.shape[2]
    group_count = channels // GROUP
    part = channels // PIECES
    held_count = counts[0]
    first_dest, second_dest = destinations[0], destinations[1]
    own_tile = (held_count >= 1) & (first_dest == shard_index)
    send_first = (held_count >= 1) & (first_dest == shard_index + 1)
    send_second = (held_count >= 2) & (second_dest == shard_index + 1)

    incoming = partner(phase_grads[0], "pipe", 1)
    outgoing = lax.dynamic_index_in_dim(slots, jnp.where(send_first, 0, 1), 0, False)
    arrived = from_behind(outgoing, "ctx", 1)

    nothing = jnp.zeros((), BF16)
    tail_own = jnp.where(own_tile, slots[0, rows - RIM :], nothing)
    tail_sent = jnp.where(send_first | send_second, outgoing[rows - RIM :], nothing)
    rim_a = from_behind(tail_own, "ctx", 1)
    rim_b = from_behind(tail_sent, "ctx", 2)

    tile_total = bounds.shape[0]

    def bound_at(tile_num):
        inside = (tile_num >= 0) & (tile_num < tile_total)
        return jnp.where(inside, bounds[jnp.clip(tile_num, 0, tile_total - 1)], rows)

    sc = jnp.stack(
        [bound_at(shard_index - 1), bound_at(shard_index), bound_at(shard_index + 1), own_tile.astype(jnp.int32)]
    ).astype(jnp.int32)
    taps_low = mr_taps[0].astype(BF16).astype(F32)
    taps_back = jnp.roll(taps_low[:, ::-1], 1, axis=1)
    taps_se = jnp.repeat(jnp.pad(se_taps[0].T, ((0, 1), (0, 0))), GROUP, axis=1)
    gate_se = se_gate[0]

    weighted = (mr_gate[0].astype(F32) * incoming.astype(F32)).astype(BF16)
    after = [from_behind(weighted[:, q * part : (q + 1) * part], "ctx", -1) for q in range(PIECES)]

    layer_input, mid, se_mix, mr_own = middle(sc, slots[0], arrived, rim_a, rim_b, gate_se, taps_se, taps_back)
    prior = [from_behind(mid[:, q * part : (q + 1) * part], "ctx", 1) for q in range(PIECES)]

    done = [
        back(q, PIECES, sc, weighted, after[q], incoming, mid, layer_input, rim_a, rim_b, se_mix, gate_se, taps_low)
        for q in range(PIECES)
    ]
    mid_grads, gate_grads, wses, lags, se_sums = zip(*done)
    rim_next = from_behind(jnp.concatenate([wse[:RIM] for wse in wses], axis=1), "ctx", -1)
    grad_x = input_grad(sc, mid_grads, wses, rim_next, taps_se)
    grad_gate_se = jnp.concatenate(gate_grads, axis=1)

    grad_gate_mr = ()
    for q in range(PIECES):
        grad_gate_mr = (gate_grad(q, PIECES, sc, prior[q], mr_own, incoming, taps_back, grad_gate_mr),)
    grad_gate_mr = grad_gate_mr[0]

    total = jnp.concatenate([*lags, *se_sums], axis=0)
    mask = ctx_count // 2
    while mask:
        total = total + partner(total, "ctx", mask)
        mask //= 2
    scale = 1.0 / math.sqrt(ctx_count * rows * GROUP)
    total = total * scale
    mr_total = total[:group_count]
    windows = max(group_count // LANES, 1)
    se_total = total[group_count:].reshape(windows, PIECES // windows, RIM, LANES).sum(axis=1)
    se_total = se_total.transpose(0, 2, 1).reshape(group_count, RIM)[:, : se_taps.shape[2]]
    return (grad_x[None], grad_gate_se[None], grad_gate_mr[None], se_total[None], mr_total[None])


def solution(mesh):
    return jax.shard_map(
        body,
        mesh=mesh,
        in_specs=(
            P("pipe", "ctx", None, None),
            P("ctx"),
            P("ctx"),
            P(),
            P("pipe", "ctx", None),
            P("pipe", "ctx", None),
            P("pipe", "ctx", None),
            P("pipe", None, None),
            P("pipe", None, None),
        ),
        out_specs=(
            P("pipe", "ctx", None),
            P("pipe", "ctx", None),
            P("pipe", "ctx", None),
            P("pipe", None, None),
            P("pipe", None, None),
        ),
        check_vma=False,
    )
```

time: 475 us -> 150 us (0.32)
  local copies, waits for them, and re-layouts: 174 us -> 12.9 us
  waiting for transfers between devices: 118 us -> 51.3 us
  other arithmetic: 68.4 us -> 5.44 us
  Pallas kernels: 0 us -> 43.9 us
  blocking collectives: 42.4 us -> 0 us
  matrix products: 32.8 us -> 0 us
  between operations: 19.2 us -> 5.54 us
  starting transfers between devices: 16.8 us -> 29.2 us
    psum x1 -> x0, waiting for transfers between devices: 108 us -> none  [body(): se_total, mr_total = lax.psum((se_grad, mr_grad), 'ctx')]
    reshape x14 -> x2, local copies, waits for them, and re-layouts: 100 us -> 1.85 us  [the longest x1 1.85 us: body(): taps_se = jnp.repeat(jnp.pad(se_taps[0].T, ((0, 1), (0, 0))), GROUP, axis=1)]
    pallas_call x0 -> x6, Pallas kernels: none -> 43.9 us  [the longest x2 23.5 us: back(): pl.pallas_call(functools.partial(back_kernel, piece * groups % LANES), gr...]
    psum x1 -> x0, blocking collectives: 42.4 us -> none  [body(): se_total, mr_total = lax.psum((se_grad, mr_grad), 'ctx')]
    dot_general x7 -> x0, matrix products: 32.8 us -> none  [the longest x1 11.6 us: body(): jnp.einsum('gcs,grs->gcr', mid_major, matrix_here, preferred_element_type...]
    reduce_sum x13 -> x0, other arithmetic: 28 us -> none  [the longest x4 18.5 us: tap_sums(): return jnp.sum(lagged[:, :, 1:row_count + 1], axis=1)[:, ::-1]]
    ppermute x1 -> x5, waiting for transfers between devices: 0.01 us -> 25.1 us  [partner(): return lax.ppermute(value, axis, pairs)]
    while x4 -> x0, local copies, waits for them, and re-layouts: 18.9 us -> none
  transfers between devices with their start and end apart: 7 -> 13, of which waited for: 3 -> 4; matrix products, arithmetic and copies ran while one was open for 50% -> 11% of each run, Pallas kernels for 0% -> 22%
where the time goes in v1:
time: 150 us; the launch traced here: 148 us
  waiting for transfers between devices  51.3 us (34%)
  Pallas kernels  43.9 us (29%)
  starting transfers between devices  29.2 us (19%)
  local copies, waits for them, and re-layouts  12.9 us (9%)
  between operations  5.54 us (4%)
  other arithmetic  5.44 us (4%)
    ppermute x8, waiting for transfers between devices, from_behind(): return lax.ppermute(block, axis, route)  26.2 us
    ppermute x5, waiting for transfers between devices, partner(): return lax.ppermute(value, axis, pairs)  25.1 us
    ppermute x8, starting transfers between devices, from_behind(): return lax.ppermute(block, axis, route)  23.6 us
    pallas_call x2, Pallas kernels, back(): pl.pallas_call(functools.partial(back_kernel, piece * groups % LANES), gr...  23.5 us
    pallas_call x1, Pallas kernels, middle(): pl.pallas_call(middle_kernel, grid=(channels // BLOCK,), in_specs=[pl.Blo...  8.41 us
    pallas_call x2, Pallas kernels, gate_grad(): pl.pallas_call(gate_kernel, grid=(part // BLOCK,), in_specs=[pl.BlockSpec...  7.07 us
    ppermute x5, starting transfers between devices, partner(): return lax.ppermute(value, axis, pairs)  5.59 us
    pallas_call x1, Pallas kernels, input_grad(): pl.pallas_call(input_kernel, grid=(channels // BLOCK,), in_specs=[pl.Bloc...  4.95 us
  transfers between devices with their start and end apart: 13, of which 4 were waited for; matrix products, arithmetic and copies ran while one was open for 11% of the time, Pallas kernels for 22%

profile of v1, /device:TPU:0, one launch (start us, length us, event | category | flops | bytes accessed | tf_op | source)
XLA Modules:
  0.0 148.3 jit_solution(8548509289918737603)
XLA Ops:
  0.6 0.5 collective-permute-start
  1.8 1.3 fusion.5
  3.8 1.5 fusion.2
  5.2 4.4 %collective-permute-start.3 = (bf16[8,4096]{1,0:T(8,128)(2,1)}, bf16[8,4096]{1,0:T(8,128)(2,1)S(1)}, u32[]{:S(2)}, u32[]{:S(2)}) collective-permute-start(bf16[8,4096]{1,0:T(8,128)(2,1)} %fusion.2), channel_id=1, source_target_pairs={{0,2},{2,4},{4,6},{6,8},{8,10},{10,12},{12,14},{14,16},{16,18},{18... | collective-permute-start | bytes 196616 | tf_op jit(solution)/shard_map/ppermute | solution.py:26
  10.3 0.0 copy-start.2
  10.3 3.2 %dynamic-slice_bitcast_fusion = (bf16[128,4096]{1,0:T(8,128)(2,1)}, bf16[128,4096]{1,0:T(8,128)(2,1)}) fusion(bf16[1,2,128,4096]{3,2,1,0:T(8,128)(2,1)} %param.9, s32[]{:T(128)S(6)} %select_n.42), kind=kLoop, calls=%fused_computation.3 | loop fusion | bytes 4194308 | tf_op jit(solution)/shard_map/jit(dynamic_index_in_dim)/squeeze | solution.py:360
  13.5 4.6 %collective-permute-start.2 = (bf16[128,4096]{1,0:T(8,128)(2,1)}, bf16[128,4096]{1,0:T(8,128)(2,1)}, u32[]{:S(2)}, u32[]{:S(2)}) collective-permute-start(bf16[128,4096]{1,0:T(8,128)(2,1)} %get-tuple-element.33), channel_id=1, source_target_pairs={{0,2},{2,4},{4,6},{6,8},{8,10},{10,12},{12,14},{14,16},{16,18},{18... | collective-permute-start | bytes 3145736 | tf_op jit(solution)/shard_map/ppermute | solution.py:26
  18.8 0.0 copy-start.4
  18.8 0.0 copy-start.3
  18.8 0.0 collective-permute-done.incoming
  18.8 0.2 fusion.weighted
  19.1 1.0 fusion.4
  20.1 1.4 collective-permute-start.1
  21.5 1.5 %fusion.1 = bf16[8,4096]{1,0:T(8,128)(2,1)} fusion(bf16[1,2,128,4096]{3,2,1,0:T(8,128)(2,1)} %param.9, s32[]{:T(128)S(6)} %select_n.42, s32[]{:T(128)S(6)} %add.33, pred[]{:T(512)S(6)} %or.3), kind=kLoop, calls=%fused_computation.9 | loop fusion | flops 32768 | bytes 131081 | tf_op jit(solution)/shard_map/jit(_where)/select_n | solution.py:365
  23.0 4.3 %collective-permute-start.4 = (bf16[8,4096]{1,0:T(8,128)(2,1)}, bf16[8,4096]{1,0:T(8,128)(2,1)S(1)}, u32[]{:S(2)}, u32[]{:S(2)}) collective-permute-start(bf16[8,4096]{1,0:T(8,128)(2,1)} %fusion.1), channel_id=1, source_target_pairs={{0,4},{2,6},{4,8},{6,10},{8,12},{10,14},{12,16},{14,18},{16,20},{1... | collective-permute-start | bytes 196616 | tf_op jit(solution)/shard_map/ppermute | solution.py:26
  27.3 1.3 collective-permute-start.5
  28.6 0.1 slice.76
  28.7 0.8 slice.64
  29.6 1.3 broadcast_in_dim.27
  30.9 1.8 %reshape.39.taps.refs_5_ = f32[8,4096]{1,0:T(8,128)S(1)} reshape(f32[8,256,16]{2,1,0:T(8,128)} %broadcast_in_dim.27) | data formatting | bytes 262144 | tf_op jit(solution)/shard_map/reshape | solution.py:380
  32.7 0.7 fusion.6
  35.4 1.0 pad_maximum_fusion.hr
  36.4 0.1 pad_add_fusion.sc
  36.5 5.8 %collective-permute-done.4.rim_b = bf16[8,4096]{1,0:T(8,128)(2,1)S(1)} collective-permute-done((bf16[8,4096]{1,0:T(8,128)(2,1)}, bf16[8,4096]{1,0:T(8,128)(2,1)S(1)}, u32[]{:S(2)}, u32[]{:S(2)}) %collective-permute-start.4) | collective-permute-done | bytes 65568 | tf_op jit(solution)/shard_map/ppermute | solution.py:26
  42.3 20.3 %collective-permute-done.2.arrived = bf16[128,4096]{1,0:T(8,128)(2,1)} collective-permute-done((bf16[128,4096]{1,0:T(8,128)(2,1)}, bf16[128,4096]{1,0:T(8,128)(2,1)}, u32[]{:S(2)}, u32[]{:S(2)}) %collective-permute-start.2) | collective-permute-done | bytes 1048608 | tf_op jit(solution)/shard_map/ppermute | solution.py:26
  62.6 1.2 copy-done.1
  63.9 8.4 %shard_map.128 = (bf16[128,4096]{1,0:T(8,128)(2,1)S(1)}, bf16[128,4096]{1,0:T(8,128)(2,1)S(1)}, f32[128,4096]{1,0:T(8,128)S(1)}, f32[128,4096]{1,0:T(8,128)S(1)}) custom-call(s32[4]{0:T(128)S(1)} %pad_add_fusion.sc, bf16[128,4096]{1,0:T(8,128)(2,1)S(1)} %copy-done.1, bf16[128,4096]{1,0:T(8,128)(2,1)} %collective-permute-done.2.arrived, ...), custom_call_target="tpu_custom_call" | custom-call | flops 134217728 | bytes 9437184 | tf_op jit(solution)/shard_map/pallas_call | solution.py:101
  72.3 11.7 %shard_map.129 = (bf16[128,2048]{1,0:T(8,128)(2,1)S(1)}, bf16[128,2048]{1,0:T(8,128)(2,1)S(1)}, bf16[128,2048]{1,0:T(8,128)(2,1)S(1)}, f32[128,128]{1,0:T(8,128)S(1)}, f32[8,128]{1,0:T(8,128)S(1)}) custom-call(s32[4]{0:T(128)S(1)} %pad_add_fusion.sc, bf16[128,4096]{1,0:T(8,128)(2,1)S(1)} %fusion.weighted, bf16[128,2048]{1,0:T(8,128)(2,1)} %collective-permute-done.1.after, ...), custom_call_target="tpu_custom_call" | custom-call | flops 268435456 | bytes 5767168 | tf_op jit(solution)/shard_map/pallas_call | solution.py:201
  84.1 0.0 collective-permute-done.5.after
  84.1 11.8 %shard_map.130 = (bf16[128,2048]{1,0:T(8,128)(2,1)S(1)}, bf16[128,2048]{1,0:T(8,128)(2,1)S(1)}, bf16[128,2048]{1,0:T(8,128)(2,1)S(1)}, f32[128,128]{1,0:T(8,128)S(1)}, f32[8,128]{1,0:T(8,128)S(1)}) custom-call(s32[4]{0:T(128)S(1)} %pad_add_fusion.sc, bf16[128,4096]{1,0:T(8,128)(2,1)S(1)} %fusion.weighted, bf16[128,2048]{1,0:T(8,128)(2,1)} %collective-permute-done.5.after, ...), custom_call_target="tpu_custom_call" | custom-call | flops 268435456 | bytes 5767168 | tf_op jit(solution)/shard_map/pallas_call | solution.py:201
  95.9 2.5 %collective-permute-start.9 = (f32[272,128]{1,0:T(8,128)S(1)}, f32[272,128]{1,0:T(8,128)S(1)}, u32[]{:S(2)}, u32[]{:S(2)}) collective-permute-start(f32[272,128]{1,0:T(8,128)S(1)} %constant_dynamic-update-slice_fusion), channel_id=1, source_target_pairs={{0,16},{2,18},{4,20},{6,22},{8,24},{10,26},{12,28},{14,30},{16,0},... | collective-permute-start | bytes 417800 | tf_op jit(solution)/shard_map/ppermute | solution.py:31
  98.3 6.5 %collective-permute-done.9 = f32[272,128]{1,0:T(8,128)S(1)} collective-permute-done((f32[272,128]{1,0:T(8,128)S(1)}, f32[272,128]{1,0:T(8,128)S(1)}, u32[]{:S(2)}, u32[]{:S(2)}) %collective-permute-start.9) | collective-permute-done | bytes 139296 | tf_op jit(solution)/shard_map/ppermute | solution.py:31
  104.8 0.1 collective-permute-start.10
  104.9 0.1 fusion.3
  105.0 4.4 %collective-permute-start.8 = (bf16[128,2048]{1,0:T(8,128)(2,1)S(1)}, bf16[128,2048]{1,0:T(8,128)(2,1)S(1)}, u32[]{:S(2)}, u32[]{:S(2)}) collective-permute-start(bf16[128,2048]{1,0:T(8,128)(2,1)S(1)} %get-tuple-element.35), channel_id=1, source_target_pairs={{0,2},{2,4},{4,6},{6,8},{8,10},{10,12},{12,14},{14,16},{16,18},{18... | collective-permute-start | bytes 1572872 | tf_op jit(solution)/shard_map/ppermute | solution.py:26
  109.4 1.9 %collective-permute-start.7 = (bf16[128,2048]{1,0:T(8,128)(2,1)S(1)}, bf16[128,2048]{1,0:T(8,128)(2,1)S(1)}, u32[]{:S(2)}, u32[]{:S(2)}) collective-permute-start(bf16[128,2048]{1,0:T(8,128)(2,1)S(1)} %get-tuple-element.36), channel_id=1, source_target_pairs={{0,2},{2,4},{4,6},{6,8},{8,10},{10,12},{12,14},{14,16},{16,18},{18... | collective-permute-start | bytes 1572872 | tf_op jit(solution)/shard_map/ppermute | solution.py:26
  111.4 0.0 collective-permute-done.10
  111.4 2.5 %collective-permute-start.11 = (f32[272,128]{1,0:T(8,128)S(1)}, f32[272,128]{1,0:T(8,128)S(1)}, u32[]{:S(2)}, u32[]{:S(2)}) collective-permute-start(f32[272,128]{1,0:T(8,128)S(1)} %add.27), channel_id=1, source_target_pairs={{0,4},{2,6},{4,0},{6,2},{8,12},{10,14},{12,8},{14,10},{16,20},{18,... | collective-permute-start | bytes 417800 | tf_op jit(solution)/shard_map/ppermute | solution.py:31
  113.9 1.3 collective-permute-start.6
  115.2 18.6 %collective-permute-done.11 = f32[272,128]{1,0:T(8,128)S(1)} collective-permute-done((f32[272,128]{1,0:T(8,128)S(1)}, f32[272,128]{1,0:T(8,128)S(1)}, u32[]{:S(2)}, u32[]{:S(2)}) %collective-permute-start.11) | collective-permute-done | bytes 139296 | tf_op jit(solution)/shard_map/ppermute | solution.py:31
  133.8 0.1 collective-permute-start.12
  133.9 1.1 maximum_bitcast_fusion
  135.0 0.0 collective-permute-done.8.prior
  135.0 3.5 %shard_map.132.rest_0_ = bf16[128,4096]{1,0:T(8,128)(2,1)} custom-call(s32[4]{0:T(128)S(1)} %pad_add_fusion.sc, bf16[128,2048]{1,0:T(8,128)(2,1)S(1)} %collective-permute-done.8.prior, f32[128,4096]{1,0:T(8,128)S(1)} %get-tuple-element.28.own, bf16[128,4096]{1,0:T(8,128)(2,1)S(1)} %collective-permute-done.incoming, f32[256,128]{1,0:T(8,128)S(1)} %pad_maximum_fusion.hr), custom_call_target="tpu_custom_call" | custom-call | flops 67108864 | bytes 2621440 | tf_op jit(solution)/shard_map/pallas_call | solution.py:326
  138.5 3.5 %shard_map.133 = bf16[128,4096]{1,0:T(8,128)(2,1)} custom-call(s32[4]{0:T(128)S(1)} %pad_add_fusion.sc, bf16[128,2048]{1,0:T(8,128)(2,1)S(1)} %collective-permute-done.7.prior, f32[128,4096]{1,0:T(8,128)S(1)} %get-tuple-element.28.own, bf16[128,4096]{1,0:T(8,128)(2,1)S(1)} %collective-permute-done.incoming, ...), custom_call_target="tpu_custom_call", output_to_operand_aliasing={{}: (5, {})} | custom-call | flops 67108864 | bytes 2621440 | tf_op jit(solution)/shard_map/pallas_call | solution.py:326
  142.0 4.9 %shard_map.131 = bf16[128,4096]{1,0:T(8,128)(2,1)} custom-call(s32[4]{0:T(128)S(1)} %pad_add_fusion.sc, bf16[128,2048]{1,0:T(8,128)(2,1)S(1)} %get-tuple-element.22.refs_0_, bf16[128,2048]{1,0:T(8,128)(2,1)S(1)} %get-tuple-element.23.refs_1_, bf16[128,2048]{1,0:T(8,128)(2,1)S(1)} %get-tuple-element.24.refs_2_, ...), custom_call_target="tpu_custom_call" | custom-call | flops 7340032 | bytes 3145728 | tf_op jit(solution)/shard_map/pallas_call | solution.py:286
  147.0 0.7 slice_bitcast_fusion.1
  147.7 0.6 broadcast_in_dim.31
  (28 shorter events, 0.2 us)
Async XLA Ops:
  0.6 18.1 %collective-permute-start = (bf16[128,4096]{1,0:T(8,128)(2,1)}, bf16[128,4096]{1,0:T(8,128)(2,1)S(1)}, u32[]{:S(2)}, u32[]{:S(2)}) collective-permute-start(bf16[128,4096]{1,0:T(8,128)(2,1)} %bitcast.58), channel_id=1, source_target_pairs={{0,1},{1,0},{2,3},{3,2},{4,5},{5,4},{6,7},{7,6},{8,9},{9,8},{10,11... | collective-permute-start | bytes 3145736 | tf_op jit(solution)/shard_map/ppermute | solution.py:31
  5.2 31.2 %collective-permute-start.3 = (bf16[8,4096]{1,0:T(8,128)(2,1)}, bf16[8,4096]{1,0:T(8,128)(2,1)S(1)}, u32[]{:S(2)}, u32[]{:S(2)}) collective-permute-start(bf16[8,4096]{1,0:T(8,128)(2,1)} %fusion.2), channel_id=1, source_target_pairs={{0,2},{2,4},{4,6},{6,8},{8,10},{10,12},{12,14},{14,16},{16,18},{18... | collective-permute-start | bytes 196616 | tf_op jit(solution)/shard_map/ppermute | solution.py:26
  10.3 8.5 %copy-start.2 = (bf16[1,128,4096]{2,1,0:T(8,128)(2,1)S(1)}, bf16[1,128,4096]{2,1,0:T(8,128)(2,1)}, u32[]{:S(2)}) copy-start(bf16[1,128,4096]{2,1,0:T(8,128)(2,1)} %param.14) | copy-start | bytes 3145732
  13.5 49.2 %collective-permute-start.2 = (bf16[128,4096]{1,0:T(8,128)(2,1)}, bf16[128,4096]{1,0:T(8,128)(2,1)}, u32[]{:S(2)}, u32[]{:S(2)}) collective-permute-start(bf16[128,4096]{1,0:T(8,128)(2,1)} %get-tuple-element.33), channel_id=1, source_target_pairs={{0,2},{2,4},{4,6},{6,8},{8,10},{10,12},{12,14},{14,16},{16,18},{18... | collective-permute-start | bytes 3145736 | tf_op jit(solution)/shard_map/ppermute | solution.py:26
  18.8 8.5 %copy-start.4 = (f32[1,256,7]{1,0,2:T(1,128)S(1)}, f32[1,256,7]{1,0,2:T(1,128)}, u32[]{:S(2)}) copy-start(f32[1,256,7]{1,0,2:T(1,128)} %param.16) | copy-start | bytes 21508
  18.8 9.8 %copy-start.3 = (f32[1,256,128]{2,1,0:T(8,128)S(1)}, f32[1,256,128]{2,1,0:T(8,128)}, u32[]{:S(2)}) copy-start(f32[1,256,128]{2,1,0:T(8,128)} %param.17) | copy-start | bytes 393220
  20.1 12.6 %copy-start.5 = (s32[16]{0:T(128)S(1)}, s32[16]{0:T(128)}, u32[]{:S(2)}) copy-start(s32[16]{0:T(128)} %param.12) | copy-start | bytes 196
  20.1 42.6 %copy-start = (bf16[1,128,4096]{2,1,0:T(8,128)(2,1)S(1)}, bf16[1,128,4096]{2,1,0:T(8,128)(2,1)}, u32[]{:S(2)}) copy-start(bf16[1,128,4096]{2,1,0:T(8,128)(2,1)} %param.13) | copy-start | bytes 3145732
  20.1 52.2 %collective-permute-start.1 = (bf16[128,2048]{1,0:T(8,128)(2,1)}, bf16[128,2048]{1,0:T(8,128)(2,1)}, u32[]{:S(2)}, u32[]{:S(2)}) collective-permute-start(bf16[128,2048]{1,0:T(8,128)(2,1)} %get-tuple-element.38), channel_id=1, source_target_pairs={{2,0},{4,2},{6,4},{8,6},{10,8},{12,10},{14,12},{16,14},{18,16},{20... | collective-permute-start | bytes 1572872 | tf_op jit(solution)/shard_map/ppermute | solution.py:26
  23.0 19.3 %collective-permute-start.4 = (bf16[8,4096]{1,0:T(8,128)(2,1)}, bf16[8,4096]{1,0:T(8,128)(2,1)S(1)}, u32[]{:S(2)}, u32[]{:S(2)}) collective-permute-start(bf16[8,4096]{1,0:T(8,128)(2,1)} %fusion.1), channel_id=1, source_target_pairs={{0,4},{2,6},{4,8},{6,10},{8,12},{10,14},{12,16},{14,18},{16,20},{1... | collective-permute-start | bytes 196616 | tf_op jit(solution)/shard_map/ppermute | solution.py:26
  27.3 56.8 %collective-permute-start.5 = (bf16[128,2048]{1,0:T(8,128)(2,1)}, bf16[128,2048]{1,0:T(8,128)(2,1)}, u32[]{:S(2)}, u32[]{:S(2)}) collective-permute-start(bf16[128,2048]{1,0:T(8,128)(2,1)} %get-tuple-element.37), channel_id=1, source_target_pairs={{2,0},{4,2},{6,4},{8,6},{10,8},{12,10},{14,12},{16,14},{18,16},{20... | collective-permute-start | bytes 1572872 | tf_op jit(solution)/shard_map/ppermute | solution.py:26
  62.6 1.2 copy-start.1
  95.9 8.9 %collective-permute-start.9 = (f32[272,128]{1,0:T(8,128)S(1)}, f32[272,128]{1,0:T(8,128)S(1)}, u32[]{:S(2)}, u32[]{:S(2)}) collective-permute-start(f32[272,128]{1,0:T(8,128)S(1)} %constant_dynamic-update-slice_fusion), channel_id=1, source_target_pairs={{0,16},{2,18},{4,20},{6,22},{8,24},{10,26},{12,28},{14,30},{16,0},... | collective-permute-start | bytes 417800 | tf_op jit(solution)/shard_map/ppermute | solution.py:31
  104.8 6.5 %collective-permute-start.10 = (f32[272,128]{1,0:T(8,128)S(1)}, f32[272,128]{1,0:T(8,128)S(1)}, u32[]{:S(2)}, u32[]{:S(2)}) collective-permute-start(f32[272,128]{1,0:T(8,128)S(1)} %add.26), channel_id=1, source_target_pairs={{0,8},{2,10},{4,12},{6,14},{8,0},{10,2},{12,4},{14,6},{16,24},{18,... | collective-permute-start | bytes 417800 | tf_op jit(solution)/shard_map/ppermute | solution.py:31
  105.0 30.0 %collective-permute-start.8 = (bf16[128,2048]{1,0:T(8,128)(2,1)S(1)}, bf16[128,2048]{1,0:T(8,128)(2,1)S(1)}, u32[]{:S(2)}, u32[]{:S(2)}) collective-permute-start(bf16[128,2048]{1,0:T(8,128)(2,1)S(1)} %get-tuple-element.35), channel_id=1, source_target_pairs={{0,2},{2,4},{4,6},{6,8},{8,10},{10,12},{12,14},{14,16},{16,18},{18... | collective-permute-start | bytes 1572872 | tf_op jit(solution)/shard_map/ppermute | solution.py:26
  109.4 29.1 %collective-permute-start.7 = (bf16[128,2048]{1,0:T(8,128)(2,1)S(1)}, bf16[128,2048]{1,0:T(8,128)(2,1)S(1)}, u32[]{:S(2)}, u32[]{:S(2)}) collective-permute-start(bf16[128,2048]{1,0:T(8,128)(2,1)S(1)} %get-tuple-element.36), channel_id=1, source_target_pairs={{0,2},{2,4},{4,6},{6,8},{8,10},{10,12},{12,14},{14,16},{16,18},{18... | collective-permute-start | bytes 1572872 | tf_op jit(solution)/shard_map/ppermute | solution.py:26
  111.4 22.4 %collective-permute-start.11 = (f32[272,128]{1,0:T(8,128)S(1)}, f32[272,128]{1,0:T(8,128)S(1)}, u32[]{:S(2)}, u32[]{:S(2)}) collective-permute-start(f32[272,128]{1,0:T(8,128)S(1)} %add.27), channel_id=1, source_target_pairs={{0,4},{2,6},{4,0},{6,2},{8,12},{10,14},{12,8},{14,10},{16,20},{18,... | collective-permute-start | bytes 417800 | tf_op jit(solution)/shard_map/ppermute | solution.py:31
  113.9 28.1 %collective-permute-start.6 = (bf16[8,4096]{1,0:T(8,128)(2,1)S(1)}, bf16[8,4096]{1,0:T(8,128)(2,1)S(1)}, u32[]{:S(2)}, u32[]{:S(2)}) collective-permute-start(bf16[8,4096]{1,0:T(8,128)(2,1)S(1)} %pad_maximum_fusion.1), channel_id=1, source_target_pairs={{2,0},{4,2},{6,4},{8,6},{10,8},{12,10},{14,12},{16,14},{18,16},{20... | collective-permute-start | bytes 196616 | tf_op jit(solution)/shard_map/ppermute | solution.py:26
  133.8 13.2 %collective-permute-start.12 = (f32[272,128]{1,0:T(8,128)S(1)}, f32[272,128]{1,0:T(8,128)S(1)}, u32[]{:S(2)}, u32[]{:S(2)}) collective-permute-start(f32[272,128]{1,0:T(8,128)S(1)} %add.28), channel_id=1, source_target_pairs={{0,2},{2,0},{4,6},{6,4},{8,10},{10,8},{12,14},{14,12},{16,18},{18,... | collective-permute-start | bytes 417800 | tf_op jit(solution)/shard_map/ppermute | solution.py:31

commit v2 on v1

v2 whole, which is shorter than its diff:
```python
import functools
import math

import jax
import jax.numpy as jnp
from jax import lax
from jax.experimental import pallas as pl
from jax.experimental.pallas import tpu as pltpu
from jax.sharding import PartitionSpec as P

GROUP = 16
LANES = 128
PER_BLOCK = LANES // GROUP
RIM = 8
FAR = 1 << 20
PIECES = 2
BLOCK = 2048

F32 = jnp.float32
BF16 = jnp.bfloat16


def from_behind(block, axis, distance):
    devices = range(lax.axis_size(axis))
    route = [(i - distance, i) for i in devices if i - distance in devices]
    return lax.ppermute(block, axis, route)


def partner(value, axis, mask):
    pairs = [(source, source ^ mask) for source in range(lax.axis_size(axis))]
    return lax.ppermute(value, axis, pairs)


def exchange_order(count):
    masks = [1 << bit for bit in range(count.bit_length() - 1)]
    return masks[1:] + masks[:1]


def grid_of(rows, which):
    return lax.broadcasted_iota(jnp.int32, (rows, rows), which)


def same_tile(out_row, in_row, bound):
    return (out_row >= in_row) & ((out_row < bound) | (in_row >= bound))


def tile_before(out_row, in_row, bound, earlier, rows):
    return (out_row < in_row) & (out_row < bound) & ((earlier >= rows) | (in_row >= earlier))


def as_mask(flags, dtype):
    return jnp.where(flags, 1.0, 0.0).astype(F32).astype(dtype)


def room_of(row, bound, earlier, rows):
    before = jnp.where(earlier < rows, row + (rows - earlier), FAR)
    return jnp.where(row >= bound, row - bound, before)


def rolled(line, rows):
    return pltpu.roll(jnp.broadcast_to(line, (rows, rows)), 0, 1, stride=1, stride_axis=0)


def lanes(start):
    return pl.ds(start, LANES)


def bounds_near(bounds, rows):
    count = bounds.shape[0]
    shard = lax.axis_index("ctx")
    near = []
    for tile in (shard - 1, shard, shard + 1):
        bound = bounds[jnp.clip(tile, 0, count - 1)]
        near.append(jnp.where((tile >= 0) & (tile < count), bound, rows))
    return near


def holds_own(counts, destinations):
    return (counts[0] >= 1) & (destinations[0] == lax.axis_index("ctx"))


SCALARS = pl.BlockSpec(memory_space=pltpu.SMEM)
FREE = pl.CostEstimate(flops=1, bytes_accessed=1, transcendentals=0)
ROOM = pltpu.CompilerParams(vmem_limit_bytes=40 << 20)


def pick_kernel(counts, destinations, slot, first, *outs):
    *pieces, sent_tail = outs
    rows = slot.shape[0]
    shard = lax.axis_index("ctx")
    sends = ((counts[0] >= 1) & (destinations[0] == shard + 1)) | ((counts[0] >= 2) & (destinations[1] == shard + 1))
    picked = slot[...]
    own = jnp.where(holds_own(counts, destinations), first[...].astype(F32), 0.0)[-RIM:].astype(BF16)
    for number, piece in enumerate(pieces):

        @pl.when(pl.program_id(0) == number)
        def _(piece=piece):
            piece[:rows] = picked
            piece[rows:] = own

    sent_tail[...] = jnp.where(sends, picked[-2 * RIM :].astype(F32), 0.0)[-RIM:].astype(BF16)


def pick_outgoing(counts, destinations, loaded):
    rows, channels = loaded.shape[2:]
    width = channels // PIECES
    shape = lambda height, size: jax.ShapeDtypeStruct((height, size), loaded.dtype)
    return pl.pallas_call(
        pick_kernel,
        grid_spec=pltpu.PrefetchScalarGridSpec(
            num_scalar_prefetch=2,
            grid=(PIECES,),
            in_specs=[
                pl.BlockSpec((None, None, rows, width), lambda i, held, _: (0, jnp.where(held[0] == 2, 1, 0), 0, i)),
                pl.BlockSpec((None, None, 2 * RIM, width), lambda i, *_: (0, 0, rows // (2 * RIM) - 1, i)),
            ],
            out_specs=[pl.BlockSpec((rows + RIM, width), lambda i, *_: (0, 0))] * PIECES
            + [pl.BlockSpec((RIM, width), lambda i, *_: (0, i))],
        ),
        out_shape=[shape(rows + RIM, width)] * PIECES + [shape(RIM, channels)],
        cost_estimate=FREE,
    )(counts, destinations, loaded, loaded)


def taps_kernel(mr, se, low, mirrored, spread):
    groups, count = mr.shape
    rounded = mr[...].astype(BF16)
    low[...] = rounded.astype(F32)
    mirror = as_mask(lax.rem(grid_of(count, 0) + grid_of(count, 1), count) == 0, BF16)
    mirrored[...] = jnp.dot(rounded, mirror, preferred_element_type=F32)
    taps = se.shape[1]
    group = lax.broadcasted_iota(jnp.int32, (PER_BLOCK, LANES), 0)
    owner = lax.broadcasted_iota(jnp.int32, (PER_BLOCK, LANES), 1) // GROUP
    widen = as_mask(group == owner, F32)
    for block in range(groups // PER_BLOCK):
        part = se[block * PER_BLOCK : (block + 1) * PER_BLOCK]
        for tap in range(taps):
            line = jnp.sum(part[:, tap : tap + 1] * widen, axis=0, keepdims=True)
            spread[tap : tap + 1, lanes(block * LANES)] = line
    spread[taps:] = jnp.zeros((spread.shape[0] - taps, spread.shape[1]), F32)


def taps_forms(mr_taps, se_taps):
    groups, count = mr_taps.shape
    return pl.pallas_call(
        taps_kernel,
        out_shape=[
            jax.ShapeDtypeStruct((groups, count), F32),
            jax.ShapeDtypeStruct((groups, count), F32),
            jax.ShapeDtypeStruct((RIM, groups * GROUP), F32),
        ],
        cost_estimate=FREE,
    )(mr_taps, se_taps)


def filtered(matrix_of, values, rows):
    lane_group = lax.broadcasted_iota(jnp.int32, (rows, LANES), 1) // GROUP
    total = jnp.zeros((rows, LANES), F32)
    for group in range(PER_BLOCK):
        product = jnp.dot(matrix_of(group), values, preferred_element_type=F32)
        total = jnp.where(lane_group == group, product, total)
    return total


def own_back_kernel(bounds, weighted, incoming, low, out, mask):
    rows = weighted.shape[0]
    _, bound, _ = bounds_near(bounds, rows)

    @pl.when(pl.program_id(0) == 0)
    def _():
        mask[...] = as_mask(same_tile(grid_of(rows, 1), grid_of(rows, 0), bound), BF16)

    for block in range(weighted.shape[1] // LANES):
        at = lanes(block * LANES)

        def matrix_of(group):
            line = block * PER_BLOCK + group
            return rolled(low[line : line + 1], rows).astype(BF16) * mask[...]

        out[:, at] = incoming[:, at].astype(F32) + filtered(matrix_of, weighted[:, at], rows)


def own_back(bounds, weighted, incoming, low):
    rows, channels = weighted.shape
    wide = lambda height: pl.BlockSpec((height, BLOCK), lambda i: (0, i))
    return pl.pallas_call(
        own_back_kernel,
        grid=(channels // BLOCK,),
        in_specs=[SCALARS, wide(rows), wide(rows), pl.BlockSpec((BLOCK // GROUP, rows), lambda i: (i, 0))],
        out_specs=wide(rows),
        out_shape=jax.ShapeDtypeStruct((rows, channels), F32),
        scratch_shapes=[pltpu.VMEM((rows, rows), BF16)],
        compiler_params=ROOM,
        cost_estimate=FREE,
    )(bounds, weighted, incoming, low)


def next_back_kernel(bounds, after, base, gate, low, mid_grad, wse, mask):
    rows = after.shape[0]
    _, bound, later = bounds_near(bounds, rows)

    @pl.when(pl.program_id(0) == 0)
    def _():
        mask[...] = as_mask(tile_before(grid_of(rows, 1), grid_of(rows, 0), later, bound, rows), BF16)

    for block in range(after.shape[1] // LANES):
        at = lanes(block * LANES)

        def matrix_of(group):
            line = block * PER_BLOCK + group
            return rolled(low[line : line + 1], rows).astype(BF16) * mask[...]

        grad = (base[:, at] + filtered(matrix_of, after[:, at], rows)).astype(BF16)
        mid_grad[:, at] = grad
        wse[:, at] = (gate[:, at].astype(F32) * grad.astype(F32)).astype(BF16)


def next_back(bounds, after, base, gate, low):
    rows, channels = after.shape
    wide = lambda height: pl.BlockSpec((height, BLOCK), lambda i: (0, i))
    return pl.pallas_call(
        next_back_kernel,
        grid=(channels // BLOCK,),
        in_specs=[
            SCALARS,
            wide(rows),
            wide(rows),
            wide(rows),
            pl.BlockSpec((BLOCK // GROUP, rows), lambda i: (i, 0)),
        ],
        out_specs=[wide(rows)] * 2,
        out_shape=[jax.ShapeDtypeStruct((rows, channels), BF16)] * 2,
        scratch_shapes=[pltpu.VMEM((rows, rows), BF16)],
        compiler_params=ROOM,
        cost_estimate=FREE,
    )(bounds, after, base, gate, low)


def middle_kernel(shift, bounds, counts, destinations, slot, arrived, rim, gate, taps, grad, wse, *rest):
    mid_out, gate_grad, se_out, ext, room, spread = rest[-6:]
    rows = slot.shape[0]
    step = pl.program_id(0)
    earlier, bound, _ = bounds_near(bounds, rows)
    own_here = holds_own(counts, destinations)

    @pl.when(step == 0)
    def _():
        row = lax.broadcasted_iota(jnp.int32, (rows, LANES), 0)
        room[...] = room_of(row, bound, earlier, rows)
        se_out[...] = jnp.zeros_like(se_out)
        spread[...] = as_mask(grid_of(LANES, 0) // GROUP == grid_of(LANES, 1), BF16)

    blocks = slot.shape[1] // LANES
    thirds = []
    for block in range(blocks):
        at = lanes(block * LANES)
        x = jnp.where(own_here, slot[:, at].astype(F32), arrived[:rows, at].astype(F32))
        ext[block, :RIM] = arrived[rows:, at].astype(F32) + rim[:, at].astype(F32)
        ext[block, RIM:] = x
        mix = jnp.zeros((rows, LANES), F32)
        wide_wse = wse[:, at].astype(F32)
        sums = []
        for lag in range(taps.shape[0] - 1):
            kept = jnp.where(room[...] >= lag, ext[block, RIM - lag : RIM - lag + rows], 0.0)
            mix = mix + taps[lag : lag + 1, at] * kept
            sums.append(jnp.sum(wide_wse * kept, axis=0, keepdims=True))
        sums.append(jnp.zeros((1, LANES), F32))
        mid_out[:, at] = (x + gate[:, at].astype(F32) * mix).astype(BF16)
        gate_grad[:, at] = (grad[:, at].astype(F32) * mix).astype(BF16)
        left = jnp.concatenate(sums, axis=0)
        for _ in range(3):
            term = left.astype(BF16).astype(F32)
            thirds.append(term)
            left = left - term
    parts = jnp.dot(jnp.concatenate(thirds, axis=0).astype(BF16), spread[...], preferred_element_type=F32)
    gathered = jnp.zeros((RIM, LANES), F32)
    for block in range(blocks):
        first = 3 * RIM * block
        part = parts[first : first + RIM] + parts[first + RIM : first + 2 * RIM] + parts[first + 2 * RIM : first + 3 * RIM]
        gathered = gathered + (pltpu.roll(part, block * PER_BLOCK, 1) if block else part)
    place = lax.rem(shift + step * blocks * PER_BLOCK, LANES)
    se_out[...] += pltpu.roll(gathered, place, 1)


def middle(piece, bounds, counts, destinations, loaded, arrived, rim, gate, taps, grad, wse, held):
    rows, channels = gate.shape
    part = channels // PIECES
    groups = channels // GROUP
    first = piece * part // BLOCK
    full = lambda height: pl.BlockSpec((height, BLOCK), lambda i: (0, first + i))
    own = lambda height: pl.BlockSpec((height, BLOCK), lambda i: (0, i))
    return pl.pallas_call(
        functools.partial(middle_kernel, (piece * groups // PIECES) % LANES),
        grid=(part // BLOCK,),
        in_specs=[
            SCALARS,
            SCALARS,
            SCALARS,
            pl.BlockSpec((None, None, rows, BLOCK), lambda i: (0, 0, 0, first + i)),
            own(rows + RIM),
            full(RIM),
            full(rows),
            full(taps.shape[0]),
            full(rows),
            full(rows),
        ]
        + [pl.BlockSpec(memory_space=pl.ANY)] * len(held),
        out_specs=[own(rows), full(rows), pl.BlockSpec((RIM, LANES), lambda i: (0, 0))],
        out_shape=[
            jax.ShapeDtypeStruct((rows, part), BF16),
            jax.ShapeDtypeStruct((rows, channels), BF16),
            jax.ShapeDtypeStruct((RIM, LANES), F32),
        ],
        scratch_shapes=[
            pltpu.VMEM((BLOCK // LANES, rows + RIM, LANES), F32),
            pltpu.VMEM((rows, LANES), jnp.int32),
            pltpu.VMEM((LANES, LANES), BF16),
        ],
        input_output_aliases={10: 1} if held else {},
        compiler_params=ROOM,
        cost_estimate=FREE,
    )(bounds, counts, destinations, loaded, arrived, rim, gate, taps, grad, wse, *held)


def lag_kernel(bounds, mid, weighted, after, *rest):
    out, lag_own, lag_next, flip, flipped = rest[-5:]
    rows = mid.shape[0]
    _, bound, later = bounds_near(bounds, rows)

    @pl.when(pl.program_id(0) == 0)
    def _():
        target = grid_of(rows, 1)
        mirrored = rows - 1 - grid_of(rows, 0)
        lag_own[...] = as_mask(same_tile(target, mirrored, bound), F32)
        lag_next[...] = as_mask(tile_before(target, mirrored, later, bound, rows), F32)
        flip[...] = as_mask(mirrored == target, BF16)

    one_row = lax.broadcasted_iota(jnp.int32, (1, LANES), 1) // GROUP
    for block in range(mid.shape[1] // LANES):
        flipped[block] = jnp.dot(flip[...], mid[:, lanes(block * LANES)], preferred_element_type=F32).astype(BF16)
    for block in range(mid.shape[1] // LANES):
        at = lanes(block * LANES)
        pair = jnp.concatenate([weighted[:, at], after[:, at]], axis=0).T
        mirrored_mid = flipped[block]
        lags = []
        for group in range(PER_BLOCK):
            chosen = mirrored_mid * as_mask(one_row == group, BF16)
            products = jnp.dot(chosen, pair, preferred_element_type=F32)
            kept = products[:, :rows] * lag_own[...] + products[:, rows:] * lag_next[...]
            kept = pltpu.roll(kept, 1, 1, stride=1, stride_axis=0)
            lags.append(jnp.sum(kept, axis=0, keepdims=True))
        out[block * PER_BLOCK : (block + 1) * PER_BLOCK] = jnp.concatenate(lags, axis=0)


def lag_grads(piece, bounds, mid, weighted, after, held):
    rows, channels = weighted.shape
    part = channels // PIECES
    first = piece * part // BLOCK
    full = lambda height: pl.BlockSpec((height, BLOCK), lambda i: (0, first + i))
    square = lambda dtype: pltpu.VMEM((rows, rows), dtype)
    return pl.pallas_call(
        lag_kernel,
        grid=(part // BLOCK,),
        in_specs=[SCALARS, pl.BlockSpec((rows, BLOCK), lambda i: (0, i)), full(rows), full(rows)]
        + [pl.BlockSpec(memory_space=pl.ANY)] * len(held),
        out_specs=pl.BlockSpec((BLOCK // GROUP, rows), lambda i: (first + i, 0)),
        out_shape=jax.ShapeDtypeStruct((channels // GROUP, rows), F32),
        scratch_shapes=[square(F32), square(F32), square(BF16), pltpu.VMEM((BLOCK // LANES, rows, LANES), BF16)],
        input_output_aliases={4: 0} if held else {},
        compiler_params=ROOM,
        cost_estimate=FREE,
    )(bounds, mid, weighted, after, *held)


def input_kernel(bounds, grad, wse, taps, out, ext, room):
    rows = out.shape[0]
    earlier, bound, _ = bounds_near(bounds, rows)

    @pl.when(pl.program_id(0) == 0)
    def _():
        row = lax.broadcasted_iota(jnp.int32, (rows, LANES), 0)
        room[:rows] = room_of(row, bound, earlier, rows)
        room[rows:] = jnp.zeros((RIM, LANES), jnp.int32)

    for block in range(out.shape[1] // LANES):
        at = lanes(block * LANES)
        ext[block, :rows] = wse[:, at].astype(F32)
        ext[block, rows:] = jnp.zeros((RIM, LANES), F32)
        total = grad[:, at].astype(F32)
        for lag in range(taps.shape[0] - 1):
            shifted = ext[block, lag : lag + rows]
            total = total + jnp.where(room[lag : lag + rows] >= lag, taps[lag : lag + 1, at] * shifted, 0.0)
        out[:, at] = total.astype(BF16)


def input_grad(bounds, grad, wse, taps):
    rows, channels = grad.shape
    wide = lambda height: pl.BlockSpec((height, BLOCK), lambda i: (0, i))
    return pl.pallas_call(
        input_kernel,
        grid=(channels // BLOCK,),
        in_specs=[SCALARS, wide(rows), wide(rows), wide(taps.shape[0])],
        out_specs=wide(rows),
        out_shape=jax.ShapeDtypeStruct((rows, channels), BF16),
        scratch_shapes=[
            pltpu.VMEM((BLOCK // LANES, rows + RIM, LANES), F32),
            pltpu.VMEM((rows + RIM, LANES), jnp.int32),
        ],
        compiler_params=ROOM,
        cost_estimate=FREE,
    )(bounds, grad, wse, taps)


def rim_kernel(rows, bounds, grad, wse, rim, taps, held, out, ext):
    del held
    some = out.shape[0]
    earlier, bound, later = bounds_near(bounds, rows)
    row = lax.broadcasted_iota(jnp.int32, (some, out.shape[1]), 0) + (rows - some)
    rim_row = lax.broadcasted_iota(jnp.int32, (RIM, out.shape[1]), 0)
    ext[0, :some] = wse[...].astype(F32)
    ext[0, some:] = rim[...].astype(F32)
    ext[1, :some] = room_of(row, bound, earlier, rows).astype(F32)
    ext[1, some:] = room_of(rim_row, later, bound, rows).astype(F32)
    total = grad[...].astype(F32)
    for lag in range(taps.shape[0] - 1):
        shifted = ext[0, lag : lag + some]
        total = total + jnp.where(ext[1, lag : lag + some] >= lag, taps[lag : lag + 1] * shifted, 0.0)
    out[...] = total.astype(BF16)


def rim_grad(bounds, grad, wse, rim, taps, held):
    rows, channels = grad.shape
    some, width = 2 * RIM, channels // 2
    last = pl.BlockSpec((some, width), lambda i: (rows // some - 1, i))
    wide = lambda height: pl.BlockSpec((height, width), lambda i: (0, i))
    return pl.pallas_call(
        functools.partial(rim_kernel, rows),
        grid=(channels // width,),
        in_specs=[SCALARS, last, last, wide(RIM), wide(taps.shape[0]), pl.BlockSpec(memory_space=pl.ANY)],
        out_specs=last,
        out_shape=jax.ShapeDtypeStruct((rows, channels), BF16),
        scratch_shapes=[pltpu.VMEM((2, some + RIM, width), F32)],
        input_output_aliases={5: 0},
        compiler_params=ROOM,
        cost_estimate=FREE,
    )(bounds, grad, wse, rim, taps, held)


def gate_kernel(bounds, prior, mid, incoming, mirrored, *rest):
    out, mask_own, mask_prior = rest[-3:]
    rows = prior.shape[0]
    earlier, bound, _ = bounds_near(bounds, rows)

    @pl.when(pl.program_id(0) == 0)
    def _():
        mask_own[...] = as_mask(same_tile(grid_of(rows, 0), grid_of(rows, 1), bound), BF16)
        mask_prior[...] = as_mask(tile_before(grid_of(rows, 0), grid_of(rows, 1), bound, earlier, rows), BF16)

    for block in range(prior.shape[1] // LANES):
        at = lanes(block * LANES)

        def matrix_of(group):
            line = block * PER_BLOCK + group
            circle = rolled(mirrored[line : line + 1], rows).astype(BF16)
            return jnp.concatenate([circle * mask_own[...], circle * mask_prior[...]], axis=1)

        pair = jnp.concatenate([mid[:, at], prior[:, at]], axis=0)
        out[:, at] = (incoming[:, at].astype(F32) * filtered(matrix_of, pair, rows)).astype(BF16)


def gate_grad(piece, bounds, prior, mid, incoming, mirrored, held):
    rows, channels = incoming.shape
    part = channels // PIECES
    first = piece * part // BLOCK
    full = lambda: pl.BlockSpec((rows, BLOCK), lambda i: (0, first + i))
    own = lambda: pl.BlockSpec((rows, BLOCK), lambda i: (0, i))
    return pl.pallas_call(
        gate_kernel,
        grid=(part // BLOCK,),
        in_specs=[SCALARS, own(), own(), full(), pl.BlockSpec((BLOCK // GROUP, rows), lambda i: (first + i, 0))]
        + [pl.BlockSpec(memory_space=pl.ANY)] * len(held),
        out_specs=full(),
        out_shape=jax.ShapeDtypeStruct((rows, channels), BF16),
        scratch_shapes=[pltpu.VMEM((rows, rows), BF16)] * 2,
        input_output_aliases={5: 0} if held else {},
        compiler_params=ROOM,
        cost_estimate=FREE,
    )(bounds, prior, mid, incoming, mirrored, *held)


def body(loaded, counts, destinations, bounds, se_gate, mr_gate, phase_grads, se_taps, mr_taps):
    ctx_count = lax.axis_size("ctx")
    rows, channels = loaded.shape[2:]
    group_count = channels // GROUP
    gate_se = se_gate[0]

    incoming = partner(phase_grads[0], "pipe", 1)
    weighted = (mr_gate[0].astype(F32) * incoming.astype(F32)).astype(BF16)
    after = from_behind(weighted, "ctx", -1)
    low, mirrored, taps_se = taps_forms(mr_taps[0], se_taps[0])
    base = own_back(bounds, weighted, incoming, low)

    *outgoing, sent_tail = pick_outgoing(counts, destinations, loaded)
    rim = from_behind(sent_tail, "ctx", 2)
    after, rim, base, low, mirrored, taps_se, *outgoing = lax.optimization_barrier(
        (after, rim, base, low, mirrored, taps_se, *outgoing)
    )
    arrived = [from_behind(piece, "ctx", 1) for piece in outgoing]

    mid_grad, wse = next_back(bounds, after, base, gate_se, low)
    rim_next = from_behind(wse[:RIM], "ctx", -1)
    grad_x = input_grad(bounds, mid_grad, wse, taps_se)
    arrived[0], grad_x = lax.optimization_barrier((arrived[0], grad_x))

    mid, prior, se_sums, gates, lags = [], [], [], (), ()
    for q in range(PIECES):
        mid_piece, gate_piece, se_sum = middle(
            q, bounds, counts, destinations, loaded, arrived[q], rim, gate_se, taps_se, mid_grad, wse, gates
        )
        gates = (gate_piece,)
        lags = (lag_grads(q, bounds, mid_piece, weighted, after, lags),)
        mid.append(mid_piece)
        se_sums.append(se_sum)
        if q < PIECES - 1:
            prior.append(from_behind(mid_piece, "ctx", 1))
    grad_gate_se = gates[0]

    windows = max(group_count // LANES, 1)
    each = PIECES // windows
    se_windows = [sum(se_sums[w * each : (w + 1) * each]) for w in range(windows)]
    total = jnp.concatenate([lags[0], *se_windows], axis=0)
    prior.append(from_behind(mid[-1], "ctx", 1))

    mask = ctx_count // 2
    grad_gate_mr = ()
    while mask > 2:
        total = total + partner(total, "ctx", mask)
        if not grad_gate_mr:
            grad_gate_mr = (gate_grad(0, bounds, prior[0], mid[0], incoming, mirrored, ()),)
            total, *grad_gate_mr = lax.optimization_barrier((total, *grad_gate_mr))
        mask //= 2
    total, rim_next, *prior[1:] = lax.optimization_barrier((total, rim_next, *prior[1:]))
    one, two, three = (partner(total, "ctx", mask) for mask in (1, 2, 3))
    grad_x = rim_grad(bounds, mid_grad, wse, rim_next, taps_se, grad_x)
    for q in range(1, PIECES):
        grad_gate_mr = (gate_grad(q, bounds, prior[q], mid[q], incoming, mirrored, tuple(grad_gate_mr)),)
    total = (total + one) + (two + three)

    scale = 1.0 / math.sqrt(ctx_count * rows * GROUP)
    total = total * scale
    mr_total = total[:group_count]
    se_total = total[group_count:].reshape(windows, RIM, -1).transpose(0, 2, 1)
    se_total = se_total.reshape(group_count, RIM)[:, : se_taps.shape[2]]
    return (grad_x[None], grad_gate_se[None], grad_gate_mr[0][None], se_total[None], mr_total[None])


def solution(mesh):
    return jax.shard_map(
        body,
        mesh=mesh,
        in_specs=(
            P("pipe", "ctx", None, None),
            P("ctx"),
            P("ctx"),
            P(),
            P("pipe", "ctx", None),
            P("pipe", "ctx", None),
            P("pipe", "ctx", None),
            P("pipe", None, None),
            P("pipe", None, None),
        ),
        out_specs=(
            P("pipe", "ctx", None),
            P("pipe", "ctx", None),
            P("pipe", "ctx", None),
            P("pipe", None, None),
            P("pipe", None, None),
        ),
        check_vma=False,
    )
```

time: 150 us -> 115 us (0.77)
  waiting for transfers between devices: 51.3 us -> 24.8 us
  starting transfers between devices: 29.2 us -> 43.9 us
  local copies, waits for them, and re-layouts: 12.9 us -> 3.02 us
  between operations: 5.54 us -> 1.49 us
  Pallas kernels: 43.9 us -> 40 us
  other arithmetic: 5.44 us -> 1.57 us
    ppermute x5 -> x6, waiting for transfers between devices: 25.1 us -> 10.7 us  [partner(): return lax.ppermute(value, axis, pairs)]
    ppermute x8 -> x7, waiting for transfers between devices: 26.2 us -> 14.1 us  [from_behind(): return lax.ppermute(block, axis, route)]
    ppermute x5 -> x6, starting transfers between devices: 5.59 us -> 17.2 us  [partner(): return lax.ppermute(value, axis, pairs)]
    pallas_call x6 -> x12, Pallas kernels: 43.9 us -> 40 us  [the longest x2 7.51 us: gate_grad(): pl.pallas_call(gate_kernel, grid=(part // BLOCK,), in_specs=[SCALARS, own...]
    slice x7 -> x1, local copies, waits for them, and re-layouts: 3.35 us -> 0.01 us  [body(): rim_next = from_behind(wse[:RIM], 'ctx', -1)]
    squeeze x1 -> x0, local copies, waits for them, and re-layouts: 3.17 us -> none  [body(): lax.dynamic_index_in_dim(slots, jnp.where(send_first, 0, 1), 0, False)]
    ppermute x8 -> x7, starting transfers between devices: 23.6 us -> 26.7 us  [from_behind(): return lax.ppermute(block, axis, route)]
    select_n x2 -> x0, other arithmetic: 2.95 us -> none  [the longest x1 1.49 us: body(): jnp.where(send_first | send_second, outgoing[rows - RIM:], nothing)]
  transfers between devices with their start and end apart: 13 -> 13, of which waited for: 4 -> 7; matrix products, arithmetic and copies ran while one was open for 11% -> 1% of each run, Pallas kernels for 22% -> 35%
where the time goes in v2:
time: 115 us
  starting transfers between devices  43.9 us (38%)
  Pallas kernels  40 us (35%)
  waiting for transfers between devices  24.8 us (22%)
  local copies, waits for them, and re-layouts  3.02 us (3%)
  other arithmetic  1.57 us (1%)
  between operations  1.49 us (1%)
    ppermute x7, starting transfers between devices, from_behind(): return lax.ppermute(block, axis, route)  26.7 us
    ppermute x6, starting transfers between devices, partner(): return lax.ppermute(value, axis, pairs)  17.2 us
    ppermute x7, waiting for transfers between devices, from_behind(): return lax.ppermute(block, axis, route)  14.1 us
    ppermute x6, waiting for transfers between devices, partner(): return lax.ppermute(value, axis, pairs)  10.7 us
    pallas_call x2, Pallas kernels, gate_grad(): pl.pallas_call(gate_kernel, grid=(part // BLOCK,), in_specs=[SCALARS, own...  7.51 us
    pallas_call x2, Pallas kernels, middle(): pl.pallas_call(functools.partial(middle_kernel, piece * groups // PIECES...  7.36 us
    pallas_call x2, Pallas kernels, lag_grads(): pl.pallas_call(lag_kernel, grid=(part // BLOCK,), in_specs=[SCALARS, pl.B...  6.54 us
    pallas_call x1, Pallas kernels, input_grad(): pl.pallas_call(input_kernel, grid=(channels // BLOCK,), in_specs=[SCALARS...  4.16 us
  transfers between devices with their start and end apart: 13, of which 7 were waited for; matrix products, arithmetic and copies ran while one was open for 1% of the time, Pallas kernels for 35%

profile of v2, /device:TPU:0, one launch (start us, length us, event | category | flops | bytes accessed | tf_op | source)
XLA Modules:
  0.0 114.7 jit_solution(3420348689282491448)
XLA Ops:
  0.6 0.5 collective-permute-start
  1.1 2.5 %collective-permute-done.incoming = bf16[128,4096]{1,0:T(8,128)(2,1)S(1)} collective-permute-done((bf16[128,4096]{1,0:T(8,128)(2,1)}, bf16[128,4096]{1,0:T(8,128)(2,1)S(1)}, u32[]{:S(2)}, u32[]{:S(2)}) %collective-permute-start) | collective-permute-done | bytes 1048608 | tf_op jit(solution)/shard_map/ppermute | solution.py:31
  3.6 1.5 %fusion.weighted = bf16[128,4096]{1,0:T(8,128)(2,1)S(1)} fusion(bf16[128,4096]{1,0:T(8,128)(2,1)S(1)} %collective-permute-done.incoming, bf16[1,128,4096]{2,1,0:T(8,128)(2,1)} %param.14), kind=kLoop, calls=%fused_computation.1 | loop fusion | flops 2097152 | bytes 3145728 | tf_op jit(solution)/shard_map/convert_element_type | solution.py:498
  5.1 1.3 %collective-permute-start.1 = (bf16[128,4096]{1,0:T(8,128)(2,1)S(1)}, bf16[128,4096]{1,0:T(8,128)(2,1)S(1)}, u32[]{:S(2)}, u32[]{:S(2)}) collective-permute-start(bf16[128,4096]{1,0:T(8,128)(2,1)S(1)} %fusion.weighted), channel_id=1, source_target_pairs={{2,0},{4,2},{6,4},{8,6},{10,8},{12,10},{14,12},{16,14},{18,16},{20... | collective-permute-start | bytes 3145736 | tf_op jit(solution)/shard_map/ppermute | solution.py:26
  7.1 0.0 copy-start.7
  7.1 0.0 copy-start.5
  7.1 3.1 %shard_map.128 = (bf16[136,2048]{1,0:T(8,128)(2,1)}, bf16[136,2048]{1,0:T(8,128)(2,1)}, bf16[8,4096]{1,0:T(8,128)(2,1)}) custom-call(s32[1]{0:T(128)S(6)} %copy.23.counts, s32[2]{0:T(128)} %destinations.5, bf16[1,2,128,4096]{3,2,1,0:T(8,128)(2,1)} %slot.5, bf16[1,2,128,4096]{3,2,1,0:T(8,128)(2,1)} %slot.5), custom_call_target="tpu_custom_call" | custom-call | flops 1 | bytes 1 | tf_op jit(solution)/shard_map/pallas_call | solution.py:108
  10.2 6.8 %collective-permute-start.2 = (bf16[8,4096]{1,0:T(8,128)(2,1)}, bf16[8,4096]{1,0:T(8,128)(2,1)S(1)}, u32[]{:S(2)}, u32[]{:S(2)}) collective-permute-start(bf16[8,4096]{1,0:T(8,128)(2,1)} %get-tuple-element.34), channel_id=1, source_target_pairs={{0,4},{2,6},{4,8},{6,10},{8,12},{10,14},{12,16},{14,18},{16,20},{1... | collective-permute-start | bytes 196616 | tf_op jit(solution)/shard_map/ppermute | solution.py:26
  17.1 0.8 copy.18
  17.9 2.1 %shard_map.129 = (f32[256,128]{1,0:T(8,128)}, f32[256,128]{1,0:T(8,128)}, f32[8,4096]{1,0:T(8,128)}) custom-call(f32[256,128]{1,0:T(8,128)} %bitcast.28, f32[256,7]{1,0:T(8,128)} %bitcast.27), custom_call_target="tpu_custom_call" | custom-call | flops 1 | bytes 1 | tf_op jit(solution)/shard_map/pallas_call | solution.py:145
  19.9 0.9 copy-done.4
  20.9 3.5 %shard_map.130.base = f32[128,4096]{1,0:T(8,128)S(1)} custom-call(s32[16]{0:T(128)S(1)} %copy-done.5, bf16[128,4096]{1,0:T(8,128)(2,1)S(1)} %fusion.weighted, bf16[128,4096]{1,0:T(8,128)(2,1)S(1)} %collective-permute-done.incoming, f32[256,128]{1,0:T(8,128)S(1)} %copy-done.4), custom_call_target="tpu_custom_call" | custom-call | flops 1 | bytes 1 | tf_op jit(solution)/shard_map/pallas_call | solution.py:186
  24.4 0.0 collective-permute-done.2.rim
  24.4 9.0 %collective-permute-done.1.after = bf16[128,4096]{1,0:T(8,128)(2,1)S(1)} collective-permute-done((bf16[128,4096]{1,0:T(8,128)(2,1)S(1)}, bf16[128,4096]{1,0:T(8,128)(2,1)S(1)}, u32[]{:S(2)}, u32[]{:S(2)}) %collective-permute-start.1) | collective-permute-done | bytes 1048608 | tf_op jit(solution)/shard_map/ppermute | solution.py:26
  33.3 6.0 %collective-permute-start.4 = (bf16[136,2048]{1,0:T(8,128)(2,1)S(1)}, bf16[136,2048]{1,0:T(8,128)(2,1)S(1)}, u32[]{:S(2)}, u32[]{:S(2)}) collective-permute-start(bf16[136,2048]{1,0:T(8,128)(2,1)S(1)} %copy-done.9), channel_id=1, source_target_pairs={{0,2},{2,4},{4,6},{6,8},{8,10},{10,12},{12,14},{14,16},{16,18},{18... | collective-permute-start | bytes 1671176 | tf_op jit(solution)/shard_map/ppermute | solution.py:26
  39.4 1.9 %collective-permute-start.3 = (bf16[136,2048]{1,0:T(8,128)(2,1)S(1)}, bf16[136,2048]{1,0:T(8,128)(2,1)S(1)}, u32[]{:S(2)}, u32[]{:S(2)}) collective-permute-start(bf16[136,2048]{1,0:T(8,128)(2,1)S(1)} %copy-done.8), channel_id=1, source_target_pairs={{0,2},{2,4},{4,6},{6,8},{8,10},{10,12},{12,14},{14,16},{16,18},{18... | collective-permute-start | bytes 1671176 | tf_op jit(solution)/shard_map/ppermute | solution.py:26
  41.3 0.0 copy-done.1
  41.3 3.9 %shard_map.131 = (bf16[128,4096]{1,0:T(8,128)(2,1)S(1)}, bf16[128,4096]{1,0:T(8,128)(2,1)S(1)}) custom-call(s32[16]{0:T(128)S(1)} %copy-done.5, bf16[128,4096]{1,0:T(8,128)(2,1)S(1)} %collective-permute-done.1.after, f32[128,4096]{1,0:T(8,128)S(1)} %shard_map.130.base, bf16[128,4096]{1,0:T(8,128)(2,1)S(1)} %bitcast.21, f32[256,128]{1,0:T(8,128)S(1)} %copy-done.4), custom_call_target="tpu_custom_call" | custom-call | flops 1 | bytes 1 | tf_op jit(solution)/shard_map/pallas_call | solution.py:221
  45.2 0.0 copy-start
  45.2 0.0 copy-start.6
  45.2 4.2 %shard_map.132.held = bf16[128,4096]{1,0:T(8,128)(2,1)} custom-call(s32[16]{0:T(128)S(1)} %copy-done.5, bf16[128,4096]{1,0:T(8,128)(2,1)S(1)} %get-tuple-element.43.grad, bf16[128,4096]{1,0:T(8,128)(2,1)S(1)} %get-tuple-element.44.wse, f32[8,4096]{1,0:T(8,128)S(1)} %copy-done.2), custom_call_target="tpu_custom_call" | custom-call | flops 1 | bytes 1 | tf_op jit(solution)/shard_map/pallas_call | solution.py:399
  49.4 2.9 %collective-permute-done.4.arrived = bf16[136,2048]{1,0:T(8,128)(2,1)S(1)} collective-permute-done((bf16[136,2048]{1,0:T(8,128)(2,1)S(1)}, bf16[136,2048]{1,0:T(8,128)(2,1)S(1)}, u32[]{:S(2)}, u32[]{:S(2)}) %collective-permute-start.4) | collective-permute-done | bytes 557088 | tf_op jit(solution)/shard_map/ppermute | solution.py:26
  52.3 3.7 %shard_map.133 = (bf16[128,2048]{1,0:T(8,128)(2,1)S(1)}, bf16[128,4096]{1,0:T(8,128)(2,1)}, f32[8,128]{1,0:T(8,128)S(1)}) custom-call(s32[16]{0:T(128)S(1)} %copy-done.5, s32[1]{0:T(128)S(6)} %copy.23.counts, s32[2]{0:T(128)S(1)} %copy-done.6, bf16[1,2,128,4096]{3,2,1,0:T(8,128)(2,1)S(1)} %copy-done, bf16[136,2048]{1,0:T(8,128)(2,1)S(1)} %collective-permute-done.4.arrived, ...), custom_call_target="tpu_custom_call" | custom-call | flops 1 | bytes 1 | tf_op jit(solution)/shard_map/pallas_call | solution.py:292
  56.0 4.6 %collective-permute-start.6 = (bf16[128,2048]{1,0:T(8,128)(2,1)S(1)}, bf16[128,2048]{1,0:T(8,128)(2,1)S(1)}, u32[]{:S(2)}, u32[]{:S(2)}) collective-permute-start(bf16[128,2048]{1,0:T(8,128)(2,1)S(1)} %get-tuple-element.52.mid), channel_id=1, source_target_pairs={{0,2},{2,4},{4,6},{6,8},{8,10},{10,12},{12,14},{14,16},{16,18},{18... | collective-permute-start | bytes 1572872 | tf_op jit(solution)/shard_map/ppermute | solution.py:26
  60.6 3.3 %shard_map.135.rest_0_ = f32[256,128]{1,0:T(8,128)S(1)} custom-call(s32[16]{0:T(128)S(1)} %copy-done.5, bf16[128,2048]{1,0:T(8,128)(2,1)S(1)} %get-tuple-element.52.mid, bf16[128,4096]{1,0:T(8,128)(2,1)S(1)} %fusion.weighted, bf16[128,4096]{1,0:T(8,128)(2,1)S(1)} %collective-permute-done.1.after), custom_call_target="tpu_custom_call" | custom-call | flops 1 | bytes 1 | tf_op jit(solution)/shard_map/pallas_call | solution.py:361
  63.9 0.4 collective-permute-done.3.arrived
  64.3 3.7 %shard_map.134 = (bf16[128,2048]{1,0:T(8,128)(2,1)S(1)}, bf16[128,4096]{1,0:T(8,128)(2,1)}, f32[8,128]{1,0:T(8,128)S(1)}) custom-call(s32[16]{0:T(128)S(1)} %copy-done.5, s32[1]{0:T(128)S(6)} %copy.23.counts, s32[2]{0:T(128)S(1)} %copy-done.6, bf16[1,2,128,4096]{3,2,1,0:T(8,128)(2,1)S(1)} %copy-done, ...), custom_call_target="tpu_custom_call", output_to_operand_aliasing={{1}: (10, {})} | custom-call | flops 1 | bytes 1 | tf_op jit(solution)/shard_map/pallas_call | solution.py:292
  67.9 4.5 %collective-permute-start.9 = (bf16[128,2048]{1,0:T(8,128)(2,1)S(1)}, bf16[128,2048]{1,0:T(8,128)(2,1)S(1)}, u32[]{:S(2)}, u32[]{:S(2)}) collective-permute-start(bf16[128,2048]{1,0:T(8,128)(2,1)S(1)} %get-tuple-element.51.mid), channel_id=1, source_target_pairs={{0,2},{2,4},{4,6},{6,8},{8,10},{10,12},{12,14},{14,16},{16,18},{18... | collective-permute-start | bytes 1572872 | tf_op jit(solution)/shard_map/ppermute | solution.py:26
  72.5 3.3 %shard_map.136 = f32[256,128]{1,0:T(8,128)S(1)} custom-call(s32[16]{0:T(128)S(1)} %copy-done.5, bf16[128,2048]{1,0:T(8,128)(2,1)S(1)} %get-tuple-element.51.mid, bf16[128,4096]{1,0:T(8,128)(2,1)S(1)} %fusion.weighted, bf16[128,4096]{1,0:T(8,128)(2,1)S(1)} %collective-permute-done.1.after, ...), custom_call_target="tpu_custom_call", output_to_operand_aliasing={{}: (4, {})} | custom-call | flops 1 | bytes 1 | tf_op jit(solution)/shard_map/pallas_call | solution.py:361
  75.8 2.6 %collective-permute-start.5 = (f32[272,128]{1,0:T(8,128)S(1)}, f32[272,128]{1,0:T(8,128)S(1)}, u32[]{:S(2)}, u32[]{:S(2)}) collective-permute-start(f32[272,128]{1,0:T(8,128)S(1)} %pad_maximum_fusion), channel_id=1, source_target_pairs={{0,16},{2,18},{4,20},{6,22},{8,24},{10,26},{12,28},{14,30},{16,0},... | collective-permute-start | bytes 417800 | tf_op jit(solution)/shard_map/ppermute | solution.py:31
  78.4 5.3 %collective-permute-done.5 = f32[272,128]{1,0:T(8,128)S(1)} collective-permute-done((f32[272,128]{1,0:T(8,128)S(1)}, f32[272,128]{1,0:T(8,128)S(1)}, u32[]{:S(2)}, u32[]{:S(2)}) %collective-permute-start.5) | collective-permute-done | bytes 139296 | tf_op jit(solution)/shard_map/ppermute | solution.py:31
  83.8 0.0 collective-permute-done.6.prior
  83.8 3.8 %shard_map.137.rest_0_ = bf16[128,4096]{1,0:T(8,128)(2,1)} custom-call(s32[16]{0:T(128)S(1)} %copy-done.5, bf16[128,2048]{1,0:T(8,128)(2,1)S(1)} %collective-permute-done.6.prior, bf16[128,2048]{1,0:T(8,128)(2,1)S(1)} %get-tuple-element.52.mid, bf16[128,4096]{1,0:T(8,128)(2,1)S(1)} %collective-permute-done.incoming, f32[256,128]{1,0:T(8,128)S(1)} %copy-done.3), custom_call_target="tpu_custom_call" | custom-call | flops 1 | bytes 1 | tf_op jit(solution)/shard_map/pallas_call | solution.py:477
  87.6 0.7 collective-permute-start.7
  88.3 1.5 %collective-permute-start.8 = (bf16[8,4096]{1,0:T(8,128)(2,1)S(1)}, bf16[8,4096]{1,0:T(8,128)(2,1)S(1)}, u32[]{:S(2)}, u32[]{:S(2)}) collective-permute-start(bf16[8,4096]{1,0:T(8,128)(2,1)S(1)} %slice.12), channel_id=1, source_target_pairs={{2,0},{4,2},{6,4},{8,6},{10,8},{12,10},{14,12},{16,14},{18,16},{20... | collective-permute-start | bytes 196616 | tf_op jit(solution)/shard_map/ppermute | solution.py:26
  89.8 2.8 %collective-permute-done.7 = f32[272,128]{1,0:T(8,128)S(1)} collective-permute-done((f32[272,128]{1,0:T(8,128)S(1)}, f32[272,128]{1,0:T(8,128)S(1)}, u32[]{:S(2)}, u32[]{:S(2)}) %collective-permute-start.7) | collective-permute-done | bytes 139296 | tf_op jit(solution)/shard_map/ppermute | solution.py:31
  92.6 1.8 %collective-permute-done.8.rim = bf16[8,4096]{1,0:T(8,128)(2,1)S(1)} collective-permute-done((bf16[8,4096]{1,0:T(8,128)(2,1)S(1)}, bf16[8,4096]{1,0:T(8,128)(2,1)S(1)}, u32[]{:S(2)}, u32[]{:S(2)}) %collective-permute-start.8) | collective-permute-done | bytes 65568 | tf_op jit(solution)/shard_map/ppermute | solution.py:26
  94.4 0.0 collective-permute-done.9.prior
  94.4 9.5 %collective-permute-start.11 = (f32[272,128]{1,0:T(8,128)S(1)}, f32[272,128]{1,0:T(8,128)S(1)}, u32[]{:S(2)}, u32[]{:S(2)}) collective-permute-start(f32[272,128]{1,0:T(8,128)S(1)} %add.16), channel_id=1, source_target_pairs={{0,4},{2,6},{4,0},{6,2},{8,12},{10,14},{12,8},{14,10},{16,20},{18,... | collective-permute-start | bytes 417800 | tf_op jit(solution)/shard_map/ppermute | solution.py:31
  103.9 3.3 %collective-permute-start.12 = (f32[272,128]{1,0:T(8,128)S(1)}, f32[272,128]{1,0:T(8,128)S(1)}, u32[]{:S(2)}, u32[]{:S(2)}) collective-permute-start(f32[272,128]{1,0:T(8,128)S(1)} %add.16), channel_id=1, source_target_pairs={{0,6},{2,4},{4,2},{6,0},{8,14},{10,12},{12,10},{14,8},{16,22},{18,... | collective-permute-start | bytes 417800 | tf_op jit(solution)/shard_map/ppermute | solution.py:31
  107.2 0.6 collective-permute-start.10
  107.8 1.9 %shard_map.138 = bf16[128,4096]{1,0:T(8,128)(2,1)} custom-call(s32[16]{0:T(128)S(1)} %copy-done.5, bf16[128,4096]{1,0:T(8,128)(2,1)S(1)} %get-tuple-element.43.grad, bf16[128,4096]{1,0:T(8,128)(2,1)S(1)} %get-tuple-element.44.wse, bf16[8,4096]{1,0:T(8,128)(2,1)S(1)} %collective-permute-done.8.rim, ...), custom_call_target="tpu_custom_call", output_to_operand_aliasing={{}: (5, {})} | custom-call | flops 1 | bytes 1 | tf_op jit(solution)/shard_map/pallas_call | solution.py:436
  109.6 3.7 %shard_map.139 = bf16[128,4096]{1,0:T(8,128)(2,1)} custom-call(s32[16]{0:T(128)S(1)} %copy-done.5, bf16[128,2048]{1,0:T(8,128)(2,1)S(1)} %collective-permute-done.9.prior, bf16[128,2048]{1,0:T(8,128)(2,1)S(1)} %get-tuple-element.51.mid, bf16[128,4096]{1,0:T(8,128)(2,1)S(1)} %collective-permute-done.incoming, ...), custom_call_target="tpu_custom_call", output_to_operand_aliasing={{}: (5, {})} | custom-call | flops 1 | bytes 1 | tf_op jit(solution)/shard_map/pallas_call | solution.py:477
  113.4 0.0 collective-permute-done.11
  113.4 0.0 collective-permute-done.12
  113.4 0.0 collective-permute-done.10
  113.5 0.7 slice_bitcast_fusion
  114.1 0.6 broadcast_in_dim.18
  (20 shorter events, 0.1 us)
Async XLA Ops:
  0.6 3.0 %collective-permute-start = (bf16[128,4096]{1,0:T(8,128)(2,1)}, bf16[128,4096]{1,0:T(8,128)(2,1)S(1)}, u32[]{:S(2)}, u32[]{:S(2)}) collective-permute-start(bf16[128,4096]{1,0:T(8,128)(2,1)} %bitcast.30), channel_id=1, source_target_pairs={{0,1},{1,0},{2,3},{3,2},{4,5},{5,4},{6,7},{7,6},{8,9},{9,8},{10,11... | collective-permute-start | bytes 3145736 | tf_op jit(solution)/shard_map/ppermute | solution.py:31
  5.1 28.2 %collective-permute-start.1 = (bf16[128,4096]{1,0:T(8,128)(2,1)S(1)}, bf16[128,4096]{1,0:T(8,128)(2,1)S(1)}, u32[]{:S(2)}, u32[]{:S(2)}) collective-permute-start(bf16[128,4096]{1,0:T(8,128)(2,1)S(1)} %fusion.weighted), channel_id=1, source_target_pairs={{2,0},{4,2},{6,4},{8,6},{10,8},{12,10},{14,12},{16,14},{18,16},{20... | collective-permute-start | bytes 3145736 | tf_op jit(solution)/shard_map/ppermute | solution.py:26
  7.1 10.0 %copy-start.7 = (f32[1,256,7]{1,0,2:T(1,128)S(1)}, f32[1,256,7]{1,0,2:T(1,128)}, u32[]{:S(2)}) copy-start(f32[1,256,7]{1,0,2:T(1,128)} %param.16) | copy-start | bytes 21508
  7.1 12.9 %copy-start.5 = (s32[16]{0:T(128)S(1)}, s32[16]{0:T(128)}, u32[]{:S(2)}) copy-start(s32[16]{0:T(128)} %bounds.19) | copy-start | bytes 196
  10.2 14.2 %collective-permute-start.2 = (bf16[8,4096]{1,0:T(8,128)(2,1)}, bf16[8,4096]{1,0:T(8,128)(2,1)S(1)}, u32[]{:S(2)}, u32[]{:S(2)}) collective-permute-start(bf16[8,4096]{1,0:T(8,128)(2,1)} %get-tuple-element.34), channel_id=1, source_target_pairs={{0,4},{2,6},{4,8},{6,10},{8,12},{10,14},{12,16},{14,18},{16,20},{1... | collective-permute-start | bytes 196616 | tf_op jit(solution)/shard_map/ppermute | solution.py:26
  19.9 0.9 copy-start.4
  20.9 12.5 %copy-start.9 = (bf16[136,2048]{1,0:T(8,128)(2,1)S(1)}, bf16[136,2048]{1,0:T(8,128)(2,1)}, u32[]{:S(2)}) copy-start(bf16[136,2048]{1,0:T(8,128)(2,1)} %get-tuple-element.48) | copy-start | bytes 1671172
  20.9 18.5 %copy-start.8 = (bf16[136,2048]{1,0:T(8,128)(2,1)S(1)}, bf16[136,2048]{1,0:T(8,128)(2,1)}, u32[]{:S(2)}) copy-start(bf16[136,2048]{1,0:T(8,128)(2,1)} %get-tuple-element.45) | copy-start | bytes 1671172
  20.9 20.5 %copy-start.1 = (bf16[1,128,4096]{2,1,0:T(8,128)(2,1)S(1)}, bf16[1,128,4096]{2,1,0:T(8,128)(2,1)}, u32[]{:S(2)}) copy-start(bf16[1,128,4096]{2,1,0:T(8,128)(2,1)} %param.13) | copy-start | bytes 3145732
  33.3 19.0 %collective-permute-start.4 = (bf16[136,2048]{1,0:T(8,128)(2,1)S(1)}, bf16[136,2048]{1,0:T(8,128)(2,1)S(1)}, u32[]{:S(2)}, u32[]{:S(2)}) collective-permute-start(bf16[136,2048]{1,0:T(8,128)(2,1)S(1)} %copy-done.9), channel_id=1, source_target_pairs={{0,2},{2,4},{4,6},{6,8},{8,10},{10,12},{12,14},{14,16},{16,18},{18... | collective-permute-start | bytes 1671176 | tf_op jit(solution)/shard_map/ppermute | solution.py:26
  39.4 24.9 %collective-permute-start.3 = (bf16[136,2048]{1,0:T(8,128)(2,1)S(1)}, bf16[136,2048]{1,0:T(8,128)(2,1)S(1)}, u32[]{:S(2)}, u32[]{:S(2)}) collective-permute-start(bf16[136,2048]{1,0:T(8,128)(2,1)S(1)} %copy-done.8), channel_id=1, source_target_pairs={{0,2},{2,4},{4,6},{6,8},{8,10},{10,12},{12,14},{14,16},{16,18},{18... | collective-permute-start | bytes 1671176 | tf_op jit(solution)/shard_map/ppermute | solution.py:26
  41.3 3.9 %copy-start.2 = (f32[8,4096]{1,0:T(8,128)S(1)}, f32[8,4096]{1,0:T(8,128)}, u32[]{:S(2)}) copy-start(f32[8,4096]{1,0:T(8,128)} %get-tuple-element.47.taps) | copy-start | bytes 393220
  45.2 7.1 %copy-start = (bf16[1,2,128,4096]{3,2,1,0:T(8,128)(2,1)S(1)}, bf16[1,2,128,4096]{3,2,1,0:T(8,128)(2,1)}, u32[]{:S(2)}) copy-start(bf16[1,2,128,4096]{3,2,1,0:T(8,128)(2,1)} %slot.5) | copy-start | bytes 6291460
  45.2 7.1 %copy-start.6 = (s32[2]{0:T(128)S(1)}, s32[2]{0:T(128)}, u32[]{:S(2)}) copy-start(s32[2]{0:T(128)} %destinations.5) | copy-start | bytes 28
  56.0 27.8 %collective-permute-start.6 = (bf16[128,2048]{1,0:T(8,128)(2,1)S(1)}, bf16[128,2048]{1,0:T(8,128)(2,1)S(1)}, u32[]{:S(2)}, u32[]{:S(2)}) collective-permute-start(bf16[128,2048]{1,0:T(8,128)(2,1)S(1)} %get-tuple-element.52.mid), channel_id=1, source_target_pairs={{0,2},{2,4},{4,6},{6,8},{8,10},{10,12},{12,14},{14,16},{16,18},{18... | collective-permute-start | bytes 1572872 | tf_op jit(solution)/shard_map/ppermute | solution.py:26
  67.9 15.8 %copy-start.3 = (f32[256,128]{1,0:T(8,128)S(1)}, f32[256,128]{1,0:T(8,128)}, u32[]{:S(2)}) copy-start(f32[256,128]{1,0:T(8,128)} %get-tuple-element.55.mirrored) | copy-start | bytes 393220
  67.9 26.5 %collective-permute-start.9 = (bf16[128,2048]{1,0:T(8,128)(2,1)S(1)}, bf16[128,2048]{1,0:T(8,128)(2,1)S(1)}, u32[]{:S(2)}, u32[]{:S(2)}) collective-permute-start(bf16[128,2048]{1,0:T(8,128)(2,1)S(1)} %get-tuple-element.51.mid), channel_id=1, source_target_pairs={{0,2},{2,4},{4,6},{6,8},{8,10},{10,12},{12,14},{14,16},{16,18},{18... | collective-permute-start | bytes 1572872 | tf_op jit(solution)/shard_map/ppermute | solution.py:26
  75.8 8.0 %collective-permute-start.5 = (f32[272,128]{1,0:T(8,128)S(1)}, f32[272,128]{1,0:T(8,128)S(1)}, u32[]{:S(2)}, u32[]{:S(2)}) collective-permute-start(f32[272,128]{1,0:T(8,128)S(1)} %pad_maximum_fusion), channel_id=1, source_target_pairs={{0,16},{2,18},{4,20},{6,22},{8,24},{10,26},{12,28},{14,30},{16,0},... | collective-permute-start | bytes 417800 | tf_op jit(solution)/shard_map/ppermute | solution.py:31
  87.6 5.1 %collective-permute-start.7 = (f32[272,128]{1,0:T(8,128)S(1)}, f32[272,128]{1,0:T(8,128)S(1)}, u32[]{:S(2)}, u32[]{:S(2)}) collective-permute-start(f32[272,128]{1,0:T(8,128)S(1)} %fusion.1), channel_id=1, source_target_pairs={{0,8},{2,10},{4,12},{6,14},{8,0},{10,2},{12,4},{14,6},{16,24},{18,... | collective-permute-start | bytes 417800 | tf_op jit(solution)/shard_map/ppermute | solution.py:31
  88.3 6.1 %collective-permute-start.8 = (bf16[8,4096]{1,0:T(8,128)(2,1)S(1)}, bf16[8,4096]{1,0:T(8,128)(2,1)S(1)}, u32[]{:S(2)}, u32[]{:S(2)}) collective-permute-start(bf16[8,4096]{1,0:T(8,128)(2,1)S(1)} %slice.12), channel_id=1, source_target_pairs={{2,0},{4,2},{6,4},{8,6},{10,8},{12,10},{14,12},{16,14},{18,16},{20... | collective-permute-start | bytes 196616 | tf_op jit(solution)/shard_map/ppermute | solution.py:26
  94.4 19.0 %collective-permute-start.11 = (f32[272,128]{1,0:T(8,128)S(1)}, f32[272,128]{1,0:T(8,128)S(1)}, u32[]{:S(2)}, u32[]{:S(2)}) collective-permute-start(f32[272,128]{1,0:T(8,128)S(1)} %add.16), channel_id=1, source_target_pairs={{0,4},{2,6},{4,0},{6,2},{8,12},{10,14},{12,8},{14,10},{16,20},{18,... | collective-permute-start | bytes 417800 | tf_op jit(solution)/shard_map/ppermute | solution.py:31
  103.9 9.5 %collective-permute-start.12 = (f32[272,128]{1,0:T(8,128)S(1)}, f32[272,128]{1,0:T(8,128)S(1)}, u32[]{:S(2)}, u32[]{:S(2)}) collective-permute-start(f32[272,128]{1,0:T(8,128)S(1)} %add.16), channel_id=1, source_target_pairs={{0,6},{2,4},{4,2},{6,0},{8,14},{10,12},{12,10},{14,8},{16,22},{18,... | collective-permute-start | bytes 417800 | tf_op jit(solution)/shard_map/ppermute | solution.py:31
  107.2 6.2 %collective-permute-start.10 = (f32[272,128]{1,0:T(8,128)S(1)}, f32[272,128]{1,0:T(8,128)S(1)}, u32[]{:S(2)}, u32[]{:S(2)}) collective-permute-start(f32[272,128]{1,0:T(8,128)S(1)} %add.16), channel_id=1, source_target_pairs={{0,2},{2,0},{4,6},{6,4},{8,10},{10,8},{12,14},{14,12},{16,18},{18,... | collective-permute-start | bytes 417800 | tf_op jit(solution)/shard_map/ppermute | solution.py:31

commit v3 on v2

--- a/solution.py
+++ b/solution.py
@@ -508,7 +508,6 @@
     arrived = [from_behind(piece, "ctx", 1) for piece in outgoing]
 
     mid_grad, wse = next_back(bounds, after, base, gate_se, low)
-    rim_next = from_behind(wse[:RIM], "ctx", -1)
     grad_x = input_grad(bounds, mid_grad, wse, taps_se)
     arrived[0], grad_x = lax.optimization_barrier((arrived[0], grad_x))
 
@@ -529,21 +528,24 @@
     each = PIECES // windows
     se_windows = [sum(se_sums[w * each : (w + 1) * each]) for w in range(windows)]
     total = jnp.concatenate([lags[0], *se_windows], axis=0)
+    total, mid[-1] = lax.optimization_barrier((total, mid[-1]))
     prior.append(from_behind(mid[-1], "ctx", 1))
+    grad_gate_mr = (gate_grad(0, bounds, prior[0], mid[0], incoming, mirrored, ()),)
+    total, wse, *grad_gate_mr = lax.optimization_barrier((total, wse, *grad_gate_mr))
+    rim_next = from_behind(wse[:RIM], "ctx", -1)
 
     mask = ctx_count // 2
-    grad_gate_mr = ()
     while mask > 2:
         total = total + partner(total, "ctx", mask)
-        if not grad_gate_mr:
-            grad_gate_mr = (gate_grad(0, bounds, prior[0], mid[0], incoming, mirrored, ()),)
+        if mask == 4:
+            for q in range(1, PIECES):
+                grad_gate_mr = (gate_grad(q, bounds, prior[q], mid[q], incoming, mirrored, tuple(grad_gate_mr)),)
             total, *grad_gate_mr = lax.optimization_barrier((total, *grad_gate_mr))
+        else:
+            total, rim_next = lax.optimization_barrier((total, rim_next))
         mask //= 2
-    total, rim_next, *prior[1:] = lax.optimization_barrier((total, rim_next, *prior[1:]))
     one, two, three = (partner(total, "ctx", mask) for mask in (1, 2, 3))
     grad_x = rim_grad(bounds, mid_grad, wse, rim_next, taps_se, grad_x)
-    for q in range(1, PIECES):
-        grad_gate_mr = (gate_grad(q, bounds, prior[q], mid[q], incoming, mirrored, tuple(grad_gate_mr)),)
     total = (total + one) + (two + three)
 
     scale = 1.0 / math.sqrt(ctx_count * rows * GROUP)

time: 115 us -> 108 us (0.939)
  starting transfers between devices: 43.9 us -> 37.7 us
    ppermute x6, starting transfers between devices: 17.2 us -> 11.2 us  [partner(): return lax.ppermute(value, axis, pairs)]
    ppermute x7, waiting for transfers between devices: 14.1 us -> 12.3 us  [from_behind(): return lax.ppermute(block, axis, route)]
  transfers between devices with their start and end apart: 13 -> 13, of which waited for: 7 -> 8; matrix products, arithmetic and copies ran while one was open for 1% -> 1% of each run, Pallas kernels for 35% -> 37%
where the time goes in v3:
time: 108 us
  Pallas kernels  40 us (37%)
  starting transfers between devices  37.7 us (35%)
  waiting for transfers between devices  23.9 us (22%)
  local copies, waits for them, and re-layouts  3.02 us (3%)
  other arithmetic  1.55 us (1%)
  between operations  1.51 us (1%)
    ppermute x7, starting transfers between devices, from_behind(): return lax.ppermute(block, axis, route)  26.6 us
    ppermute x7, waiting for transfers between devices, from_behind(): return lax.ppermute(block, axis, route)  12.3 us
    ppermute x6, waiting for transfers between devices, partner(): return lax.ppermute(value, axis, pairs)  11.6 us
    ppermute x6, starting transfers between devices, partner(): return lax.ppermute(value, axis, pairs)  11.2 us
    pallas_call x2, Pallas kernels, gate_grad(): pl.pallas_call(gate_kernel, grid=(part // BLOCK,), in_specs=[SCALARS, own...  7.5 us
    pallas_call x2, Pallas kernels, middle(): pl.pallas_call(functools.partial(middle_kernel, piece * groups // PIECES...  7.36 us
    pallas_call x2, Pallas kernels, lag_grads(): pl.pallas_call(lag_kernel, grid=(part // BLOCK,), in_specs=[SCALARS, pl.B...  6.54 us
    pallas_call x1, Pallas kernels, input_grad(): pl.pallas_call(input_kernel, grid=(channels // BLOCK,), in_specs=[SCALARS...  4.16 us
  transfers between devices with their start and end apart: 13, of which 8 were waited for; matrix products, arithmetic and copies ran while one was open for 1% of the time, Pallas kernels for 37%

profile of v3, /device:TPU:0, one launch (start us, length us, event | category | flops | bytes accessed | tf_op | source)
XLA Modules:
  0.0 107.7 jit_solution(12847745184524539804)
XLA Ops:
  0.6 0.5 collective-permute-start
  1.1 2.5 %collective-permute-done.incoming = bf16[128,4096]{1,0:T(8,128)(2,1)S(1)} collective-permute-done((bf16[128,4096]{1,0:T(8,128)(2,1)}, bf16[128,4096]{1,0:T(8,128)(2,1)S(1)}, u32[]{:S(2)}, u32[]{:S(2)}) %collective-permute-start) | collective-permute-done | bytes 1048608 | tf_op jit(solution)/shard_map/ppermute | solution.py:31
  3.6 1.5 %fusion.weighted = bf16[128,4096]{1,0:T(8,128)(2,1)S(1)} fusion(bf16[128,4096]{1,0:T(8,128)(2,1)S(1)} %collective-permute-done.incoming, bf16[1,128,4096]{2,1,0:T(8,128)(2,1)} %param.14), kind=kLoop, calls=%fused_computation.1 | loop fusion | flops 2097152 | bytes 3145728 | tf_op jit(solution)/shard_map/convert_element_type | solution.py:498
  5.1 1.3 %collective-permute-start.1 = (bf16[128,4096]{1,0:T(8,128)(2,1)S(1)}, bf16[128,4096]{1,0:T(8,128)(2,1)S(1)}, u32[]{:S(2)}, u32[]{:S(2)}) collective-permute-start(bf16[128,4096]{1,0:T(8,128)(2,1)S(1)} %fusion.weighted), channel_id=1, source_target_pairs={{2,0},{4,2},{6,4},{8,6},{10,8},{12,10},{14,12},{16,14},{18,16},{20... | collective-permute-start | bytes 3145736 | tf_op jit(solution)/shard_map/ppermute | solution.py:26
  7.1 0.0 copy-start.7
  7.1 0.0 copy-start.5
  7.1 3.1 %shard_map.128 = (bf16[136,2048]{1,0:T(8,128)(2,1)}, bf16[136,2048]{1,0:T(8,128)(2,1)}, bf16[8,4096]{1,0:T(8,128)(2,1)}) custom-call(s32[1]{0:T(128)S(6)} %copy.23.counts, s32[2]{0:T(128)} %destinations.5, bf16[1,2,128,4096]{3,2,1,0:T(8,128)(2,1)} %slot.5, bf16[1,2,128,4096]{3,2,1,0:T(8,128)(2,1)} %slot.5), custom_call_target="tpu_custom_call" | custom-call | flops 1 | bytes 1 | tf_op jit(solution)/shard_map/pallas_call | solution.py:108
  10.2 6.8 %collective-permute-start.2 = (bf16[8,4096]{1,0:T(8,128)(2,1)}, bf16[8,4096]{1,0:T(8,128)(2,1)S(1)}, u32[]{:S(2)}, u32[]{:S(2)}) collective-permute-start(bf16[8,4096]{1,0:T(8,128)(2,1)} %get-tuple-element.38), channel_id=1, source_target_pairs={{0,4},{2,6},{4,8},{6,10},{8,12},{10,14},{12,16},{14,18},{16,20},{1... | collective-permute-start | bytes 196616 | tf_op jit(solution)/shard_map/ppermute | solution.py:26
  17.1 0.8 copy.18
  17.9 2.1 %shard_map.129 = (f32[256,128]{1,0:T(8,128)}, f32[256,128]{1,0:T(8,128)}, f32[8,4096]{1,0:T(8,128)}) custom-call(f32[256,128]{1,0:T(8,128)} %bitcast.28, f32[256,7]{1,0:T(8,128)} %bitcast.27), custom_call_target="tpu_custom_call" | custom-call | flops 1 | bytes 1 | tf_op jit(solution)/shard_map/pallas_call | solution.py:145
  19.9 0.9 copy-done.4
  20.9 3.5 %shard_map.130.base = f32[128,4096]{1,0:T(8,128)S(1)} custom-call(s32[16]{0:T(128)S(1)} %copy-done.5, bf16[128,4096]{1,0:T(8,128)(2,1)S(1)} %fusion.weighted, bf16[128,4096]{1,0:T(8,128)(2,1)S(1)} %collective-permute-done.incoming, f32[256,128]{1,0:T(8,128)S(1)} %copy-done.4), custom_call_target="tpu_custom_call" | custom-call | flops 1 | bytes 1 | tf_op jit(solution)/shard_map/pallas_call | solution.py:186
  24.4 0.0 collective-permute-done.2.rim
  24.4 9.0 %collective-permute-done.1.after = bf16[128,4096]{1,0:T(8,128)(2,1)S(1)} collective-permute-done((bf16[128,4096]{1,0:T(8,128)(2,1)S(1)}, bf16[128,4096]{1,0:T(8,128)(2,1)S(1)}, u32[]{:S(2)}, u32[]{:S(2)}) %collective-permute-start.1) | collective-permute-done | bytes 1048608 | tf_op jit(solution)/shard_map/ppermute | solution.py:26
  33.3 6.0 %collective-permute-start.4 = (bf16[136,2048]{1,0:T(8,128)(2,1)S(1)}, bf16[136,2048]{1,0:T(8,128)(2,1)S(1)}, u32[]{:S(2)}, u32[]{:S(2)}) collective-permute-start(bf16[136,2048]{1,0:T(8,128)(2,1)S(1)} %copy-done.9), channel_id=1, source_target_pairs={{0,2},{2,4},{4,6},{6,8},{8,10},{10,12},{12,14},{14,16},{16,18},{18... | collective-permute-start | bytes 1671176 | tf_op jit(solution)/shard_map/ppermute | solution.py:26
  39.4 1.9 %collective-permute-start.3 = (bf16[136,2048]{1,0:T(8,128)(2,1)S(1)}, bf16[136,2048]{1,0:T(8,128)(2,1)S(1)}, u32[]{:S(2)}, u32[]{:S(2)}) collective-permute-start(bf16[136,2048]{1,0:T(8,128)(2,1)S(1)} %copy-done.8), channel_id=1, source_target_pairs={{0,2},{2,4},{4,6},{6,8},{8,10},{10,12},{12,14},{14,16},{16,18},{18... | collective-permute-start | bytes 1671176 | tf_op jit(solution)/shard_map/ppermute | solution.py:26
  41.3 3.9 %shard_map.131 = (bf16[128,4096]{1,0:T(8,128)(2,1)S(1)}, bf16[128,4096]{1,0:T(8,128)(2,1)S(1)}) custom-call(s32[16]{0:T(128)S(1)} %copy-done.5, bf16[128,4096]{1,0:T(8,128)(2,1)S(1)} %collective-permute-done.1.after, f32[128,4096]{1,0:T(8,128)S(1)} %shard_map.130.base, bf16[128,4096]{1,0:T(8,128)(2,1)S(1)} %bitcast.21, f32[256,128]{1,0:T(8,128)S(1)} %copy-done.4), custom_call_target="tpu_custom_call" | custom-call | flops 1 | bytes 1 | tf_op jit(solution)/shard_map/pallas_call | solution.py:221
  45.2 0.0 copy-start
  45.2 0.0 copy-start.6
  45.2 0.0 copy-done.2
  45.2 4.2 %shard_map.132.held = bf16[128,4096]{1,0:T(8,128)(2,1)} custom-call(s32[16]{0:T(128)S(1)} %copy-done.5, bf16[128,4096]{1,0:T(8,128)(2,1)S(1)} %get-tuple-element.47.grad, bf16[128,4096]{1,0:T(8,128)(2,1)S(1)} %get-tuple-element.61.wse, f32[8,4096]{1,0:T(8,128)S(1)} %copy-done.2), custom_call_target="tpu_custom_call" | custom-call | flops 1 | bytes 1 | tf_op jit(solution)/shard_map/pallas_call | solution.py:399
  49.4 2.9 %collective-permute-done.4.arrived = bf16[136,2048]{1,0:T(8,128)(2,1)S(1)} collective-permute-done((bf16[136,2048]{1,0:T(8,128)(2,1)S(1)}, bf16[136,2048]{1,0:T(8,128)(2,1)S(1)}, u32[]{:S(2)}, u32[]{:S(2)}) %collective-permute-start.4) | collective-permute-done | bytes 557088 | tf_op jit(solution)/shard_map/ppermute | solution.py:26
  52.3 3.7 %shard_map.133 = (bf16[128,2048]{1,0:T(8,128)(2,1)S(1)}, bf16[128,4096]{1,0:T(8,128)(2,1)}, f32[8,128]{1,0:T(8,128)S(1)}) custom-call(s32[16]{0:T(128)S(1)} %copy-done.5, s32[1]{0:T(128)S(6)} %copy.23.counts, s32[2]{0:T(128)S(1)} %copy-done.6, bf16[1,2,128,4096]{3,2,1,0:T(8,128)(2,1)S(1)} %copy-done, bf16[136,2048]{1,0:T(8,128)(2,1)S(1)} %collective-permute-done.4.arrived, ...), custom_call_target="tpu_custom_call" | custom-call | flops 1 | bytes 1 | tf_op jit(solution)/shard_map/pallas_call | solution.py:292
  56.0 4.6 %collective-permute-start.5 = (bf16[128,2048]{1,0:T(8,128)(2,1)S(1)}, bf16[128,2048]{1,0:T(8,128)(2,1)S(1)}, u32[]{:S(2)}, u32[]{:S(2)}) collective-permute-start(bf16[128,2048]{1,0:T(8,128)(2,1)S(1)} %get-tuple-element.56.mid), channel_id=1, source_target_pairs={{0,2},{2,4},{4,6},{6,8},{8,10},{10,12},{12,14},{14,16},{16,18},{18... | collective-permute-start | bytes 1572872 | tf_op jit(solution)/shard_map/ppermute | solution.py:26
  60.6 3.3 %shard_map.135.rest_0_ = f32[256,128]{1,0:T(8,128)S(1)} custom-call(s32[16]{0:T(128)S(1)} %copy-done.5, bf16[128,2048]{1,0:T(8,128)(2,1)S(1)} %get-tuple-element.56.mid, bf16[128,4096]{1,0:T(8,128)(2,1)S(1)} %fusion.weighted, bf16[128,4096]{1,0:T(8,128)(2,1)S(1)} %collective-permute-done.1.after), custom_call_target="tpu_custom_call" | custom-call | flops 1 | bytes 1 | tf_op jit(solution)/shard_map/pallas_call | solution.py:361
  63.9 0.4 collective-permute-done.3.arrived
  64.3 3.7 %shard_map.134 = (bf16[128,2048]{1,0:T(8,128)(2,1)S(1)}, bf16[128,4096]{1,0:T(8,128)(2,1)}, f32[8,128]{1,0:T(8,128)S(1)}) custom-call(s32[16]{0:T(128)S(1)} %copy-done.5, s32[1]{0:T(128)S(6)} %copy.23.counts, s32[2]{0:T(128)S(1)} %copy-done.6, bf16[1,2,128,4096]{3,2,1,0:T(8,128)(2,1)S(1)} %copy-done, ...), custom_call_target="tpu_custom_call", output_to_operand_aliasing={{1}: (10, {})} | custom-call | flops 1 | bytes 1 | tf_op jit(solution)/shard_map/pallas_call | solution.py:292
  67.9 3.3 %shard_map.136 = f32[256,128]{1,0:T(8,128)S(1)} custom-call(s32[16]{0:T(128)S(1)} %copy-done.5, bf16[128,2048]{1,0:T(8,128)(2,1)S(1)} %get-tuple-element.67.mid, bf16[128,4096]{1,0:T(8,128)(2,1)S(1)} %fusion.weighted, bf16[128,4096]{1,0:T(8,128)(2,1)S(1)} %collective-permute-done.1.after, ...), custom_call_target="tpu_custom_call", output_to_operand_aliasing={{}: (4, {})} | custom-call | flops 1 | bytes 1 | tf_op jit(solution)/shard_map/pallas_call | solution.py:361
  71.2 4.4 %collective-permute-start.9 = (bf16[128,2048]{1,0:T(8,128)(2,1)S(1)}, bf16[128,2048]{1,0:T(8,128)(2,1)S(1)}, u32[]{:S(2)}, u32[]{:S(2)}) collective-permute-start(bf16[128,2048]{1,0:T(8,128)(2,1)S(1)} %get-tuple-element.67.mid), channel_id=1, source_target_pairs={{0,2},{2,4},{4,6},{6,8},{8,10},{10,12},{12,14},{14,16},{16,18},{18... | collective-permute-start | bytes 1572872 | tf_op jit(solution)/shard_map/ppermute | solution.py:26
  75.7 0.0 collective-permute-done.5.prior
  75.7 3.8 %shard_map.137.rest_0_ = bf16[128,4096]{1,0:T(8,128)(2,1)} custom-call(s32[16]{0:T(128)S(1)} %copy-done.5, bf16[128,2048]{1,0:T(8,128)(2,1)S(1)} %collective-permute-done.5.prior, bf16[128,2048]{1,0:T(8,128)(2,1)S(1)} %get-tuple-element.56.mid, bf16[128,4096]{1,0:T(8,128)(2,1)S(1)} %collective-permute-done.incoming, f32[256,128]{1,0:T(8,128)S(1)} %copy-done.3), custom_call_target="tpu_custom_call" | custom-call | flops 1 | bytes 1 | tf_op jit(solution)/shard_map/pallas_call | solution.py:477
  79.4 3.9 %collective-permute-start.6 = (f32[272,128]{1,0:T(8,128)S(1)}, f32[272,128]{1,0:T(8,128)S(1)}, u32[]{:S(2)}, u32[]{:S(2)}) collective-permute-start(f32[272,128]{1,0:T(8,128)S(1)} %pad_maximum_fusion), channel_id=1, source_target_pairs={{0,16},{2,18},{4,20},{6,22},{8,24},{10,26},{12,28},{14,30},{16,0},... | collective-permute-start | bytes 417800 | tf_op jit(solution)/shard_map/ppermute | solution.py:31
  83.3 1.5 %collective-permute-start.7 = (bf16[8,4096]{1,0:T(8,128)(2,1)S(1)}, bf16[8,4096]{1,0:T(8,128)(2,1)S(1)}, u32[]{:S(2)}, u32[]{:S(2)}) collective-permute-start(bf16[8,4096]{1,0:T(8,128)(2,1)S(1)} %slice.12), channel_id=1, source_target_pairs={{2,0},{4,2},{6,4},{8,6},{10,8},{12,10},{14,12},{16,14},{18,16},{20... | collective-permute-start | bytes 196616 | tf_op jit(solution)/shard_map/ppermute | solution.py:26
  84.9 5.5 %collective-permute-done.6 = f32[272,128]{1,0:T(8,128)S(1)} collective-permute-done((f32[272,128]{1,0:T(8,128)S(1)}, f32[272,128]{1,0:T(8,128)S(1)}, u32[]{:S(2)}, u32[]{:S(2)}) %collective-permute-start.6) | collective-permute-done | bytes 139296 | tf_op jit(solution)/shard_map/ppermute | solution.py:31
  90.4 0.0 collective-permute-done.7.rim
  90.4 0.7 collective-permute-start.8
  91.1 0.0 collective-permute-done.9.prior
  91.1 3.7 %shard_map.139 = bf16[128,4096]{1,0:T(8,128)(2,1)} custom-call(s32[16]{0:T(128)S(1)} %copy-done.5, bf16[128,2048]{1,0:T(8,128)(2,1)S(1)} %collective-permute-done.9.prior, bf16[128,2048]{1,0:T(8,128)(2,1)S(1)} %get-tuple-element.67.mid, bf16[128,4096]{1,0:T(8,128)(2,1)S(1)} %collective-permute-done.incoming, ...), custom_call_target="tpu_custom_call", output_to_operand_aliasing={{}: (5, {})} | custom-call | flops 1 | bytes 1 | tf_op jit(solution)/shard_map/pallas_call | solution.py:477
  94.8 0.7 collective-permute-done.8
  95.5 5.4 %collective-permute-start.12 = (f32[272,128]{1,0:T(8,128)S(1)}, f32[272,128]{1,0:T(8,128)S(1)}, u32[]{:S(2)}, u32[]{:S(2)}) collective-permute-start(f32[272,128]{1,0:T(8,128)S(1)} %add.16), channel_id=1, source_target_pairs={{0,6},{2,4},{4,2},{6,0},{8,14},{10,12},{12,10},{14,8},{16,22},{18,... | collective-permute-start | bytes 417800 | tf_op jit(solution)/shard_map/ppermute | solution.py:31
  100.9 0.0 collective-permute-start.11
  100.9 0.6 collective-permute-start.10
  101.6 1.9 %shard_map.138 = bf16[128,4096]{1,0:T(8,128)(2,1)} custom-call(s32[16]{0:T(128)S(1)} %copy-done.5, bf16[128,4096]{1,0:T(8,128)(2,1)S(1)} %get-tuple-element.47.grad, bf16[128,4096]{1,0:T(8,128)(2,1)S(1)} %get-tuple-element.61.wse, bf16[8,4096]{1,0:T(8,128)(2,1)S(1)} %collective-permute-done.7.rim, ...), custom_call_target="tpu_custom_call", output_to_operand_aliasing={{}: (5, {})} | custom-call | flops 1 | bytes 1 | tf_op jit(solution)/shard_map/pallas_call | solution.py:436
  103.5 1.7 %collective-permute-done.12 = f32[272,128]{1,0:T(8,128)S(1)} collective-permute-done((f32[272,128]{1,0:T(8,128)S(1)}, f32[272,128]{1,0:T(8,128)S(1)}, u32[]{:S(2)}, u32[]{:S(2)}) %collective-permute-start.12) | collective-permute-done | bytes 139296 | tf_op jit(solution)/shard_map/ppermute | solution.py:31
  105.2 1.2 %collective-permute-done.11 = f32[272,128]{1,0:T(8,128)S(1)} collective-permute-done((f32[272,128]{1,0:T(8,128)S(1)}, f32[272,128]{1,0:T(8,128)S(1)}, u32[]{:S(2)}, u32[]{:S(2)}) %collective-permute-start.11) | collective-permute-done | bytes 139296 | tf_op jit(solution)/shard_map/ppermute | solution.py:31
  106.4 0.0 collective-permute-done.10
  106.5 0.7 slice_bitcast_fusion
  107.1 0.6 broadcast_in_dim.18
  (20 shorter events, 0.1 us)
Async XLA Ops:
  0.6 3.0 %collective-permute-start = (bf16[128,4096]{1,0:T(8,128)(2,1)}, bf16[128,4096]{1,0:T(8,128)(2,1)S(1)}, u32[]{:S(2)}, u32[]{:S(2)}) collective-permute-start(bf16[128,4096]{1,0:T(8,128)(2,1)} %bitcast.30), channel_id=1, source_target_pairs={{0,1},{1,0},{2,3},{3,2},{4,5},{5,4},{6,7},{7,6},{8,9},{9,8},{10,11... | collective-permute-start | bytes 3145736 | tf_op jit(solution)/shard_map/ppermute | solution.py:31
  5.1 28.2 %collective-permute-start.1 = (bf16[128,4096]{1,0:T(8,128)(2,1)S(1)}, bf16[128,4096]{1,0:T(8,128)(2,1)S(1)}, u32[]{:S(2)}, u32[]{:S(2)}) collective-permute-start(bf16[128,4096]{1,0:T(8,128)(2,1)S(1)} %fusion.weighted), channel_id=1, source_target_pairs={{2,0},{4,2},{6,4},{8,6},{10,8},{12,10},{14,12},{16,14},{18,16},{20... | collective-permute-start | bytes 3145736 | tf_op jit(solution)/shard_map/ppermute | solution.py:26
  7.1 10.0 %copy-start.7 = (f32[1,256,7]{1,0,2:T(1,128)S(1)}, f32[1,256,7]{1,0,2:T(1,128)}, u32[]{:S(2)}) copy-start(f32[1,256,7]{1,0,2:T(1,128)} %param.16) | copy-start | bytes 21508
  7.1 12.9 %copy-start.5 = (s32[16]{0:T(128)S(1)}, s32[16]{0:T(128)}, u32[]{:S(2)}) copy-start(s32[16]{0:T(128)} %bounds.19) | copy-start | bytes 196
  10.2 14.2 %collective-permute-start.2 = (bf16[8,4096]{1,0:T(8,128)(2,1)}, bf16[8,4096]{1,0:T(8,128)(2,1)S(1)}, u32[]{:S(2)}, u32[]{:S(2)}) collective-permute-start(bf16[8,4096]{1,0:T(8,128)(2,1)} %get-tuple-element.38), channel_id=1, source_target_pairs={{0,4},{2,6},{4,8},{6,10},{8,12},{10,14},{12,16},{14,18},{16,20},{1... | collective-permute-start | bytes 196616 | tf_op jit(solution)/shard_map/ppermute | solution.py:26
  19.9 0.9 copy-start.4
  20.9 12.5 %copy-start.9 = (bf16[136,2048]{1,0:T(8,128)(2,1)S(1)}, bf16[136,2048]{1,0:T(8,128)(2,1)}, u32[]{:S(2)}) copy-start(bf16[136,2048]{1,0:T(8,128)(2,1)} %get-tuple-element.52) | copy-start | bytes 1671172
  20.9 18.5 %copy-start.8 = (bf16[136,2048]{1,0:T(8,128)(2,1)S(1)}, bf16[136,2048]{1,0:T(8,128)(2,1)}, u32[]{:S(2)}) copy-start(bf16[136,2048]{1,0:T(8,128)(2,1)} %get-tuple-element.48) | copy-start | bytes 1671172
  20.9 20.5 %copy-start.1 = (bf16[1,128,4096]{2,1,0:T(8,128)(2,1)S(1)}, bf16[1,128,4096]{2,1,0:T(8,128)(2,1)}, u32[]{:S(2)}) copy-start(bf16[1,128,4096]{2,1,0:T(8,128)(2,1)} %param.13) | copy-start | bytes 3145732
  33.3 19.0 %collective-permute-start.4 = (bf16[136,2048]{1,0:T(8,128)(2,1)S(1)}, bf16[136,2048]{1,0:T(8,128)(2,1)S(1)}, u32[]{:S(2)}, u32[]{:S(2)}) collective-permute-start(bf16[136,2048]{1,0:T(8,128)(2,1)S(1)} %copy-done.9), channel_id=1, source_target_pairs={{0,2},{2,4},{4,6},{6,8},{8,10},{10,12},{12,14},{14,16},{16,18},{18... | collective-permute-start | bytes 1671176 | tf_op jit(solution)/shard_map/ppermute | solution.py:26
  39.4 24.9 %collective-permute-start.3 = (bf16[136,2048]{1,0:T(8,128)(2,1)S(1)}, bf16[136,2048]{1,0:T(8,128)(2,1)S(1)}, u32[]{:S(2)}, u32[]{:S(2)}) collective-permute-start(bf16[136,2048]{1,0:T(8,128)(2,1)S(1)} %copy-done.8), channel_id=1, source_target_pairs={{0,2},{2,4},{4,6},{6,8},{8,10},{10,12},{12,14},{14,16},{16,18},{18... | collective-permute-start | bytes 1671176 | tf_op jit(solution)/shard_map/ppermute | solution.py:26
  41.3 3.9 %copy-start.2 = (f32[8,4096]{1,0:T(8,128)S(1)}, f32[8,4096]{1,0:T(8,128)}, u32[]{:S(2)}) copy-start(f32[8,4096]{1,0:T(8,128)} %get-tuple-element.50.taps) | copy-start | bytes 393220
  45.2 7.1 %copy-start = (bf16[1,2,128,4096]{3,2,1,0:T(8,128)(2,1)S(1)}, bf16[1,2,128,4096]{3,2,1,0:T(8,128)(2,1)}, u32[]{:S(2)}) copy-start(bf16[1,2,128,4096]{3,2,1,0:T(8,128)(2,1)} %slot.5) | copy-start | bytes 6291460
  45.2 7.1 %copy-start.6 = (s32[2]{0:T(128)S(1)}, s32[2]{0:T(128)}, u32[]{:S(2)}) copy-start(s32[2]{0:T(128)} %destinations.5) | copy-start | bytes 28
  56.0 19.6 %collective-permute-start.5 = (bf16[128,2048]{1,0:T(8,128)(2,1)S(1)}, bf16[128,2048]{1,0:T(8,128)(2,1)S(1)}, u32[]{:S(2)}, u32[]{:S(2)}) collective-permute-start(bf16[128,2048]{1,0:T(8,128)(2,1)S(1)} %get-tuple-element.56.mid), channel_id=1, source_target_pairs={{0,2},{2,4},{4,6},{6,8},{8,10},{10,12},{12,14},{14,16},{16,18},{18... | collective-permute-start | bytes 1572872 | tf_op jit(solution)/shard_map/ppermute | solution.py:26
  67.9 7.7 %copy-start.3 = (f32[256,128]{1,0:T(8,128)S(1)}, f32[256,128]{1,0:T(8,128)}, u32[]{:S(2)}) copy-start(f32[256,128]{1,0:T(8,128)} %get-tuple-element.60.mirrored) | copy-start | bytes 393220
  71.2 19.9 %collective-permute-start.9 = (bf16[128,2048]{1,0:T(8,128)(2,1)S(1)}, bf16[128,2048]{1,0:T(8,128)(2,1)S(1)}, u32[]{:S(2)}, u32[]{:S(2)}) collective-permute-start(bf16[128,2048]{1,0:T(8,128)(2,1)S(1)} %get-tuple-element.67.mid), channel_id=1, source_target_pairs={{0,2},{2,4},{4,6},{6,8},{8,10},{10,12},{12,14},{14,16},{16,18},{18... | collective-permute-start | bytes 1572872 | tf_op jit(solution)/shard_map/ppermute | solution.py:26
  79.4 10.9 %collective-permute-start.6 = (f32[272,128]{1,0:T(8,128)S(1)}, f32[272,128]{1,0:T(8,128)S(1)}, u32[]{:S(2)}, u32[]{:S(2)}) collective-permute-start(f32[272,128]{1,0:T(8,128)S(1)} %pad_maximum_fusion), channel_id=1, source_target_pairs={{0,16},{2,18},{4,20},{6,22},{8,24},{10,26},{12,28},{14,30},{16,0},... | collective-permute-start | bytes 417800 | tf_op jit(solution)/shard_map/ppermute | solution.py:31
  83.3 7.0 %collective-permute-start.7 = (bf16[8,4096]{1,0:T(8,128)(2,1)S(1)}, bf16[8,4096]{1,0:T(8,128)(2,1)S(1)}, u32[]{:S(2)}, u32[]{:S(2)}) collective-permute-start(bf16[8,4096]{1,0:T(8,128)(2,1)S(1)} %slice.12), channel_id=1, source_target_pairs={{2,0},{4,2},{6,4},{8,6},{10,8},{12,10},{14,12},{16,14},{18,16},{20... | collective-permute-start | bytes 196616 | tf_op jit(solution)/shard_map/ppermute | solution.py:26
  90.4 5.1 %collective-permute-start.8 = (f32[272,128]{1,0:T(8,128)S(1)}, f32[272,128]{1,0:T(8,128)S(1)}, u32[]{:S(2)}, u32[]{:S(2)}) collective-permute-start(f32[272,128]{1,0:T(8,128)S(1)} %add.15), channel_id=1, source_target_pairs={{0,8},{2,10},{4,12},{6,14},{8,0},{10,2},{12,4},{14,6},{16,24},{18,... | collective-permute-start | bytes 417800 | tf_op jit(solution)/shard_map/ppermute | solution.py:31
  95.5 9.6 %collective-permute-start.12 = (f32[272,128]{1,0:T(8,128)S(1)}, f32[272,128]{1,0:T(8,128)S(1)}, u32[]{:S(2)}, u32[]{:S(2)}) collective-permute-start(f32[272,128]{1,0:T(8,128)S(1)} %add.16), channel_id=1, source_target_pairs={{0,6},{2,4},{4,2},{6,0},{8,14},{10,12},{12,10},{14,8},{16,22},{18,... | collective-permute-start | bytes 417800 | tf_op jit(solution)/shard_map/ppermute | solution.py:31
  100.9 5.5 %collective-permute-start.11 = (f32[272,128]{1,0:T(8,128)S(1)}, f32[272,128]{1,0:T(8,128)S(1)}, u32[]{:S(2)}, u32[]{:S(2)}) collective-permute-start(f32[272,128]{1,0:T(8,128)S(1)} %add.16), channel_id=1, source_target_pairs={{0,4},{2,6},{4,0},{6,2},{8,12},{10,14},{12,8},{14,10},{16,20},{18,... | collective-permute-start | bytes 417800 | tf_op jit(solution)/shard_map/ppermute | solution.py:31
  100.9 5.5 %collective-permute-start.10 = (f32[272,128]{1,0:T(8,128)S(1)}, f32[272,128]{1,0:T(8,128)S(1)}, u32[]{:S(2)}, u32[]{:S(2)}) collective-permute-start(f32[272,128]{1,0:T(8,128)S(1)} %add.16), channel_id=1, source_target_pairs={{0,2},{2,0},{4,6},{6,4},{8,10},{10,8},{12,14},{14,12},{16,18},{18,... | collective-permute-start | bytes 417800 | tf_op jit(solution)/shard_map/ppermute | solution.py:31

commit v4 on v3

--- a/solution.py
+++ b/solution.py
@@ -501,13 +501,17 @@
     base = own_back(bounds, weighted, incoming, low)
 
     *outgoing, sent_tail = pick_outgoing(counts, destinations, loaded)
-    rim = from_behind(sent_tail, "ctx", 2)
+    shards = range(ctx_count - 2)
+    rim = lax.ppermute(sent_tail, "ctx", [(i, i + 2) for i in shards if i % 4 != 1])
+    rim_last = lax.ppermute(sent_tail, "ctx", [(i, i + 2) for i in shards if i % 4 == 1])
     after, rim, base, low, mirrored, taps_se, *outgoing = lax.optimization_barrier(
         (after, rim, base, low, mirrored, taps_se, *outgoing)
     )
     arrived = [from_behind(piece, "ctx", 1) for piece in outgoing]
 
     mid_grad, wse = next_back(bounds, after, base, gate_se, low)
+    mid_grad, rim, rim_last = lax.optimization_barrier((mid_grad, rim, rim_last))
+    rim = rim + rim_last
     grad_x = input_grad(bounds, mid_grad, wse, taps_se)
     arrived[0], grad_x = lax.optimization_barrier((arrived[0], grad_x))
 

time: 108 us -> 106 us (0.981)
  waiting for transfers between devices: 23.9 us -> 20.3 us
    ppermute x7 -> x6, starting transfers between devices: 26.6 us -> 18.7 us  [from_behind(): return lax.ppermute(block, axis, route)]
    ppermute x0 -> x2, starting transfers between devices: none -> 7.5 us  [the longest x1 6.83 us: body(): lax.ppermute(sent_tail, 'ctx', [(i, i + 2) for i in shards if i % 4 != 1])]
    ppermute x6, waiting for transfers between devices: 11.6 us -> 8.92 us  [partner(): return lax.ppermute(value, axis, pairs)]
    ppermute x6, starting transfers between devices: 11.2 us -> 12.4 us  [partner(): return lax.ppermute(value, axis, pairs)]
    ppermute x7 -> x6, waiting for transfers between devices: 12.3 us -> 11.4 us  [from_behind(): return lax.ppermute(block, axis, route)]
  transfers between devices with their start and end apart: 13 -> 14, of which waited for: 8 -> 7; matrix products, arithmetic and copies ran while one was open for 1% -> 1% of each run, Pallas kernels for 37% -> 38%
where the time goes in v4:
time: 106 us; the launch traced here: 105 us
  Pallas kernels  40 us (38%)
  starting transfers between devices  38.6 us (36%)
  waiting for transfers between devices  20.3 us (19%)
  local copies, waits for them, and re-layouts  3.02 us (3%)
  other arithmetic  1.57 us (1%)
  between operations  1.54 us (1%)
    ppermute x6, starting transfers between devices, from_behind(): return lax.ppermute(block, axis, route)  18.7 us
    ppermute x6, starting transfers between devices, partner(): return lax.ppermute(value, axis, pairs)  12.4 us
    ppermute x6, waiting for transfers between devices, from_behind(): return lax.ppermute(block, axis, route)  11.4 us
    ppermute x6, waiting for transfers between devices, partner(): return lax.ppermute(value, axis, pairs)  8.92 us
    pallas_call x2, Pallas kernels, gate_grad(): pl.pallas_call(gate_kernel, grid=(part // BLOCK,), in_specs=[SCALARS, own...  7.51 us
    pallas_call x2, Pallas kernels, middle(): pl.pallas_call(functools.partial(middle_kernel, piece * groups // PIECES...  7.37 us
    ppermute x1, starting transfers between devices, body(): lax.ppermute(sent_tail, 'ctx', [(i, i + 2) for i in shards if i % 4 != 1])  6.83 us
    pallas_call x2, Pallas kernels, lag_grads(): pl.pallas_call(lag_kernel, grid=(part // BLOCK,), in_specs=[SCALARS, pl.B...  6.54 us
  transfers between devices with their start and end apart: 14, of which 7 were waited for; matrix products, arithmetic and copies ran while one was open for 1% of the time, Pallas kernels for 38%

profile of v4, /device:TPU:0, one launch (start us, length us, event | category | flops | bytes accessed | tf_op | source)
XLA Modules:
  0.0 105.1 jit_solution(10078658886797961395)
XLA Ops:
  0.6 0.5 collective-permute-start
  1.1 2.5 %collective-permute-done.incoming = bf16[128,4096]{1,0:T(8,128)(2,1)S(1)} collective-permute-done((bf16[128,4096]{1,0:T(8,128)(2,1)}, bf16[128,4096]{1,0:T(8,128)(2,1)S(1)}, u32[]{:S(2)}, u32[]{:S(2)}) %collective-permute-start) | collective-permute-done | bytes 1048608 | tf_op jit(solution)/shard_map/ppermute | solution.py:31
  3.6 1.5 %fusion.weighted = bf16[128,4096]{1,0:T(8,128)(2,1)S(1)} fusion(bf16[128,4096]{1,0:T(8,128)(2,1)S(1)} %collective-permute-done.incoming, bf16[1,128,4096]{2,1,0:T(8,128)(2,1)} %param.14), kind=kLoop, calls=%fused_computation.1 | loop fusion | flops 2097152 | bytes 3145728 | tf_op jit(solution)/shard_map/convert_element_type | solution.py:498
  5.1 1.3 %collective-permute-start.1 = (bf16[128,4096]{1,0:T(8,128)(2,1)S(1)}, bf16[128,4096]{1,0:T(8,128)(2,1)S(1)}, u32[]{:S(2)}, u32[]{:S(2)}) collective-permute-start(bf16[128,4096]{1,0:T(8,128)(2,1)S(1)} %fusion.weighted), channel_id=1, source_target_pairs={{2,0},{4,2},{6,4},{8,6},{10,8},{12,10},{14,12},{16,14},{18,16},{20... | collective-permute-start | bytes 3145736 | tf_op jit(solution)/shard_map/ppermute | solution.py:26
  7.1 0.0 copy-start.7
  7.1 0.0 copy-start.5
  7.1 3.1 %shard_map.128 = (bf16[136,2048]{1,0:T(8,128)(2,1)}, bf16[136,2048]{1,0:T(8,128)(2,1)}, bf16[8,4096]{1,0:T(8,128)(2,1)}) custom-call(s32[1]{0:T(128)S(6)} %copy.23.counts, s32[2]{0:T(128)} %destinations.5, bf16[1,2,128,4096]{3,2,1,0:T(8,128)(2,1)} %slot.5, bf16[1,2,128,4096]{3,2,1,0:T(8,128)(2,1)} %slot.5), custom_call_target="tpu_custom_call" | custom-call | flops 1 | bytes 1 | tf_op jit(solution)/shard_map/pallas_call | solution.py:108
  10.2 6.8 %collective-permute-start.2 = (bf16[8,4096]{1,0:T(8,128)(2,1)}, bf16[8,4096]{1,0:T(8,128)(2,1)S(1)}, u32[]{:S(2)}, u32[]{:S(2)}) collective-permute-start(bf16[8,4096]{1,0:T(8,128)(2,1)} %get-tuple-element.41), channel_id=1, source_target_pairs={{0,4},{4,8},{6,10},{8,12},{12,16},{14,18},{16,20},{20,24},{22,26},... | collective-permute-start | bytes 196616 | tf_op jit(solution)/shard_map/ppermute | solution.py:505
  17.1 0.8 copy.18
  17.9 2.1 %shard_map.129 = (f32[256,128]{1,0:T(8,128)}, f32[256,128]{1,0:T(8,128)}, f32[8,4096]{1,0:T(8,128)}) custom-call(f32[256,128]{1,0:T(8,128)} %bitcast.28, f32[256,7]{1,0:T(8,128)} %bitcast.27), custom_call_target="tpu_custom_call" | custom-call | flops 1 | bytes 1 | tf_op jit(solution)/shard_map/pallas_call | solution.py:145
  20.0 0.9 copy-done.4
  20.9 3.5 %shard_map.130.base = f32[128,4096]{1,0:T(8,128)S(1)} custom-call(s32[16]{0:T(128)S(1)} %copy-done.5, bf16[128,4096]{1,0:T(8,128)(2,1)S(1)} %fusion.weighted, bf16[128,4096]{1,0:T(8,128)(2,1)S(1)} %collective-permute-done.incoming, f32[256,128]{1,0:T(8,128)S(1)} %copy-done.4), custom_call_target="tpu_custom_call" | custom-call | flops 1 | bytes 1 | tf_op jit(solution)/shard_map/pallas_call | solution.py:186
  24.4 0.0 collective-permute-done.2
  24.4 9.0 %collective-permute-done.1.after = bf16[128,4096]{1,0:T(8,128)(2,1)S(1)} collective-permute-done((bf16[128,4096]{1,0:T(8,128)(2,1)S(1)}, bf16[128,4096]{1,0:T(8,128)(2,1)S(1)}, u32[]{:S(2)}, u32[]{:S(2)}) %collective-permute-start.1) | collective-permute-done | bytes 1048608 | tf_op jit(solution)/shard_map/ppermute | solution.py:26
  33.3 4.6 %collective-permute-start.5 = (bf16[136,2048]{1,0:T(8,128)(2,1)S(1)}, bf16[136,2048]{1,0:T(8,128)(2,1)S(1)}, u32[]{:S(2)}, u32[]{:S(2)}) collective-permute-start(bf16[136,2048]{1,0:T(8,128)(2,1)S(1)} %copy-done.9), channel_id=1, source_target_pairs={{0,2},{2,4},{4,6},{6,8},{8,10},{10,12},{12,14},{14,16},{16,18},{18... | collective-permute-start | bytes 1671176 | tf_op jit(solution)/shard_map/ppermute | solution.py:26
  37.9 2.5 %collective-permute-start.4 = (bf16[136,2048]{1,0:T(8,128)(2,1)S(1)}, bf16[136,2048]{1,0:T(8,128)(2,1)S(1)}, u32[]{:S(2)}, u32[]{:S(2)}) collective-permute-start(bf16[136,2048]{1,0:T(8,128)(2,1)S(1)} %copy-done.8), channel_id=1, source_target_pairs={{0,2},{2,4},{4,6},{6,8},{8,10},{10,12},{12,14},{14,16},{16,18},{18... | collective-permute-start | bytes 1671176 | tf_op jit(solution)/shard_map/ppermute | solution.py:26
  40.4 0.7 collective-permute-start.3
  41.1 3.9 %shard_map.131 = (bf16[128,4096]{1,0:T(8,128)(2,1)S(1)}, bf16[128,4096]{1,0:T(8,128)(2,1)S(1)}) custom-call(s32[16]{0:T(128)S(1)} %copy-done.5, bf16[128,4096]{1,0:T(8,128)(2,1)S(1)} %collective-permute-done.1.after, f32[128,4096]{1,0:T(8,128)S(1)} %shard_map.130.base, bf16[128,4096]{1,0:T(8,128)(2,1)S(1)} %bitcast.21, f32[256,128]{1,0:T(8,128)S(1)} %copy-done.4), custom_call_target="tpu_custom_call" | custom-call | flops 1 | bytes 1 | tf_op jit(solution)/shard_map/pallas_call | solution.py:221
  45.0 0.0 copy-start
  45.0 0.0 copy-start.6
  45.0 4.2 %shard_map.132.held = bf16[128,4096]{1,0:T(8,128)(2,1)} custom-call(s32[16]{0:T(128)S(1)} %copy-done.5, bf16[128,4096]{1,0:T(8,128)(2,1)S(1)} %get-tuple-element.52.grad, bf16[128,4096]{1,0:T(8,128)(2,1)S(1)} %get-tuple-element.67.wse, f32[8,4096]{1,0:T(8,128)S(1)} %copy-done.2), custom_call_target="tpu_custom_call" | custom-call | flops 1 | bytes 1 | tf_op jit(solution)/shard_map/pallas_call | solution.py:399
  49.2 1.7 %collective-permute-done.5.arrived = bf16[136,2048]{1,0:T(8,128)(2,1)S(1)} collective-permute-done((bf16[136,2048]{1,0:T(8,128)(2,1)S(1)}, bf16[136,2048]{1,0:T(8,128)(2,1)S(1)}, u32[]{:S(2)}, u32[]{:S(2)}) %collective-permute-start.5) | collective-permute-done | bytes 557088 | tf_op jit(solution)/shard_map/ppermute | solution.py:26
  51.0 3.7 %shard_map.133 = (bf16[128,2048]{1,0:T(8,128)(2,1)S(1)}, bf16[128,4096]{1,0:T(8,128)(2,1)}, f32[8,128]{1,0:T(8,128)S(1)}) custom-call(s32[16]{0:T(128)S(1)} %copy-done.5, s32[1]{0:T(128)S(6)} %copy.23.counts, s32[2]{0:T(128)S(1)} %copy-done.6, bf16[1,2,128,4096]{3,2,1,0:T(8,128)(2,1)S(1)} %copy-done, bf16[136,2048]{1,0:T(8,128)(2,1)S(1)} %collective-permute-done.5.arrived, ...), custom_call_target="tpu_custom_call" | custom-call | flops 1 | bytes 1 | tf_op jit(solution)/shard_map/pallas_call | solution.py:292
  54.6 6.9 %collective-permute-start.6 = (bf16[128,2048]{1,0:T(8,128)(2,1)S(1)}, bf16[128,2048]{1,0:T(8,128)(2,1)S(1)}, u32[]{:S(2)}, u32[]{:S(2)}) collective-permute-start(bf16[128,2048]{1,0:T(8,128)(2,1)S(1)} %get-tuple-element.62.mid), channel_id=1, source_target_pairs={{0,2},{2,4},{4,6},{6,8},{8,10},{10,12},{12,14},{14,16},{16,18},{18... | collective-permute-start | bytes 1572872 | tf_op jit(solution)/shard_map/ppermute | solution.py:26
  61.6 3.3 %shard_map.135.rest_0_ = f32[256,128]{1,0:T(8,128)S(1)} custom-call(s32[16]{0:T(128)S(1)} %copy-done.5, bf16[128,2048]{1,0:T(8,128)(2,1)S(1)} %get-tuple-element.62.mid, bf16[128,4096]{1,0:T(8,128)(2,1)S(1)} %fusion.weighted, bf16[128,4096]{1,0:T(8,128)(2,1)S(1)} %collective-permute-done.1.after), custom_call_target="tpu_custom_call" | custom-call | flops 1 | bytes 1 | tf_op jit(solution)/shard_map/pallas_call | solution.py:361
  64.9 0.0 collective-permute-done.4.arrived
  64.9 3.7 %shard_map.134 = (bf16[128,2048]{1,0:T(8,128)(2,1)S(1)}, bf16[128,4096]{1,0:T(8,128)(2,1)}, f32[8,128]{1,0:T(8,128)S(1)}) custom-call(s32[16]{0:T(128)S(1)} %copy-done.5, s32[1]{0:T(128)S(6)} %copy.23.counts, s32[2]{0:T(128)S(1)} %copy-done.6, bf16[1,2,128,4096]{3,2,1,0:T(8,128)(2,1)S(1)} %copy-done, ...), custom_call_target="tpu_custom_call", output_to_operand_aliasing={{1}: (10, {})} | custom-call | flops 1 | bytes 1 | tf_op jit(solution)/shard_map/pallas_call | solution.py:292
  68.6 3.3 %shard_map.136 = f32[256,128]{1,0:T(8,128)S(1)} custom-call(s32[16]{0:T(128)S(1)} %copy-done.5, bf16[128,2048]{1,0:T(8,128)(2,1)S(1)} %get-tuple-element.73.mid, bf16[128,4096]{1,0:T(8,128)(2,1)S(1)} %fusion.weighted, bf16[128,4096]{1,0:T(8,128)(2,1)S(1)} %collective-permute-done.1.after, ...), custom_call_target="tpu_custom_call", output_to_operand_aliasing={{}: (4, {})} | custom-call | flops 1 | bytes 1 | tf_op jit(solution)/shard_map/pallas_call | solution.py:361
  71.9 1.9 %collective-permute-start.10 = (bf16[128,2048]{1,0:T(8,128)(2,1)S(1)}, bf16[128,2048]{1,0:T(8,128)(2,1)S(1)}, u32[]{:S(2)}, u32[]{:S(2)}) collective-permute-start(bf16[128,2048]{1,0:T(8,128)(2,1)S(1)} %get-tuple-element.73.mid), channel_id=1, source_target_pairs={{0,2},{2,4},{4,6},{6,8},{8,10},{10,12},{12,14},{14,16},{16,18},{18... | collective-permute-start | bytes 1572872 | tf_op jit(solution)/shard_map/ppermute | solution.py:26
  73.8 0.0 collective-permute-done.6.prior
  73.8 3.7 %shard_map.137.rest_0_ = bf16[128,4096]{1,0:T(8,128)(2,1)} custom-call(s32[16]{0:T(128)S(1)} %copy-done.5, bf16[128,2048]{1,0:T(8,128)(2,1)S(1)} %collective-permute-done.6.prior, bf16[128,2048]{1,0:T(8,128)(2,1)S(1)} %get-tuple-element.62.mid, bf16[128,4096]{1,0:T(8,128)(2,1)S(1)} %collective-permute-done.incoming, f32[256,128]{1,0:T(8,128)S(1)} %copy-done.3), custom_call_target="tpu_custom_call" | custom-call | flops 1 | bytes 1 | tf_op jit(solution)/shard_map/pallas_call | solution.py:477
  77.6 4.5 %collective-permute-start.7 = (f32[272,128]{1,0:T(8,128)S(1)}, f32[272,128]{1,0:T(8,128)S(1)}, u32[]{:S(2)}, u32[]{:S(2)}) collective-permute-start(f32[272,128]{1,0:T(8,128)S(1)} %pad_maximum_fusion), channel_id=1, source_target_pairs={{0,16},{2,18},{4,20},{6,22},{8,24},{10,26},{12,28},{14,30},{16,0},... | collective-permute-start | bytes 417800 | tf_op jit(solution)/shard_map/ppermute | solution.py:31
  82.0 1.5 %collective-permute-start.8 = (bf16[8,4096]{1,0:T(8,128)(2,1)S(1)}, bf16[8,4096]{1,0:T(8,128)(2,1)S(1)}, u32[]{:S(2)}, u32[]{:S(2)}) collective-permute-start(bf16[8,4096]{1,0:T(8,128)(2,1)S(1)} %slice.12), channel_id=1, source_target_pairs={{2,0},{4,2},{6,4},{8,6},{10,8},{12,10},{14,12},{16,14},{18,16},{20... | collective-permute-start | bytes 196616 | tf_op jit(solution)/shard_map/ppermute | solution.py:26
  83.5 3.9 %collective-permute-done.7 = f32[272,128]{1,0:T(8,128)S(1)} collective-permute-done((f32[272,128]{1,0:T(8,128)S(1)}, f32[272,128]{1,0:T(8,128)S(1)}, u32[]{:S(2)}, u32[]{:S(2)}) %collective-permute-start.7) | collective-permute-done | bytes 139296 | tf_op jit(solution)/shard_map/ppermute | solution.py:31
  87.5 0.7 collective-permute-done.8.rim
  88.2 1.8 %collective-permute-start.9 = (f32[272,128]{1,0:T(8,128)S(1)}, f32[272,128]{1,0:T(8,128)S(1)}, u32[]{:S(2)}, u32[]{:S(2)}) collective-permute-start(f32[272,128]{1,0:T(8,128)S(1)} %add.19), channel_id=1, source_target_pairs={{0,8},{2,10},{4,12},{6,14},{8,0},{10,2},{12,4},{14,6},{16,24},{18,... | collective-permute-start | bytes 417800 | tf_op jit(solution)/shard_map/ppermute | solution.py:31
  90.0 0.0 collective-permute-done.10.prior
  90.0 3.8 %shard_map.139 = bf16[128,4096]{1,0:T(8,128)(2,1)} custom-call(s32[16]{0:T(128)S(1)} %copy-done.5, bf16[128,2048]{1,0:T(8,128)(2,1)S(1)} %collective-permute-done.10.prior, bf16[128,2048]{1,0:T(8,128)(2,1)S(1)} %get-tuple-element.73.mid, bf16[128,4096]{1,0:T(8,128)(2,1)S(1)} %collective-permute-done.incoming, ...), custom_call_target="tpu_custom_call", output_to_operand_aliasing={{}: (5, {})} | custom-call | flops 1 | bytes 1 | tf_op jit(solution)/shard_map/pallas_call | solution.py:477
  93.7 0.0 collective-permute-done.9
  93.8 4.9 %collective-permute-start.13 = (f32[272,128]{1,0:T(8,128)S(1)}, f32[272,128]{1,0:T(8,128)S(1)}, u32[]{:S(2)}, u32[]{:S(2)}) collective-permute-start(f32[272,128]{1,0:T(8,128)S(1)} %add.20), channel_id=1, source_target_pairs={{0,6},{2,4},{4,2},{6,0},{8,14},{10,12},{12,10},{14,8},{16,22},{18,... | collective-permute-start | bytes 417800 | tf_op jit(solution)/shard_map/ppermute | solution.py:31
  98.7 0.0 collective-permute-start.12
  98.7 0.6 collective-permute-start.11
  99.4 1.9 %shard_map.138 = bf16[128,4096]{1,0:T(8,128)(2,1)} custom-call(s32[16]{0:T(128)S(1)} %copy-done.5, bf16[128,4096]{1,0:T(8,128)(2,1)S(1)} %get-tuple-element.52.grad, bf16[128,4096]{1,0:T(8,128)(2,1)S(1)} %get-tuple-element.67.wse, bf16[8,4096]{1,0:T(8,128)(2,1)S(1)} %collective-permute-done.8.rim, ...), custom_call_target="tpu_custom_call", output_to_operand_aliasing={{}: (5, {})} | custom-call | flops 1 | bytes 1 | tf_op jit(solution)/shard_map/pallas_call | solution.py:436
  101.2 0.5 collective-permute-done.13
  101.8 2.0 %collective-permute-done.12 = f32[272,128]{1,0:T(8,128)S(1)} collective-permute-done((f32[272,128]{1,0:T(8,128)S(1)}, f32[272,128]{1,0:T(8,128)S(1)}, u32[]{:S(2)}, u32[]{:S(2)}) %collective-permute-start.12) | collective-permute-done | bytes 139296 | tf_op jit(solution)/shard_map/ppermute | solution.py:31
  103.8 0.0 collective-permute-done.11
  103.8 0.7 slice_bitcast_fusion
  104.5 0.6 broadcast_in_dim.18
  (25 shorter events, 0.1 us)
Async XLA Ops:
  0.6 3.0 %collective-permute-start = (bf16[128,4096]{1,0:T(8,128)(2,1)}, bf16[128,4096]{1,0:T(8,128)(2,1)S(1)}, u32[]{:S(2)}, u32[]{:S(2)}) collective-permute-start(bf16[128,4096]{1,0:T(8,128)(2,1)} %bitcast.30), channel_id=1, source_target_pairs={{0,1},{1,0},{2,3},{3,2},{4,5},{5,4},{6,7},{7,6},{8,9},{9,8},{10,11... | collective-permute-start | bytes 3145736 | tf_op jit(solution)/shard_map/ppermute | solution.py:31
  5.1 28.2 %collective-permute-start.1 = (bf16[128,4096]{1,0:T(8,128)(2,1)S(1)}, bf16[128,4096]{1,0:T(8,128)(2,1)S(1)}, u32[]{:S(2)}, u32[]{:S(2)}) collective-permute-start(bf16[128,4096]{1,0:T(8,128)(2,1)S(1)} %fusion.weighted), channel_id=1, source_target_pairs={{2,0},{4,2},{6,4},{8,6},{10,8},{12,10},{14,12},{16,14},{18,16},{20... | collective-permute-start | bytes 3145736 | tf_op jit(solution)/shard_map/ppermute | solution.py:26
  7.1 10.0 %copy-start.7 = (f32[1,256,7]{1,0,2:T(1,128)S(1)}, f32[1,256,7]{1,0,2:T(1,128)}, u32[]{:S(2)}) copy-start(f32[1,256,7]{1,0,2:T(1,128)} %param.16) | copy-start | bytes 21508
  7.1 12.9 %copy-start.5 = (s32[16]{0:T(128)S(1)}, s32[16]{0:T(128)}, u32[]{:S(2)}) copy-start(s32[16]{0:T(128)} %bounds.19) | copy-start | bytes 196
  10.2 14.2 %collective-permute-start.2 = (bf16[8,4096]{1,0:T(8,128)(2,1)}, bf16[8,4096]{1,0:T(8,128)(2,1)S(1)}, u32[]{:S(2)}, u32[]{:S(2)}) collective-permute-start(bf16[8,4096]{1,0:T(8,128)(2,1)} %get-tuple-element.41), channel_id=1, source_target_pairs={{0,4},{4,8},{6,10},{8,12},{12,16},{14,18},{16,20},{20,24},{22,26},... | collective-permute-start | bytes 196616 | tf_op jit(solution)/shard_map/ppermute | solution.py:505
  20.0 0.9 copy-start.4
  20.9 12.5 %copy-start.9 = (bf16[136,2048]{1,0:T(8,128)(2,1)S(1)}, bf16[136,2048]{1,0:T(8,128)(2,1)}, u32[]{:S(2)}) copy-start(bf16[136,2048]{1,0:T(8,128)(2,1)} %get-tuple-element.58) | copy-start | bytes 1671172
  20.9 17.1 %copy-start.8 = (bf16[136,2048]{1,0:T(8,128)(2,1)S(1)}, bf16[136,2048]{1,0:T(8,128)(2,1)}, u32[]{:S(2)}) copy-start(bf16[136,2048]{1,0:T(8,128)(2,1)} %get-tuple-element.53) | copy-start | bytes 1671172
  20.9 19.6 %copy-start.10 = (bf16[8,4096]{1,0:T(8,128)(2,1)S(1)}, bf16[8,4096]{1,0:T(8,128)(2,1)}, u32[]{:S(2)}) copy-start(bf16[8,4096]{1,0:T(8,128)(2,1)} %get-tuple-element.41) | copy-start | bytes 196612
  20.9 20.3 %copy-start.1 = (bf16[1,128,4096]{2,1,0:T(8,128)(2,1)S(1)}, bf16[1,128,4096]{2,1,0:T(8,128)(2,1)}, u32[]{:S(2)}) copy-start(bf16[1,128,4096]{2,1,0:T(8,128)(2,1)} %param.13) | copy-start | bytes 3145732
  33.3 17.6 %collective-permute-start.5 = (bf16[136,2048]{1,0:T(8,128)(2,1)S(1)}, bf16[136,2048]{1,0:T(8,128)(2,1)S(1)}, u32[]{:S(2)}, u32[]{:S(2)}) collective-permute-start(bf16[136,2048]{1,0:T(8,128)(2,1)S(1)} %copy-done.9), channel_id=1, source_target_pairs={{0,2},{2,4},{4,6},{6,8},{8,10},{10,12},{12,14},{14,16},{16,18},{18... | collective-permute-start | bytes 1671176 | tf_op jit(solution)/shard_map/ppermute | solution.py:26
  37.9 26.9 %collective-permute-start.4 = (bf16[136,2048]{1,0:T(8,128)(2,1)S(1)}, bf16[136,2048]{1,0:T(8,128)(2,1)S(1)}, u32[]{:S(2)}, u32[]{:S(2)}) collective-permute-start(bf16[136,2048]{1,0:T(8,128)(2,1)S(1)} %copy-done.8), channel_id=1, source_target_pairs={{0,2},{2,4},{4,6},{6,8},{8,10},{10,12},{12,14},{14,16},{16,18},{18... | collective-permute-start | bytes 1671176 | tf_op jit(solution)/shard_map/ppermute | solution.py:26
  40.4 4.6 %collective-permute-start.3 = (bf16[8,4096]{1,0:T(8,128)(2,1)S(1)}, bf16[8,4096]{1,0:T(8,128)(2,1)S(1)}, u32[]{:S(2)}, u32[]{:S(2)}) collective-permute-start(bf16[8,4096]{1,0:T(8,128)(2,1)S(1)} %copy-done.10), channel_id=1, source_target_pairs={{2,6},{10,14},{18,22},{26,30},{3,7},{11,15},{19,23},{27,31}} | collective-permute-start | bytes 196616 | tf_op jit(solution)/shard_map/ppermute | solution.py:506
  41.1 3.9 %copy-start.2 = (f32[8,4096]{1,0:T(8,128)S(1)}, f32[8,4096]{1,0:T(8,128)}, u32[]{:S(2)}) copy-start(f32[8,4096]{1,0:T(8,128)} %get-tuple-element.56.taps) | copy-start | bytes 393220
  45.0 5.9 %copy-start = (bf16[1,2,128,4096]{3,2,1,0:T(8,128)(2,1)S(1)}, bf16[1,2,128,4096]{3,2,1,0:T(8,128)(2,1)}, u32[]{:S(2)}) copy-start(bf16[1,2,128,4096]{3,2,1,0:T(8,128)(2,1)} %slot.5) | copy-start | bytes 6291460
  45.0 5.9 %copy-start.6 = (s32[2]{0:T(128)S(1)}, s32[2]{0:T(128)}, u32[]{:S(2)}) copy-start(s32[2]{0:T(128)} %destinations.5) | copy-start | bytes 28
  54.6 19.1 %collective-permute-start.6 = (bf16[128,2048]{1,0:T(8,128)(2,1)S(1)}, bf16[128,2048]{1,0:T(8,128)(2,1)S(1)}, u32[]{:S(2)}, u32[]{:S(2)}) collective-permute-start(bf16[128,2048]{1,0:T(8,128)(2,1)S(1)} %get-tuple-element.62.mid), channel_id=1, source_target_pairs={{0,2},{2,4},{4,6},{6,8},{8,10},{10,12},{12,14},{14,16},{16,18},{18... | collective-permute-start | bytes 1572872 | tf_op jit(solution)/shard_map/ppermute | solution.py:26
  68.6 5.2 %copy-start.3 = (f32[256,128]{1,0:T(8,128)S(1)}, f32[256,128]{1,0:T(8,128)}, u32[]{:S(2)}) copy-start(f32[256,128]{1,0:T(8,128)} %get-tuple-element.66.mirrored) | copy-start | bytes 393220
  71.9 18.1 %collective-permute-start.10 = (bf16[128,2048]{1,0:T(8,128)(2,1)S(1)}, bf16[128,2048]{1,0:T(8,128)(2,1)S(1)}, u32[]{:S(2)}, u32[]{:S(2)}) collective-permute-start(bf16[128,2048]{1,0:T(8,128)(2,1)S(1)} %get-tuple-element.73.mid), channel_id=1, source_target_pairs={{0,2},{2,4},{4,6},{6,8},{8,10},{10,12},{12,14},{14,16},{16,18},{18... | collective-permute-start | bytes 1572872 | tf_op jit(solution)/shard_map/ppermute | solution.py:26
  77.6 9.9 %collective-permute-start.7 = (f32[272,128]{1,0:T(8,128)S(1)}, f32[272,128]{1,0:T(8,128)S(1)}, u32[]{:S(2)}, u32[]{:S(2)}) collective-permute-start(f32[272,128]{1,0:T(8,128)S(1)} %pad_maximum_fusion), channel_id=1, source_target_pairs={{0,16},{2,18},{4,20},{6,22},{8,24},{10,26},{12,28},{14,30},{16,0},... | collective-permute-start | bytes 417800 | tf_op jit(solution)/shard_map/ppermute | solution.py:31
  82.0 6.1 %collective-permute-start.8 = (bf16[8,4096]{1,0:T(8,128)(2,1)S(1)}, bf16[8,4096]{1,0:T(8,128)(2,1)S(1)}, u32[]{:S(2)}, u32[]{:S(2)}) collective-permute-start(bf16[8,4096]{1,0:T(8,128)(2,1)S(1)} %slice.12), channel_id=1, source_target_pairs={{2,0},{4,2},{6,4},{8,6},{10,8},{12,10},{14,12},{16,14},{18,16},{20... | collective-permute-start | bytes 196616 | tf_op jit(solution)/shard_map/ppermute | solution.py:26
  88.2 5.6 %collective-permute-start.9 = (f32[272,128]{1,0:T(8,128)S(1)}, f32[272,128]{1,0:T(8,128)S(1)}, u32[]{:S(2)}, u32[]{:S(2)}) collective-permute-start(f32[272,128]{1,0:T(8,128)S(1)} %add.19), channel_id=1, source_target_pairs={{0,8},{2,10},{4,12},{6,14},{8,0},{10,2},{12,4},{14,6},{16,24},{18,... | collective-permute-start | bytes 417800 | tf_op jit(solution)/shard_map/ppermute | solution.py:31
  93.8 8.0 %collective-permute-start.13 = (f32[272,128]{1,0:T(8,128)S(1)}, f32[272,128]{1,0:T(8,128)S(1)}, u32[]{:S(2)}, u32[]{:S(2)}) collective-permute-start(f32[272,128]{1,0:T(8,128)S(1)} %add.20), channel_id=1, source_target_pairs={{0,6},{2,4},{4,2},{6,0},{8,14},{10,12},{12,10},{14,8},{16,22},{18,... | collective-permute-start | bytes 417800 | tf_op jit(solution)/shard_map/ppermute | solution.py:31
  98.7 5.1 %collective-permute-start.12 = (f32[272,128]{1,0:T(8,128)S(1)}, f32[272,128]{1,0:T(8,128)S(1)}, u32[]{:S(2)}, u32[]{:S(2)}) collective-permute-start(f32[272,128]{1,0:T(8,128)S(1)} %add.20), channel_id=1, source_target_pairs={{0,4},{2,6},{4,0},{6,2},{8,12},{10,14},{12,8},{14,10},{16,20},{18,... | collective-permute-start | bytes 417800 | tf_op jit(solution)/shard_map/ppermute | solution.py:31
  98.7 5.1 %collective-permute-start.11 = (f32[272,128]{1,0:T(8,128)S(1)}, f32[272,128]{1,0:T(8,128)S(1)}, u32[]{:S(2)}, u32[]{:S(2)}) collective-permute-start(f32[272,128]{1,0:T(8,128)S(1)} %add.20), channel_id=1, source_target_pairs={{0,2},{2,0},{4,6},{6,4},{8,10},{10,8},{12,14},{14,12},{16,18},{18,... | collective-permute-start | bytes 417800 | tf_op jit(solution)/shard_map/ppermute | solution.py:31

commit v5 on v4

--- a/solution.py
+++ b/solution.py
@@ -542,14 +542,14 @@
     while mask > 2:
         total = total + partner(total, "ctx", mask)
         if mask == 4:
-            for q in range(1, PIECES):
-                grad_gate_mr = (gate_grad(q, bounds, prior[q], mid[q], incoming, mirrored, tuple(grad_gate_mr)),)
-            total, *grad_gate_mr = lax.optimization_barrier((total, *grad_gate_mr))
+            grad_x = rim_grad(bounds, mid_grad, wse, rim_next, taps_se, grad_x)
+            total, grad_x, *prior[1:] = lax.optimization_barrier((total, grad_x, *prior[1:]))
         else:
             total, rim_next = lax.optimization_barrier((total, rim_next))
         mask //= 2
     one, two, three = (partner(total, "ctx", mask) for mask in (1, 2, 3))
-    grad_x = rim_grad(bounds, mid_grad, wse, rim_next, taps_se, grad_x)
+    for q in range(1, PIECES):
+        grad_gate_mr = (gate_grad(q, bounds, prior[q], mid[q], incoming, mirrored, tuple(grad_gate_mr)),)
     total = (total + one) + (two + three)
 
     scale = 1.0 / math.sqrt(ctx_count * rows * GROUP)

time: 106 us -> 105 us (level)
  no operation moved by 1% of the time
where the time goes in v5:
time: 105 us; the launch traced here: 104 us
  Pallas kernels  40 us (38%)
  starting transfers between devices  38.4 us (37%)
  waiting for transfers between devices  19.8 us (19%)
  local copies, waits for them, and re-layouts  3.03 us (3%)
  other arithmetic  1.57 us (1%)
  between operations  1.54 us (1%)
    ppermute x6, starting transfers between devices, from_behind(): return lax.ppermute(block, axis, route)  18.7 us
    ppermute x6, starting transfers between devices, partner(): return lax.ppermute(value, axis, pairs)  12.2 us
    ppermute x6, waiting for transfers between devices, from_behind(): return lax.ppermute(block, axis, route)  11.4 us
    ppermute x6, waiting for transfers between devices, partner(): return lax.ppermute(value, axis, pairs)  8.42 us
    pallas_call x2, Pallas kernels, gate_grad(): pl.pallas_call(gate_kernel, grid=(part // BLOCK,), in_specs=[SCALARS, own...  7.5 us
    pallas_call x2, Pallas kernels, middle(): pl.pallas_call(functools.partial(middle_kernel, piece * groups // PIECES...  7.37 us
    ppermute x1, starting transfers between devices, body(): lax.ppermute(sent_tail, 'ctx', [(i, i + 2) for i in shards if i % 4 != 1])  6.83 us
    pallas_call x2, Pallas kernels, lag_grads(): pl.pallas_call(lag_kernel, grid=(part // BLOCK,), in_specs=[SCALARS, pl.B...  6.54 us
  transfers between devices with their start and end apart: 14, of which 7 were waited for; matrix products, arithmetic and copies ran while one was open for 1% of the time, Pallas kernels for 38%

profile of v5, /device:TPU:0, one launch (start us, length us, event | category | flops | bytes accessed | tf_op | source)
XLA Modules:
  0.0 104.4 jit_solution(8258479151443239033)
XLA Ops:
  0.6 0.5 collective-permute-start
  1.1 2.5 %collective-permute-done.incoming = bf16[128,4096]{1,0:T(8,128)(2,1)S(1)} collective-permute-done((bf16[128,4096]{1,0:T(8,128)(2,1)}, bf16[128,4096]{1,0:T(8,128)(2,1)S(1)}, u32[]{:S(2)}, u32[]{:S(2)}) %collective-permute-start) | collective-permute-done | bytes 1048608 | tf_op jit(solution)/shard_map/ppermute | solution.py:31
  3.6 1.5 %fusion.weighted = bf16[128,4096]{1,0:T(8,128)(2,1)S(1)} fusion(bf16[128,4096]{1,0:T(8,128)(2,1)S(1)} %collective-permute-done.incoming, bf16[1,128,4096]{2,1,0:T(8,128)(2,1)} %param.14), kind=kLoop, calls=%fused_computation.1 | loop fusion | flops 2097152 | bytes 3145728 | tf_op jit(solution)/shard_map/convert_element_type | solution.py:498
  5.1 1.3 %collective-permute-start.1 = (bf16[128,4096]{1,0:T(8,128)(2,1)S(1)}, bf16[128,4096]{1,0:T(8,128)(2,1)S(1)}, u32[]{:S(2)}, u32[]{:S(2)}) collective-permute-start(bf16[128,4096]{1,0:T(8,128)(2,1)S(1)} %fusion.weighted), channel_id=1, source_target_pairs={{2,0},{4,2},{6,4},{8,6},{10,8},{12,10},{14,12},{16,14},{18,16},{20... | collective-permute-start | bytes 3145736 | tf_op jit(solution)/shard_map/ppermute | solution.py:26
  7.1 0.0 copy-start.7
  7.1 0.0 copy-start.5
  7.1 3.1 %shard_map.128 = (bf16[136,2048]{1,0:T(8,128)(2,1)}, bf16[136,2048]{1,0:T(8,128)(2,1)}, bf16[8,4096]{1,0:T(8,128)(2,1)}) custom-call(s32[1]{0:T(128)S(6)} %copy.23.counts, s32[2]{0:T(128)} %destinations.5, bf16[1,2,128,4096]{3,2,1,0:T(8,128)(2,1)} %slot.5, bf16[1,2,128,4096]{3,2,1,0:T(8,128)(2,1)} %slot.5), custom_call_target="tpu_custom_call" | custom-call | flops 1 | bytes 1 | tf_op jit(solution)/shard_map/pallas_call | solution.py:108
  10.2 6.8 %collective-permute-start.2 = (bf16[8,4096]{1,0:T(8,128)(2,1)}, bf16[8,4096]{1,0:T(8,128)(2,1)S(1)}, u32[]{:S(2)}, u32[]{:S(2)}) collective-permute-start(bf16[8,4096]{1,0:T(8,128)(2,1)} %get-tuple-element.42), channel_id=1, source_target_pairs={{0,4},{4,8},{6,10},{8,12},{12,16},{14,18},{16,20},{20,24},{22,26},... | collective-permute-start | bytes 196616 | tf_op jit(solution)/shard_map/ppermute | solution.py:505
  17.1 0.8 copy.18
  17.9 2.1 %shard_map.129 = (f32[256,128]{1,0:T(8,128)}, f32[256,128]{1,0:T(8,128)}, f32[8,4096]{1,0:T(8,128)}) custom-call(f32[256,128]{1,0:T(8,128)} %bitcast.28, f32[256,7]{1,0:T(8,128)} %bitcast.27), custom_call_target="tpu_custom_call" | custom-call | flops 1 | bytes 1 | tf_op jit(solution)/shard_map/pallas_call | solution.py:145
  20.0 0.9 copy-done.4
  20.9 3.5 %shard_map.130.base = f32[128,4096]{1,0:T(8,128)S(1)} custom-call(s32[16]{0:T(128)S(1)} %copy-done.5, bf16[128,4096]{1,0:T(8,128)(2,1)S(1)} %fusion.weighted, bf16[128,4096]{1,0:T(8,128)(2,1)S(1)} %collective-permute-done.incoming, f32[256,128]{1,0:T(8,128)S(1)} %copy-done.4), custom_call_target="tpu_custom_call" | custom-call | flops 1 | bytes 1 | tf_op jit(solution)/shard_map/pallas_call | solution.py:186
  24.4 0.0 collective-permute-done.2
  24.4 9.0 %collective-permute-done.1.after = bf16[128,4096]{1,0:T(8,128)(2,1)S(1)} collective-permute-done((bf16[128,4096]{1,0:T(8,128)(2,1)S(1)}, bf16[128,4096]{1,0:T(8,128)(2,1)S(1)}, u32[]{:S(2)}, u32[]{:S(2)}) %collective-permute-start.1) | collective-permute-done | bytes 1048608 | tf_op jit(solution)/shard_map/ppermute | solution.py:26
  33.3 4.6 %collective-permute-start.5 = (bf16[136,2048]{1,0:T(8,128)(2,1)S(1)}, bf16[136,2048]{1,0:T(8,128)(2,1)S(1)}, u32[]{:S(2)}, u32[]{:S(2)}) collective-permute-start(bf16[136,2048]{1,0:T(8,128)(2,1)S(1)} %copy-done.9), channel_id=1, source_target_pairs={{0,2},{2,4},{4,6},{6,8},{8,10},{10,12},{12,14},{14,16},{16,18},{18... | collective-permute-start | bytes 1671176 | tf_op jit(solution)/shard_map/ppermute | solution.py:26
  37.9 2.5 %collective-permute-start.3 = (bf16[136,2048]{1,0:T(8,128)(2,1)S(1)}, bf16[136,2048]{1,0:T(8,128)(2,1)S(1)}, u32[]{:S(2)}, u32[]{:S(2)}) collective-permute-start(bf16[136,2048]{1,0:T(8,128)(2,1)S(1)} %copy-done.8), channel_id=1, source_target_pairs={{0,2},{2,4},{4,6},{6,8},{8,10},{10,12},{12,14},{14,16},{16,18},{18... | collective-permute-start | bytes 1671176 | tf_op jit(solution)/shard_map/ppermute | solution.py:26
  40.4 0.7 collective-permute-start.4
  41.1 3.9 %shard_map.131 = (bf16[128,4096]{1,0:T(8,128)(2,1)S(1)}, bf16[128,4096]{1,0:T(8,128)(2,1)S(1)}) custom-call(s32[16]{0:T(128)S(1)} %copy-done.5, bf16[128,4096]{1,0:T(8,128)(2,1)S(1)} %collective-permute-done.1.after, f32[128,4096]{1,0:T(8,128)S(1)} %shard_map.130.base, bf16[128,4096]{1,0:T(8,128)(2,1)S(1)} %bitcast.21, f32[256,128]{1,0:T(8,128)S(1)} %copy-done.4), custom_call_target="tpu_custom_call" | custom-call | flops 1 | bytes 1 | tf_op jit(solution)/shard_map/pallas_call | solution.py:221
  45.0 0.0 copy-start
  45.0 0.0 copy-start.6
  45.0 0.0 collective-permute-done.4
  45.0 4.2 %shard_map.132.held = bf16[128,4096]{1,0:T(8,128)(2,1)} custom-call(s32[16]{0:T(128)S(1)} %copy-done.5, bf16[128,4096]{1,0:T(8,128)(2,1)S(1)} %get-tuple-element.57.grad, bf16[128,4096]{1,0:T(8,128)(2,1)S(1)} %get-tuple-element.69.wse, f32[8,4096]{1,0:T(8,128)S(1)} %copy-done.2), custom_call_target="tpu_custom_call" | custom-call | flops 1 | bytes 1 | tf_op jit(solution)/shard_map/pallas_call | solution.py:399
  49.2 1.7 %collective-permute-done.5.arrived = bf16[136,2048]{1,0:T(8,128)(2,1)S(1)} collective-permute-done((bf16[136,2048]{1,0:T(8,128)(2,1)S(1)}, bf16[136,2048]{1,0:T(8,128)(2,1)S(1)}, u32[]{:S(2)}, u32[]{:S(2)}) %collective-permute-start.5) | collective-permute-done | bytes 557088 | tf_op jit(solution)/shard_map/ppermute | solution.py:26
  51.0 3.7 %shard_map.133 = (bf16[128,2048]{1,0:T(8,128)(2,1)S(1)}, bf16[128,4096]{1,0:T(8,128)(2,1)}, f32[8,128]{1,0:T(8,128)S(1)}) custom-call(s32[16]{0:T(128)S(1)} %copy-done.5, s32[1]{0:T(128)S(6)} %copy.23.counts, s32[2]{0:T(128)S(1)} %copy-done.6, bf16[1,2,128,4096]{3,2,1,0:T(8,128)(2,1)S(1)} %copy-done, bf16[136,2048]{1,0:T(8,128)(2,1)S(1)} %collective-permute-done.5.arrived, ...), custom_call_target="tpu_custom_call" | custom-call | flops 1 | bytes 1 | tf_op jit(solution)/shard_map/pallas_call | solution.py:292
  54.6 6.9 %collective-permute-start.6 = (bf16[128,2048]{1,0:T(8,128)(2,1)S(1)}, bf16[128,2048]{1,0:T(8,128)(2,1)S(1)}, u32[]{:S(2)}, u32[]{:S(2)}) collective-permute-start(bf16[128,2048]{1,0:T(8,128)(2,1)S(1)} %get-tuple-element.63.mid), channel_id=1, source_target_pairs={{0,2},{2,4},{4,6},{6,8},{8,10},{10,12},{12,14},{14,16},{16,18},{18... | collective-permute-start | bytes 1572872 | tf_op jit(solution)/shard_map/ppermute | solution.py:26
  61.6 3.3 %shard_map.135.rest_0_ = f32[256,128]{1,0:T(8,128)S(1)} custom-call(s32[16]{0:T(128)S(1)} %copy-done.5, bf16[128,2048]{1,0:T(8,128)(2,1)S(1)} %get-tuple-element.63.mid, bf16[128,4096]{1,0:T(8,128)(2,1)S(1)} %fusion.weighted, bf16[128,4096]{1,0:T(8,128)(2,1)S(1)} %collective-permute-done.1.after), custom_call_target="tpu_custom_call" | custom-call | flops 1 | bytes 1 | tf_op jit(solution)/shard_map/pallas_call | solution.py:361
  64.9 0.0 collective-permute-done.3.arrived
  64.9 3.7 %shard_map.134 = (bf16[128,2048]{1,0:T(8,128)(2,1)S(1)}, bf16[128,4096]{1,0:T(8,128)(2,1)}, f32[8,128]{1,0:T(8,128)S(1)}) custom-call(s32[16]{0:T(128)S(1)} %copy-done.5, s32[1]{0:T(128)S(6)} %copy.23.counts, s32[2]{0:T(128)S(1)} %copy-done.6, bf16[1,2,128,4096]{3,2,1,0:T(8,128)(2,1)S(1)} %copy-done, ...), custom_call_target="tpu_custom_call", output_to_operand_aliasing={{1}: (10, {})} | custom-call | flops 1 | bytes 1 | tf_op jit(solution)/shard_map/pallas_call | solution.py:292
  68.6 3.3 %shard_map.136 = f32[256,128]{1,0:T(8,128)S(1)} custom-call(s32[16]{0:T(128)S(1)} %copy-done.5, bf16[128,2048]{1,0:T(8,128)(2,1)S(1)} %get-tuple-element.73.mid, bf16[128,4096]{1,0:T(8,128)(2,1)S(1)} %fusion.weighted, bf16[128,4096]{1,0:T(8,128)(2,1)S(1)} %collective-permute-done.1.after, ...), custom_call_target="tpu_custom_call", output_to_operand_aliasing={{}: (4, {})} | custom-call | flops 1 | bytes 1 | tf_op jit(solution)/shard_map/pallas_call | solution.py:361
  71.9 1.9 %collective-permute-start.10 = (bf16[128,2048]{1,0:T(8,128)(2,1)S(1)}, bf16[128,2048]{1,0:T(8,128)(2,1)S(1)}, u32[]{:S(2)}, u32[]{:S(2)}) collective-permute-start(bf16[128,2048]{1,0:T(8,128)(2,1)S(1)} %get-tuple-element.73.mid), channel_id=1, source_target_pairs={{0,2},{2,4},{4,6},{6,8},{8,10},{10,12},{12,14},{14,16},{16,18},{18... | collective-permute-start | bytes 1572872 | tf_op jit(solution)/shard_map/ppermute | solution.py:26
  73.8 0.0 collective-permute-done.6.prior
  73.8 3.7 %shard_map.137.rest_0_ = bf16[128,4096]{1,0:T(8,128)(2,1)} custom-call(s32[16]{0:T(128)S(1)} %copy-done.5, bf16[128,2048]{1,0:T(8,128)(2,1)S(1)} %collective-permute-done.6.prior, bf16[128,2048]{1,0:T(8,128)(2,1)S(1)} %get-tuple-element.63.mid, bf16[128,4096]{1,0:T(8,128)(2,1)S(1)} %collective-permute-done.incoming, f32[256,128]{1,0:T(8,128)S(1)} %copy-done.3), custom_call_target="tpu_custom_call" | custom-call | flops 1 | bytes 1 | tf_op jit(solution)/shard_map/pallas_call | solution.py:477
  77.6 4.5 %collective-permute-start.7 = (f32[272,128]{1,0:T(8,128)S(1)}, f32[272,128]{1,0:T(8,128)S(1)}, u32[]{:S(2)}, u32[]{:S(2)}) collective-permute-start(f32[272,128]{1,0:T(8,128)S(1)} %pad_maximum_fusion), channel_id=1, source_target_pairs={{0,16},{2,18},{4,20},{6,22},{8,24},{10,26},{12,28},{14,30},{16,0},... | collective-permute-start | bytes 417800 | tf_op jit(solution)/shard_map/ppermute | solution.py:31
  82.0 1.5 %collective-permute-start.8 = (bf16[8,4096]{1,0:T(8,128)(2,1)S(1)}, bf16[8,4096]{1,0:T(8,128)(2,1)S(1)}, u32[]{:S(2)}, u32[]{:S(2)}) collective-permute-start(bf16[8,4096]{1,0:T(8,128)(2,1)S(1)} %slice.12), channel_id=1, source_target_pairs={{2,0},{4,2},{6,4},{8,6},{10,8},{12,10},{14,12},{16,14},{18,16},{20... | collective-permute-start | bytes 196616 | tf_op jit(solution)/shard_map/ppermute | solution.py:26
  83.5 3.9 %collective-permute-done.7 = f32[272,128]{1,0:T(8,128)S(1)} collective-permute-done((f32[272,128]{1,0:T(8,128)S(1)}, f32[272,128]{1,0:T(8,128)S(1)}, u32[]{:S(2)}, u32[]{:S(2)}) %collective-permute-start.7) | collective-permute-done | bytes 139296 | tf_op jit(solution)/shard_map/ppermute | solution.py:31
  87.5 0.7 collective-permute-done.8.rim
  88.2 1.8 %collective-permute-start.9 = (f32[272,128]{1,0:T(8,128)S(1)}, f32[272,128]{1,0:T(8,128)S(1)}, u32[]{:S(2)}, u32[]{:S(2)}) collective-permute-start(f32[272,128]{1,0:T(8,128)S(1)} %add.19), channel_id=1, source_target_pairs={{0,8},{2,10},{4,12},{6,14},{8,0},{10,2},{12,4},{14,6},{16,24},{18,... | collective-permute-start | bytes 417800 | tf_op jit(solution)/shard_map/ppermute | solution.py:31
  90.0 1.9 %shard_map.138 = bf16[128,4096]{1,0:T(8,128)(2,1)} custom-call(s32[16]{0:T(128)S(1)} %copy-done.5, bf16[128,4096]{1,0:T(8,128)(2,1)S(1)} %get-tuple-element.57.grad, bf16[128,4096]{1,0:T(8,128)(2,1)S(1)} %get-tuple-element.69.wse, bf16[8,4096]{1,0:T(8,128)(2,1)S(1)} %collective-permute-done.8.rim, ...), custom_call_target="tpu_custom_call", output_to_operand_aliasing={{}: (5, {})} | custom-call | flops 1 | bytes 1 | tf_op jit(solution)/shard_map/pallas_call | solution.py:436
  91.9 1.4 %collective-permute-done.9 = f32[272,128]{1,0:T(8,128)S(1)} collective-permute-done((f32[272,128]{1,0:T(8,128)S(1)}, f32[272,128]{1,0:T(8,128)S(1)}, u32[]{:S(2)}, u32[]{:S(2)}) %collective-permute-start.9) | collective-permute-done | bytes 139296 | tf_op jit(solution)/shard_map/ppermute | solution.py:31
  93.3 0.0 collective-permute-done.10.prior
  93.3 4.7 %collective-permute-start.13 = (f32[272,128]{1,0:T(8,128)S(1)}, f32[272,128]{1,0:T(8,128)S(1)}, u32[]{:S(2)}, u32[]{:S(2)}) collective-permute-start(f32[272,128]{1,0:T(8,128)S(1)} %add.20), channel_id=1, source_target_pairs={{0,6},{2,4},{4,2},{6,0},{8,14},{10,12},{12,10},{14,8},{16,22},{18,... | collective-permute-start | bytes 417800 | tf_op jit(solution)/shard_map/ppermute | solution.py:31
  98.0 0.0 collective-permute-start.12
  98.0 0.6 collective-permute-start.11
  98.6 3.8 %shard_map.139 = bf16[128,4096]{1,0:T(8,128)(2,1)} custom-call(s32[16]{0:T(128)S(1)} %copy-done.5, bf16[128,2048]{1,0:T(8,128)(2,1)S(1)} %collective-permute-done.10.prior, bf16[128,2048]{1,0:T(8,128)(2,1)S(1)} %get-tuple-element.73.mid, bf16[128,4096]{1,0:T(8,128)(2,1)S(1)} %collective-permute-done.incoming, ...), custom_call_target="tpu_custom_call", output_to_operand_aliasing={{}: (5, {})} | custom-call | flops 1 | bytes 1 | tf_op jit(solution)/shard_map/pallas_call | solution.py:477
  102.4 0.7 collective-permute-done.12
  103.1 0.0 collective-permute-done.11
  103.1 0.7 slice_bitcast_fusion
  103.8 0.6 broadcast_in_dim.18
  (25 shorter events, 0.1 us)
Async XLA Ops:
  0.6 3.0 %collective-permute-start = (bf16[128,4096]{1,0:T(8,128)(2,1)}, bf16[128,4096]{1,0:T(8,128)(2,1)S(1)}, u32[]{:S(2)}, u32[]{:S(2)}) collective-permute-start(bf16[128,4096]{1,0:T(8,128)(2,1)} %bitcast.30), channel_id=1, source_target_pairs={{0,1},{1,0},{2,3},{3,2},{4,5},{5,4},{6,7},{7,6},{8,9},{9,8},{10,11... | collective-permute-start | bytes 3145736 | tf_op jit(solution)/shard_map/ppermute | solution.py:31
  5.1 28.2 %collective-permute-start.1 = (bf16[128,4096]{1,0:T(8,128)(2,1)S(1)}, bf16[128,4096]{1,0:T(8,128)(2,1)S(1)}, u32[]{:S(2)}, u32[]{:S(2)}) collective-permute-start(bf16[128,4096]{1,0:T(8,128)(2,1)S(1)} %fusion.weighted), channel_id=1, source_target_pairs={{2,0},{4,2},{6,4},{8,6},{10,8},{12,10},{14,12},{16,14},{18,16},{20... | collective-permute-start | bytes 3145736 | tf_op jit(solution)/shard_map/ppermute | solution.py:26
  7.1 10.0 %copy-start.7 = (f32[1,256,7]{1,0,2:T(1,128)S(1)}, f32[1,256,7]{1,0,2:T(1,128)}, u32[]{:S(2)}) copy-start(f32[1,256,7]{1,0,2:T(1,128)} %param.16) | copy-start | bytes 21508
  7.1 12.9 %copy-start.5 = (s32[16]{0:T(128)S(1)}, s32[16]{0:T(128)}, u32[]{:S(2)}) copy-start(s32[16]{0:T(128)} %bounds.19) | copy-start | bytes 196
  10.2 14.2 %collective-permute-start.2 = (bf16[8,4096]{1,0:T(8,128)(2,1)}, bf16[8,4096]{1,0:T(8,128)(2,1)S(1)}, u32[]{:S(2)}, u32[]{:S(2)}) collective-permute-start(bf16[8,4096]{1,0:T(8,128)(2,1)} %get-tuple-element.42), channel_id=1, source_target_pairs={{0,4},{4,8},{6,10},{8,12},{12,16},{14,18},{16,20},{20,24},{22,26},... | collective-permute-start | bytes 196616 | tf_op jit(solution)/shard_map/ppermute | solution.py:505
  20.0 0.9 copy-start.4
  20.9 12.5 %copy-start.9 = (bf16[136,2048]{1,0:T(8,128)(2,1)S(1)}, bf16[136,2048]{1,0:T(8,128)(2,1)}, u32[]{:S(2)}) copy-start(bf16[136,2048]{1,0:T(8,128)(2,1)} %get-tuple-element.59) | copy-start | bytes 1671172
  20.9 17.1 %copy-start.8 = (bf16[136,2048]{1,0:T(8,128)(2,1)S(1)}, bf16[136,2048]{1,0:T(8,128)(2,1)}, u32[]{:S(2)}) copy-start(bf16[136,2048]{1,0:T(8,128)(2,1)} %get-tuple-element.48) | copy-start | bytes 1671172
  20.9 19.6 %copy-start.10 = (bf16[8,4096]{1,0:T(8,128)(2,1)S(1)}, bf16[8,4096]{1,0:T(8,128)(2,1)}, u32[]{:S(2)}) copy-start(bf16[8,4096]{1,0:T(8,128)(2,1)} %get-tuple-element.42) | copy-start | bytes 196612
  20.9 20.3 %copy-start.1 = (bf16[1,128,4096]{2,1,0:T(8,128)(2,1)S(1)}, bf16[1,128,4096]{2,1,0:T(8,128)(2,1)}, u32[]{:S(2)}) copy-start(bf16[1,128,4096]{2,1,0:T(8,128)(2,1)} %param.13) | copy-start | bytes 3145732
  33.3 17.6 %collective-permute-start.5 = (bf16[136,2048]{1,0:T(8,128)(2,1)S(1)}, bf16[136,2048]{1,0:T(8,128)(2,1)S(1)}, u32[]{:S(2)}, u32[]{:S(2)}) collective-permute-start(bf16[136,2048]{1,0:T(8,128)(2,1)S(1)} %copy-done.9), channel_id=1, source_target_pairs={{0,2},{2,4},{4,6},{6,8},{8,10},{10,12},{12,14},{14,16},{16,18},{18... | collective-permute-start | bytes 1671176 | tf_op jit(solution)/shard_map/ppermute | solution.py:26
  37.9 26.9 %collective-permute-start.3 = (bf16[136,2048]{1,0:T(8,128)(2,1)S(1)}, bf16[136,2048]{1,0:T(8,128)(2,1)S(1)}, u32[]{:S(2)}, u32[]{:S(2)}) collective-permute-start(bf16[136,2048]{1,0:T(8,128)(2,1)S(1)} %copy-done.8), channel_id=1, source_target_pairs={{0,2},{2,4},{4,6},{6,8},{8,10},{10,12},{12,14},{14,16},{16,18},{18... | collective-permute-start | bytes 1671176 | tf_op jit(solution)/shard_map/ppermute | solution.py:26
  40.4 4.6 %collective-permute-start.4 = (bf16[8,4096]{1,0:T(8,128)(2,1)S(1)}, bf16[8,4096]{1,0:T(8,128)(2,1)S(1)}, u32[]{:S(2)}, u32[]{:S(2)}) collective-permute-start(bf16[8,4096]{1,0:T(8,128)(2,1)S(1)} %copy-done.10), channel_id=1, source_target_pairs={{2,6},{10,14},{18,22},{26,30},{3,7},{11,15},{19,23},{27,31}} | collective-permute-start | bytes 196616 | tf_op jit(solution)/shard_map/ppermute | solution.py:506
  41.1 3.9 %copy-start.2 = (f32[8,4096]{1,0:T(8,128)S(1)}, f32[8,4096]{1,0:T(8,128)}, u32[]{:S(2)}) copy-start(f32[8,4096]{1,0:T(8,128)} %get-tuple-element.56.taps) | copy-start | bytes 393220
  45.0 5.9 %copy-start = (bf16[1,2,128,4096]{3,2,1,0:T(8,128)(2,1)S(1)}, bf16[1,2,128,4096]{3,2,1,0:T(8,128)(2,1)}, u32[]{:S(2)}) copy-start(bf16[1,2,128,4096]{3,2,1,0:T(8,128)(2,1)} %slot.5) | copy-start | bytes 6291460
  45.0 5.9 %copy-start.6 = (s32[2]{0:T(128)S(1)}, s32[2]{0:T(128)}, u32[]{:S(2)}) copy-start(s32[2]{0:T(128)} %destinations.5) | copy-start | bytes 28
  54.6 19.1 %collective-permute-start.6 = (bf16[128,2048]{1,0:T(8,128)(2,1)S(1)}, bf16[128,2048]{1,0:T(8,128)(2,1)S(1)}, u32[]{:S(2)}, u32[]{:S(2)}) collective-permute-start(bf16[128,2048]{1,0:T(8,128)(2,1)S(1)} %get-tuple-element.63.mid), channel_id=1, source_target_pairs={{0,2},{2,4},{4,6},{6,8},{8,10},{10,12},{12,14},{14,16},{16,18},{18... | collective-permute-start | bytes 1572872 | tf_op jit(solution)/shard_map/ppermute | solution.py:26
  68.6 5.2 %copy-start.3 = (f32[256,128]{1,0:T(8,128)S(1)}, f32[256,128]{1,0:T(8,128)}, u32[]{:S(2)}) copy-start(f32[256,128]{1,0:T(8,128)} %get-tuple-element.67.mirrored) | copy-start | bytes 393220
  71.9 21.4 %collective-permute-start.10 = (bf16[128,2048]{1,0:T(8,128)(2,1)S(1)}, bf16[128,2048]{1,0:T(8,128)(2,1)S(1)}, u32[]{:S(2)}, u32[]{:S(2)}) collective-permute-start(bf16[128,2048]{1,0:T(8,128)(2,1)S(1)} %get-tuple-element.73.mid), channel_id=1, source_target_pairs={{0,2},{2,4},{4,6},{6,8},{8,10},{10,12},{12,14},{14,16},{16,18},{18... | collective-permute-start | bytes 1572872 | tf_op jit(solution)/shard_map/ppermute | solution.py:26
  77.6 9.9 %collective-permute-start.7 = (f32[272,128]{1,0:T(8,128)S(1)}, f32[272,128]{1,0:T(8,128)S(1)}, u32[]{:S(2)}, u32[]{:S(2)}) collective-permute-start(f32[272,128]{1,0:T(8,128)S(1)} %pad_maximum_fusion), channel_id=1, source_target_pairs={{0,16},{2,18},{4,20},{6,22},{8,24},{10,26},{12,28},{14,30},{16,0},... | collective-permute-start | bytes 417800 | tf_op jit(solution)/shard_map/ppermute | solution.py:31
  82.0 6.1 %collective-permute-start.8 = (bf16[8,4096]{1,0:T(8,128)(2,1)S(1)}, bf16[8,4096]{1,0:T(8,128)(2,1)S(1)}, u32[]{:S(2)}, u32[]{:S(2)}) collective-permute-start(bf16[8,4096]{1,0:T(8,128)(2,1)S(1)} %slice.12), channel_id=1, source_target_pairs={{2,0},{4,2},{6,4},{8,6},{10,8},{12,10},{14,12},{16,14},{18,16},{20... | collective-permute-start | bytes 196616 | tf_op jit(solution)/shard_map/ppermute | solution.py:26
  88.2 5.1 %collective-permute-start.9 = (f32[272,128]{1,0:T(8,128)S(1)}, f32[272,128]{1,0:T(8,128)S(1)}, u32[]{:S(2)}, u32[]{:S(2)}) collective-permute-start(f32[272,128]{1,0:T(8,128)S(1)} %add.19), channel_id=1, source_target_pairs={{0,8},{2,10},{4,12},{6,14},{8,0},{10,2},{12,4},{14,6},{16,24},{18,... | collective-permute-start | bytes 417800 | tf_op jit(solution)/shard_map/ppermute | solution.py:31
  93.3 9.1 %collective-permute-start.13 = (f32[272,128]{1,0:T(8,128)S(1)}, f32[272,128]{1,0:T(8,128)S(1)}, u32[]{:S(2)}, u32[]{:S(2)}) collective-permute-start(f32[272,128]{1,0:T(8,128)S(1)} %add.20), channel_id=1, source_target_pairs={{0,6},{2,4},{4,2},{6,0},{8,14},{10,12},{12,10},{14,8},{16,22},{18,... | collective-permute-start | bytes 417800 | tf_op jit(solution)/shard_map/ppermute | solution.py:31
  98.0 5.1 %collective-permute-start.12 = (f32[272,128]{1,0:T(8,128)S(1)}, f32[272,128]{1,0:T(8,128)S(1)}, u32[]{:S(2)}, u32[]{:S(2)}) collective-permute-start(f32[272,128]{1,0:T(8,128)S(1)} %add.20), channel_id=1, source_target_pairs={{0,4},{2,6},{4,0},{6,2},{8,12},{10,14},{12,8},{14,10},{16,20},{18,... | collective-permute-start | bytes 417800 | tf_op jit(solution)/shard_map/ppermute | solution.py:31
  98.0 5.1 %collective-permute-start.11 = (f32[272,128]{1,0:T(8,128)S(1)}, f32[272,128]{1,0:T(8,128)S(1)}, u32[]{:S(2)}, u32[]{:S(2)}) collective-permute-start(f32[272,128]{1,0:T(8,128)S(1)} %add.20), channel_id=1, source_target_pairs={{0,2},{2,0},{4,6},{6,4},{8,10},{10,8},{12,14},{14,12},{16,18},{18,... | collective-permute-start | bytes 417800 | tf_op jit(solution)/shard_map/ppermute | solution.py:31
